TPU v7x, 32 devices: a whole 2x2x4 slice. The times are simulated.
32 devices in a mesh: shot: 8 (over y, x, core), rcv: 4 (over z).
Axes of the slice: x: 2, y: 2, z: 4, core: 2. Of those that a mesh axis runs over, the one named last changes fastest.
Arguments:
- data: bfloat16 [48, 1024, 256], P('shot', 'rcv'), may hold values from -6 to 6
- surface_traces: bfloat16 [128, 1024, 256], P('shot', 'rcv'), may hold values from -6 to 6
- primaries: bfloat16 [48, 64, 64], P('shot', 'rcv'), may hold values from -0.09375 to 0.09375
- panel_owner: int32 [4], replicated, may hold values from 0 to 7, as said below
Outputs:
- residual: bfloat16 [48, 1024, 256], P('shot', 'rcv')
Inputs may be any that keep to these rules, and one draw needn't show every extreme that they name: panel_owner holds 4 distinct indices of the shot axis, in an order drawn from the seed.
All inputs are finite; a program needn't handle non-finite values.
Results may differ from a plain program's by a relative error of at most 0.001.
Values may be sent and summed in bfloat16 or wider, within the bound.
No kernel may reach another device: no remote copies, remote signals or barrier semaphores. Data moves between devices by JAX's collectives and lax.ppermute only.
A program may use at most 128 MiB of HBM per device.

v0:
```python
import jax
import jax.numpy as jnp
from jax import lax
from jax.sharding import PartitionSpec as P

TAPS = 64
KP = 16
PANELS = 4
BLOCK = 128


def broadcast(value, axis, root):
    mine = lax.axis_index(axis) == root
    return lax.psum(jnp.where(mine, value, jnp.zeros_like(value)), axis)


def shift_table(taps, block):
    lag_index = lax.broadcasted_iota(jnp.int32, (2, taps, block, block), 0)
    tap_index = lax.broadcasted_iota(jnp.int32, (2, taps, block, block), 1)
    in_index = lax.broadcasted_iota(jnp.int32, (2, taps, block, block), 2)
    out_index = lax.broadcasted_iota(jnp.int32, (2, taps, block, block), 3)
    distance = out_index - in_index + lag_index * block
    return (distance == tap_index).astype(jnp.bfloat16)


def band_matrices(panel_prim, shift_ones):
    bands = jnp.einsum(
        "skt,ltio->lskio", panel_prim, shift_ones, preferred_element_type=jnp.float32
    )
    return bands.astype(jnp.bfloat16)


def convolve(traces, bands, block):
    point_count, row_count, length = traces.shape
    blocks = traces.reshape(point_count, row_count, length // block, block)
    earlier = jnp.concatenate([jnp.zeros_like(blocks[:, :, :1]), blocks[:, :, :-1]], axis=2)
    stacked = jnp.stack([blocks, earlier])
    product = jnp.einsum("lkrbi,lskio->srbo", stacked, bands, preferred_element_type=jnp.float32)
    return product.reshape(bands.shape[1], row_count, length)


def shards(data, surface_traces, primaries, panel_owner):
    shift_ones = shift_table(TAPS, BLOCK)
    summed = jnp.zeros(data.shape, jnp.float32)
    panels_here = primaries.shape[1] // KP
    for panel_id in range(PANELS):
        first_point = panel_id % panels_here * KP
        panel_prim = broadcast(primaries, "rcv", panel_id // panels_here)
        traces = broadcast(surface_traces, "shot", panel_owner[panel_id])
        summed = summed + convolve(traces, band_matrices(panel_prim, shift_ones), BLOCK)
    return (data.astype(jnp.float32) - summed).astype(jnp.bfloat16)


def solution(mesh):
    placed = (P("shot", "rcv", None), P("shot", "rcv", None), P("shot", "rcv", None), P())
    return jax.shard_map(
        shards, mesh=mesh, in_specs=placed, out_specs=P("shot", "rcv", None), check_vma=False
    )
```

profile of v0, /device:TPU:1, one launch (start us, length us, event | category | flops | bytes accessed | tf_op | source)
XLA Modules:
  0.0 200.9 jit_solution(1195274902523362135)
XLA Ops:
  6.5 0.0 all-reduce.8.cloned.1.call-start
  6.5 1.5 fusion.39
  10.6 2.9 %copy.6 = bf16[16,256,256]{1,2,0:T(8,128)(2,1)S(1)} copy(bf16[16,256,256]{2,1,0:T(8,128)(2,1)} %param.5) | data formatting | bytes 4194304 | tf_op args[1]
  13.5 3.5 %broadcast_select_fusion.3 = (bf16[16,256,256]{1,2,0:T(8,128)(2,1)}, bf16[16,256,256]{1,2,0:T(8,128)(2,1)}, bf16[16,256,256]{1,2,0:T(8,128)(2,1)}, bf16[16,256,256]{1,2,0:T(8,128)(2,1)}) fusion(bf16[16,256,256]{1,2,0:T(8,128)(2,1)S(1)} %copy.6, pred[]{:T(512)S(6)} %eq.35, pred[]{:T(512)S(6)} %eq.41, pred[]{:T(512)S(6)} %eq.39, pred[]{:T(512)S(6)} %eq.37), kind=kLoop, calls=%fused_computation.41 | loop fusion | flops 4194304 | bytes 10485764 | tf_op jit(solution)/shard_map/jit(_where)/select_n | solution.py:14
  16.9 0.0 all-reduce.8.cloned.1.call-update
  17.0 0.7 copy-done.9
  17.7 17.6 %all-reduce.5 = (bf16[6,16,64]{2,1,0:T(8,128)(2,1)S(1)}, bf16[6,16,64]{2,1,0:T(8,128)(2,1)S(1)}, bf16[6,16,64]{2,1,0:T(8,128)(2,1)S(1)}, bf16[6,16,64]{2,1,0:T(8,128)(2,1)S(1)}) all-reduce(bf16[6,16,64]{2,1,0:T(8,128)(2,1)S(1)} %get-tuple-element.19, ...), channel_id=1, replica_groups=mesh['shot'=8,'rcv'=4] {'rcv'}, use_global_device_ids=true, to_apply=%region_6.7 | all-reduce | flops 24576 | bytes 98304 | tf_op jit(solution)/shard_map/psum | solution.py:14
  35.3 1.5 fusion
  36.8 6.4 %fusion.25 = bf16[2,128,128,6,16]{2,4,3,1,0:T(8,128)(2,1)} fusion(pred[2,64,128,128,1]{3,2,1,0,4:T(32,128)(4,1)S(1)} %fusion, bf16[6,16,64]{2,1,0:T(8,128)(2,1)S(1)} %get-tuple-element.11), kind=kOutput, calls=%fused_computation.30 | convolution fusion | flops 402653184 | bytes 8400896 | tf_op jit(solution)/shard_map/skt,ltio->lskio/dot_general | solution.py:27
  43.1 9.4 %copy.25 = bf16[2,128,128,6,16]{1,2,0,4,3:T(8,128)(2,1)} copy(bf16[2,128,128,6,16]{2,4,3,1,0:T(8,128)(2,1)} %fusion.25) | data formatting | bytes 12582912 | tf_op jit(solution)/shard_map/skt,ltio->lskio/dot_general | solution.py:27
  52.6 6.4 %fusion.23 = bf16[2,128,128,6,16]{2,4,3,1,0:T(8,128)(2,1)} fusion(pred[2,64,128,128,1]{3,2,1,0,4:T(32,128)(4,1)S(1)} %fusion, bf16[6,16,64]{2,1,0:T(8,128)(2,1)S(1)} %get-tuple-element.10), kind=kOutput, calls=%fused_computation.28 | convolution fusion | flops 402653184 | bytes 8400896 | tf_op jit(solution)/shard_map/skt,ltio->lskio/dot_general | solution.py:27
  58.9 9.1 %copy.29 = bf16[2,128,128,6,16]{1,2,0,4,3:T(8,128)(2,1)} copy(bf16[2,128,128,6,16]{2,4,3,1,0:T(8,128)(2,1)} %fusion.23) | data formatting | bytes 12582912 | tf_op jit(solution)/shard_map/skt,ltio->lskio/dot_general | solution.py:27
  68.1 6.3 %fusion.21 = bf16[2,128,128,6,16]{2,4,3,1,0:T(8,128)(2,1)} fusion(pred[2,64,128,128,1]{3,2,1,0,4:T(32,128)(4,1)S(1)} %fusion, bf16[6,16,64]{2,1,0:T(8,128)(2,1)S(1)} %get-tuple-element.9), kind=kOutput, calls=%fused_computation.26 | convolution fusion | flops 402653184 | bytes 8400896 | tf_op jit(solution)/shard_map/skt,ltio->lskio/dot_general | solution.py:27
  74.4 9.2 %copy.33 = bf16[2,128,128,6,16]{1,2,0,4,3:T(8,128)(2,1)} copy(bf16[2,128,128,6,16]{2,4,3,1,0:T(8,128)(2,1)} %fusion.21) | data formatting | bytes 12582912 | tf_op jit(solution)/shard_map/skt,ltio->lskio/dot_general | solution.py:27
  83.6 6.5 %fusion.27 = bf16[2,128,128,6,16]{2,4,3,1,0:T(8,128)(2,1)} fusion(pred[2,64,128,128,1]{3,2,1,0,4:T(32,128)(4,1)S(1)} %fusion, bf16[6,16,64]{2,1,0:T(8,128)(2,1)S(1)} %get-tuple-element.12), kind=kOutput, calls=%fused_computation.32 | convolution fusion | flops 402653184 | bytes 8400896 | tf_op jit(solution)/shard_map/skt,ltio->lskio/dot_general | solution.py:27
  90.1 9.3 %copy.21 = bf16[2,128,128,6,16]{1,2,0,4,3:T(8,128)(2,1)} copy(bf16[2,128,128,6,16]{2,4,3,1,0:T(8,128)(2,1)} %fusion.27) | data formatting | bytes 12582912 | tf_op jit(solution)/shard_map/skt,ltio->lskio/dot_general | solution.py:27
  99.4 46.8 %all-reduce.8.cloned.1.call-done = (bf16[16,256,256]{1,2,0:T(8,128)(2,1)}, bf16[16,256,256]{1,2,0:T(8,128)(2,1)}, bf16[16,256,256]{1,2,0:T(8,128)(2,1)}, bf16[16,256,256]{1,2,0:T(8,128)(2,1)}) async-done(((bf16[16,256,256]{1,2,0:T(8,128)(2,1)}, bf16[16,256,256]{1,2,0:T(8,128)(2,1)}, bf16[16,256,256]{1,2,0:T(8,128)(2,1)}, bf16[16,256,256]{1,2,0:T(8,128)(2,1)}), (bf16[16,256,256]{1,2,0:T(8,128)(2,1)}, ...) | async-done | bytes 8388624 | tf_op jit(solution)/shard_map/psum | solution.py:14
  146.2 1.3 slice.33
  147.5 0.7 copy.37
  148.2 1.7 pad_bitcast_fusion.2
  149.9 4.1 %copy.11 = bf16[1,16,256,2,128]{4,2,0,1,3:T(8,128)(2,1)} copy(bf16[1,16,256,2,128]{2,4,3,1,0:T(8,128)(2,1)} %bitcast.122) | data formatting | bytes 4194304 | tf_op jit(solution)/shard_map/stack;reshape | solution.py:37
  154.0 0.0 copy-done.2
  154.0 0.1 slice.34
  154.1 0.7 copy.38
  154.7 1.7 pad_bitcast_fusion.1
  156.4 4.1 %copy.14 = bf16[1,16,256,2,128]{4,2,0,1,3:T(8,128)(2,1)} copy(bf16[1,16,256,2,128]{2,4,3,1,0:T(8,128)(2,1)} %bitcast.119) | data formatting | bytes 4194304 | tf_op jit(solution)/shard_map/stack;reshape | solution.py:37
  160.5 0.0 copy-done.1
  160.5 0.1 slice.35
  160.6 0.7 copy.39
  161.2 1.7 pad_bitcast_fusion
  163.0 4.1 %copy.17 = bf16[1,16,256,2,128]{4,2,0,1,3:T(8,128)(2,1)} copy(bf16[1,16,256,2,128]{2,4,3,1,0:T(8,128)(2,1)} %bitcast.117) | data formatting | bytes 4194304 | tf_op jit(solution)/shard_map/stack;reshape | solution.py:37
  167.1 0.1 slice.32
  167.1 0.7 copy.36
  167.8 1.6 pad_bitcast_fusion.3
  169.5 4.1 %copy.8 = bf16[1,16,256,2,128]{4,2,0,1,3:T(8,128)(2,1)} copy(bf16[1,16,256,2,128]{2,4,3,1,0:T(8,128)(2,1)} %bitcast.115) | data formatting | bytes 4194304 | tf_op jit(solution)/shard_map/stack;reshape | solution.py:37
  173.6 7.2 %fusion.5 = f32[6,128,256,2,1,1]{2,1,5,4,3,0:T(8,128)S(1)} fusion(bf16[2,128,128,6,16]{1,2,0,4,3:T(8,128)(2,1)} %copy.25, bf16[1,16,256,2,128]{4,2,0,1,3:T(8,128)(2,1)} %pad_bitcast_fusion.2, bf16[1,16,256,2,128]{4,2,0,1,3:T(8,128)(2,1)} %copy.11), kind=kOutput, calls=%fused_computation.6 | convolution fusion | flops 3229614080 | bytes 12058624 | tf_op jit(solution)/shard_map/lkrbi,lskio->srbo/dot_general | solution.py:38
  180.9 0.0 slice-start.3
  180.9 0.0 copy-start.4
  180.9 0.0 copy-start.7
  180.9 0.0 slice-start.4
  180.9 3.4 %fusion.3 = f32[6,128,256,2,1,1]{2,1,5,4,3,0:T(8,128)S(1)} fusion(bf16[2,128,128,6,16]{1,2,0,4,3:T(8,128)(2,1)S(1)} %bitcast.110, bf16[1,16,256,2,128]{4,2,0,1,3:T(8,128)(2,1)S(1)} %copy-done.3, bf16[1,16,256,2,128]{4,2,0,1,3:T(8,128)(2,1)S(1)} %copy-done.6), kind=kOutput, calls=%fused_computation.4 | convolution fusion | flops 3229614080 | bytes 12058624 | tf_op jit(solution)/shard_map/lkrbi,lskio->srbo/dot_general | solution.py:38
  184.3 0.0 slice-done.2
  184.4 0.0 slice-done.3
  184.4 0.0 slice-start.5
  184.4 3.4 %fusion.1 = f32[6,128,256,2,1,1]{2,1,5,4,3,0:T(8,128)S(1)} fusion(bf16[2,128,128,6,16]{1,2,0,4,3:T(8,128)(2,1)S(1)} %bitcast.112, bf16[1,16,256,2,128]{4,2,0,1,3:T(8,128)(2,1)S(1)} %copy-done.4, bf16[1,16,256,2,128]{4,2,0,1,3:T(8,128)(2,1)S(1)} %copy-done.7), kind=kOutput, calls=%fused_computation.2 | convolution fusion | flops 3229614080 | bytes 12058624 | tf_op jit(solution)/shard_map/lkrbi,lskio->srbo/dot_general | solution.py:38
  187.9 3.4 %bitcast_add_fusion = f32[6,128,256,2]{2,1,3,0:T(8,128)S(1)} fusion(f32[6,128,256,2,1,1]{2,1,5,4,3,0:T(8,128)S(1)} %fusion.1, f32[6,128,256,2,1,1]{2,1,5,4,3,0:T(8,128)S(1)} %fusion.3, f32[6,128,256,2,1,1]{2,1,5,4,3,0:T(8,128)S(1)} %fusion.5, bf16[1,16,256,2,128]{4,2,0,1,3:T(8,128)(2,1)S(1)} %copy-done.5, bf16[1,16,256,2,128]{4,2,0,1,3:T(8,128)(2,1)S(1)} %copy-done.8, ...), kind=kOutput, calls=%fused_computation.42 | convolution fusion | flops 3230793728 | bytes 16777216 | tf_op jit(solution)/shard_map/lkrbi,lskio->srbo/dot_general | solution.py:38
  191.4 0.5 copy.18
  191.8 2.2 %subtract_convert_fusion = bf16[6,256,256]{2,1,0:T(8,128)(2,1)} fusion(f32[6,256,256]{2,1,0:T(8,128)S(1)} %copy.18, bf16[6,256,256]{2,1,0:T(8,128)(2,1)} %param.4), kind=kLoop, calls=%fused_computation.45 | loop fusion | flops 1179648 | bytes 3145728 | tf_op jit(solution)/shard_map/convert_element_type | solution.py:51
  (27 shorter events, 0.1 us)
Async XLA Ops:
  6.5 139.7 %all-reduce.8.cloned.1.call-start = ((), (), s32[]{:S(2)}) async-start(), calls=%async_computation | async-start | bytes 16777216 | tf_op jit(solution)/shard_map/psum | solution.py:14
  16.9 0.7 copy-start.9
  149.9 4.1 %copy-start.2 = (bf16[16,256,256]{1,2,0:T(8,128)(2,1)S(1)}, bf16[16,256,256]{1,2,0:T(8,128)(2,1)}, u32[]{:S(2)}) copy-start(bf16[16,256,256]{1,2,0:T(8,128)(2,1)} %get-tuple-element.6) | copy-start | bytes 6291460
  156.4 4.1 %copy-start.1 = (bf16[16,256,256]{1,2,0:T(8,128)(2,1)S(1)}, bf16[16,256,256]{1,2,0:T(8,128)(2,1)}, u32[]{:S(2)}) copy-start(bf16[16,256,256]{1,2,0:T(8,128)(2,1)} %get-tuple-element.5) | copy-start | bytes 6291460
  163.0 4.1 %copy-start = (bf16[16,256,256]{1,2,0:T(8,128)(2,1)S(1)}, bf16[16,256,256]{1,2,0:T(8,128)(2,1)}, u32[]{:S(2)}) copy-start(bf16[16,256,256]{1,2,0:T(8,128)(2,1)} %get-tuple-element.8) | copy-start | bytes 6291460
  169.5 11.4 %slice-start = ((s8[6291456]{0:T(1024)(128)(4,1)}), s8[2097152]{0:T(1024)(128)(4,1)S(1)}, s32[]{:S(2)}) async-start(s8[6291456]{0:T(1024)(128)(4,1)} %bitcast.109), calls=%async_computation.1 | async-start | bytes 4194304
  173.6 7.3 %slice-start.1 = ((s8[6291456]{0:T(1024)(128)(4,1)}), s8[4194304]{0:T(1024)(128)(4,1)S(1)}, s32[]{:S(2)}) async-start(s8[6291456]{0:T(1024)(128)(4,1)} %bitcast.109), calls=%async_computation.2 | async-start | bytes 8388608
  173.6 7.3 %copy-start.3 = (bf16[1,16,256,2,128]{4,2,0,1,3:T(8,128)(2,1)S(1)}, bf16[1,16,256,2,128]{4,2,0,1,3:T(8,128)(2,1)}, u32[]{:S(2)}) copy-start(bf16[1,16,256,2,128]{4,2,0,1,3:T(8,128)(2,1)} %pad_bitcast_fusion.1) | copy-start | bytes 6291460
  173.6 7.3 %copy-start.6 = (bf16[1,16,256,2,128]{4,2,0,1,3:T(8,128)(2,1)S(1)}, bf16[1,16,256,2,128]{4,2,0,1,3:T(8,128)(2,1)}, u32[]{:S(2)}) copy-start(bf16[1,16,256,2,128]{4,2,0,1,3:T(8,128)(2,1)} %copy.14) | copy-start | bytes 6291460
  173.6 10.8 %slice-start.2 = ((s8[6291456]{0:T(1024)(128)(4,1)}), s8[4194304]{0:T(1024)(128)(4,1)S(1)}, s32[]{:S(2)}) async-start(s8[6291456]{0:T(1024)(128)(4,1)} %bitcast.111), calls=%async_computation.3 | async-start | bytes 8388608
  180.9 3.5 %slice-start.3 = ((s8[6291456]{0:T(1024)(128)(4,1)}), s8[2097152]{0:T(1024)(128)(4,1)S(1)}, s32[]{:S(2)}) async-start(s8[6291456]{0:T(1024)(128)(4,1)} %bitcast.111), calls=%async_computation.4 | async-start | bytes 4194304
  180.9 3.5 %copy-start.4 = (bf16[1,16,256,2,128]{4,2,0,1,3:T(8,128)(2,1)S(1)}, bf16[1,16,256,2,128]{4,2,0,1,3:T(8,128)(2,1)}, u32[]{:S(2)}) copy-start(bf16[1,16,256,2,128]{4,2,0,1,3:T(8,128)(2,1)} %pad_bitcast_fusion) | copy-start | bytes 6291460
  180.9 3.5 %copy-start.7 = (bf16[1,16,256,2,128]{4,2,0,1,3:T(8,128)(2,1)S(1)}, bf16[1,16,256,2,128]{4,2,0,1,3:T(8,128)(2,1)}, u32[]{:S(2)}) copy-start(bf16[1,16,256,2,128]{4,2,0,1,3:T(8,128)(2,1)} %copy.17) | copy-start | bytes 6291460
  180.9 7.0 %slice-start.4 = ((s8[6291456]{0:T(1024)(128)(4,1)}), s8[4194304]{0:T(1024)(128)(4,1)S(1)}, s32[]{:S(2)}) async-start(s8[6291456]{0:T(1024)(128)(4,1)} %bitcast.113), calls=%async_computation.5 | async-start | bytes 8388608
  184.4 3.5 %slice-start.5 = ((s8[6291456]{0:T(1024)(128)(4,1)}), s8[2097152]{0:T(1024)(128)(4,1)S(1)}, s32[]{:S(2)}) async-start(s8[6291456]{0:T(1024)(128)(4,1)} %bitcast.113), calls=%async_computation.6 | async-start | bytes 4194304
  184.4 3.5 %copy-start.5 = (bf16[1,16,256,2,128]{4,2,0,1,3:T(8,128)(2,1)S(1)}, bf16[1,16,256,2,128]{4,2,0,1,3:T(8,128)(2,1)}, u32[]{:S(2)}) copy-start(bf16[1,16,256,2,128]{4,2,0,1,3:T(8,128)(2,1)} %pad_bitcast_fusion.3) | copy-start | bytes 6291460
  184.4 3.5 %copy-start.8 = (bf16[1,16,256,2,128]{4,2,0,1,3:T(8,128)(2,1)S(1)}, bf16[1,16,256,2,128]{4,2,0,1,3:T(8,128)(2,1)}, u32[]{:S(2)}) copy-start(bf16[1,16,256,2,128]{4,2,0,1,3:T(8,128)(2,1)} %copy.8) | copy-start | bytes 6291460
Sparse Core Ops, SparseCore 0:
  17.1 129.0 all-reduce.7
where the time goes:
time: 203 us; the launch traced here: 201 us
  local copies, waits for them, and re-layouts  69.9 us (34%)
  waiting for transfers between devices  46.8 us (23%)
  matrix products  43.1 us (21%)
  blocking collectives  17.6 us (9%)
  between operations  16.3 us (8%)
  other arithmetic  7.15 us (4%)
    psum x1, waiting for transfers between devices, broadcast(): return lax.psum(jnp.where(mine, value, jnp.zeros_like(value)), axis)  46.8 us
    dot_general x4, local copies, waits for them, and re-layouts, band_matrices(): jnp.einsum('skt,ltio->lskio', panel_prim, shift_ones, preferred_element_t...  37.1 us
    dot_general x4, matrix products, band_matrices(): jnp.einsum('skt,ltio->lskio', panel_prim, shift_ones, preferred_element_t...  25.6 us
    another operation x8, local copies, waits for them, and re-layouts, convolve(): stacked = jnp.stack([blocks, earlier])  23 us
    psum x1, blocking collectives, broadcast(): return lax.psum(jnp.where(mine, value, jnp.zeros_like(value)), axis)  17.6 us
    dot_general x4, matrix products, convolve(): jnp.einsum('lkrbi,lskio->srbo', stacked, bands, preferred_element_type=jn...  17.6 us
    unnamed x37, local copies, waits for them, and re-layouts  6.27 us
  transfers between devices with their start and end apart: 1, of which 1 were waited for; matrix products, arithmetic and copies ran while one was open for 32% of the time, Pallas kernels for 0%

commit v1 on v0

v1 whole, which is shorter than its diff:
```python
import functools

import jax
import jax.numpy as jnp
from jax import lax
from jax.experimental import pallas as pl
from jax.experimental.pallas import tpu as pltpu
from jax.sharding import PartitionSpec as P

CORE, ACROSS, DOWN = 1, 2, 4
SQUARE = 8
CHUNKS = 2
VMEM_BYTES = 56 * 1024 * 1024


def broadcast(value, axis, root):
    mine = lax.axis_index(axis) == root
    return lax.psum(jnp.where(mine, value, jnp.zeros_like(value)), axis)


def shift_table(taps, block):
    shape = (2, taps, block, block)
    lag_index, tap_index, in_index, out_index = (lax.broadcasted_iota(jnp.int32, shape, dim) for dim in range(4))
    distance = out_index - in_index + lag_index * block
    return (distance == tap_index).astype(jnp.bfloat16)


def band_matrices(panel_prim, shift_ones):
    bands = jnp.einsum("skt,ltio->lskio", panel_prim, shift_ones, preferred_element_type=jnp.float32)
    return bands.astype(jnp.bfloat16)


def convolve(traces, bands, block):
    point_count, row_count, length = traces.shape
    blocks = traces.reshape(point_count, row_count, length // block, block)
    earlier = jnp.concatenate([jnp.zeros_like(blocks[:, :, :1]), blocks[:, :, :-1]], axis=2)
    stacked = jnp.stack([blocks, earlier])
    product = jnp.einsum("lkrbi,lskio->srbo", stacked, bands, preferred_element_type=jnp.float32)
    return product.reshape(bands.shape[1], row_count, length)


def summed_broadcasts(data, surface_traces, primaries, panel_owner):
    points, taps = surface_traces.shape[0], primaries.shape[2]
    shift_ones = shift_table(taps, 2 * taps)
    summed = jnp.zeros(data.shape, jnp.float32)
    panels_here = primaries.shape[1] // points
    for panel_id in range(panel_owner.shape[0]):
        first_point = panel_id % panels_here * points
        panel_prim = broadcast(primaries, "rcv", panel_id // panels_here)[:, first_point : first_point + points]
        traces = broadcast(surface_traces, "shot", panel_owner[panel_id])
        summed = summed + convolve(traces, band_matrices(panel_prim, shift_ones), 2 * taps)
    return (data.astype(jnp.float32) - summed).astype(jnp.bfloat16)


def flip(value, bit):
    return lax.ppermute(value, "shot", [(i, i ^ bit) for i in range(SQUARE)])


def band_kernel(place_ref, taps_ref, band_ref):
    shots, points, width = taps_ref.shape[1:]
    rows = width // 2

    def point(k, carry):
        for s in range(shots):
            row = taps_ref[0, s, pl.ds(k, 1), :]
            spread = pltpu.roll(jnp.broadcast_to(row, (rows, width)), 0, 1, stride=1, stride_axis=0)
            band_ref[pl.ds(pl.multiple_of(k * rows, rows), rows), s * width : (s + 1) * width] = spread.astype(jnp.bfloat16)
        return carry

    lax.fori_loop(0, points, point, 0)


def bands_of(blocks, place):
    panels, shots, points, width = blocks.shape
    height = points * width // 2
    return pl.pallas_call(
        band_kernel,
        out_shape=jax.ShapeDtypeStruct((panels * height, shots * width), jnp.bfloat16),
        grid_spec=pltpu.PrefetchScalarGridSpec(
            num_scalar_prefetch=1,
            grid=(panels,),
            in_specs=[pl.BlockSpec((1, shots, points, width), lambda p, place: (lax.rem(place[2] - p + panels, panels), 0, 0, 0))],
            out_specs=pl.BlockSpec((height, shots * width), lambda p, place: (p, 0)),
        ),
        compiler_params=pltpu.CompilerParams(vmem_limit_bytes=VMEM_BYTES),
        cost_estimate=pl.CostEstimate(flops=panels * height * shots * width * 8, bytes_accessed=panels * height * shots * width * 2, transcendentals=0),
        name="bands",
    )(place, blocks)


def source_of(panel, owner_ref, chip):
    panels = owner_ref.shape[0]

    def held(place):
        count = jnp.int32(0)
        for other in range(panels):
            count = count + (owner_ref[other] // 2 == place).astype(jnp.int32)
        return count

    owner = owner_ref[panel]
    there, second = owner // 2, lax.rem(owner, 2) == 1
    both = held(there) == 2
    across_full, down_full = held(chip ^ 1) == 2, held(chip ^ 2) == 2
    own = jnp.where(both & second, 1, 0)
    across = jnp.where(both & second, 4, 2)
    down = jnp.where(both & jnp.logical_not(second), 5, 3)
    single = jnp.where(down_full, 4, 5)
    double = jnp.where(second, jnp.where(across_full, 7, 4), jnp.where(down_full, 6, 5))
    diagonal = jnp.where(both, double, single)
    return jnp.where(there == chip, own, jnp.where(there == (chip ^ 1), across, jnp.where(there == (chip ^ 2), down, diagonal)))


def residual_kernel(owner_ref, place_ref, *refs):
    count = len(refs) - 10
    sources = refs[:count]
    band_ref, mine_ref, other_ref, out_mine_ref, out_other_ref, window, spread, total, arrived, _ = refs[count:]
    panel = pl.program_id(0)
    panels = pl.num_programs(0)
    points, rows, length = window.shape[1:]
    width = 128
    half = width // 2
    blocks = length // half

    @pl.when(panel == 0)
    def _():
        for p in range(window.shape[0]):
            chosen = source_of(p, owner_ref, place_ref[0])
            for index, source in enumerate(sources):
                @pl.when(chosen == index)
                def _():
                    pltpu.make_async_copy(source, window.at[p], arrived.at[p]).start()

    pltpu.make_async_copy(sources[0], window.at[panel], arrived.at[panel]).wait()
    low = lax.broadcasted_iota(jnp.int32, (rows, width), 1) < half
    for j in range(points // 2):
        for c in range(length // width):
            first = window[panel, 2 * j, :, c * width : (c + 1) * width].astype(jnp.float32)
            second = window[panel, 2 * j + 1, :, c * width : (c + 1) * width].astype(jnp.float32)
            even = jnp.where(low, first, pltpu.roll(second, half, 1))
            odd = jnp.where(low, pltpu.roll(first, half, 1), second)
            spread[2 * c * rows : (2 * c + 1) * rows, j * width : (j + 1) * width] = even.astype(jnp.bfloat16)
            spread[(2 * c + 1) * rows : (2 * c + 2) * rows, j * width : (j + 1) * width] = odd.astype(jnp.bfloat16)
    product = jnp.dot(spread[...], band_ref[...], preferred_element_type=jnp.float32)

    @pl.when(panel == 0)
    def _():
        total[...] = product

    @pl.when(panel > 0)
    def _():
        total[...] += product

    @pl.when(panel == panels - 1)
    def _():
        shots = mine_ref.shape[0]
        for s in range(2 * shots):
            data_ref, out_ref = (mine_ref, out_mine_ref) if s < shots else (other_ref, out_other_ref)

            def part(b):
                return total[b * rows : (b + 1) * rows, s * width : (s + 1) * width]

            for c in range(length // width):
                before = part(2 * c - 1) if c > 0 else jnp.zeros((rows, width), jnp.float32)
                moved = pltpu.roll(jnp.where(low, part(2 * c + 1), before), half, 1)
                here = data_ref[s % shots, :, c * width : (c + 1) * width].astype(jnp.float32)
                out_ref[s % shots, :, c * width : (c + 1) * width] = (here - (part(2 * c) + moved)).astype(jnp.bfloat16)


def residual_of(chunk, owner, place, sources, bands, data, other_data):
    points, rows, length = sources[0].shape
    panels = owner.shape[0]
    shots = data.shape[0]
    height, columns = bands.shape[0] // panels, bands.shape[1]
    piece = jax.ShapeDtypeStruct((shots, rows, length), jnp.bfloat16)
    return pl.pallas_call(
        residual_kernel,
        out_shape=(piece, piece),
        grid_spec=pltpu.PrefetchScalarGridSpec(
            num_scalar_prefetch=2,
            grid=(panels,),
            in_specs=[pl.BlockSpec(memory_space=pl.ANY)] * len(sources)
            + [
                pl.BlockSpec((height, columns), lambda p, owner, place: (p, 0)),
                pl.BlockSpec((shots, rows, length), lambda p, owner, place: (0, place[1] * CHUNKS + chunk, 0)),
                pl.BlockSpec((shots, rows, length), lambda p, owner, place: (0, chunk, 0)),
            ],
            out_specs=[pl.BlockSpec((shots, rows, length), lambda p, owner, place: (0, 0, 0))] * 2,
            scratch_shapes=[
                pltpu.VMEM((panels, points, rows, length), jnp.bfloat16),
                pltpu.VMEM((rows * length // 64, height), jnp.bfloat16),
                pltpu.VMEM((rows * length // 64, columns), jnp.float32),
                pltpu.SemaphoreType.DMA((panels,)),
                pltpu.SemaphoreType.DMA,
            ],
        ),
        compiler_params=pltpu.CompilerParams(vmem_limit_bytes=VMEM_BYTES),
        cost_estimate=pl.CostEstimate(flops=2 * rows * length // 64 * bands.size, bytes_accessed=2 * bands.size, transcendentals=0),
        name="residual",
    )(owner, place, *sources, bands, data, other_data)


def square_shards(data, surface_traces, primaries, panel_owner):
    panels = panel_owner.shape[0]
    receivers = data.shape[1]
    side = receivers // 2
    rows = side // CHUNKS
    taps = primaries.shape[2]
    me = lax.axis_index("shot")
    core, chip = me % 2, me // 2
    first_owns = jnp.any(panel_owner == 2 * chip)
    second_owns = jnp.any(panel_owner == 2 * chip + 1)
    mine_is_a = first_owns == (core == 0)
    mine_is_b = second_owns == (core == 1)
    both = first_owns & second_owns
    holds_two = [jnp.sum(panel_owner // 2 == place) == 2 for place in range(SQUARE // 2)]
    neighbours_full = functools.reduce(
        jnp.logical_or, [holds_two[place] & holds_two[place ^ bit] for place in range(SQUARE // 2) for bit in (1, 2) if place < place ^ bit]
    )
    place = jnp.stack([chip, core, lax.axis_index("rcv")]).astype(jnp.int32)

    def run(third):
        own_a, own_b = [], []
        for chunk in range(CHUNKS):
            here = lax.dynamic_slice_in_dim(surface_traces, core * side + chunk * rows, rows, axis=1)
            there = lax.dynamic_slice_in_dim(surface_traces, (1 - core) * side + chunk * rows, rows, axis=1)
            met = flip(there, CORE)
            own_a.append(jnp.where(mine_is_a, here, met))
            own_b.append(jnp.where(mine_is_b, here, met))
        across = [flip(a, ACROSS) for a in own_a]
        down = [flip(b, DOWN) for b in own_b]

        ring = lax.axis_size("rcv")
        blocks = [primaries] + [lax.ppermute(primaries, "rcv", [(i, (i + j) % ring) for i in range(ring)]) for j in range(1, ring)]
        blocks = jnp.stack(blocks)
        blocks = jnp.concatenate([blocks, flip(blocks, CORE)], axis=1)
        blocks = jnp.pad(blocks.astype(jnp.float32), ((0, 0), (0, 0), (0, 0), (0, taps)))
        bands = bands_of(blocks, place)
        other_data = flip(lax.dynamic_slice_in_dim(data, (1 - core) * side, side, axis=1), CORE)

        kept, returned = [], []
        for chunk in range(CHUNKS):
            across_again = flip(jnp.where(both, own_b[chunk], down[chunk]), ACROSS)
            down_again = flip(jnp.where(both, own_a[chunk], across[chunk]), DOWN)
            sources = [own_a[chunk], own_b[chunk], across[chunk], down[chunk], across_again, down_again]
            if third:
                sources += [flip(down_again, ACROSS), flip(across_again, DOWN)]
            mine, others = residual_of(chunk, panel_owner, place, sources, bands, data, other_data)
            kept.append(mine)
            returned.append(flip(others, CORE))
        return jnp.where(core == 0, jnp.concatenate(kept + returned, axis=1), jnp.concatenate(returned + kept, axis=1))

    return lax.cond(neighbours_full, functools.partial(run, True), functools.partial(run, False))


def solution(mesh):
    placed = (P("shot", "rcv", None), P("shot", "rcv", None), P("shot", "rcv", None), P())
    shards = square_shards if mesh.shape["shot"] == SQUARE else summed_broadcasts
    return jax.shard_map(shards, mesh=mesh, in_specs=placed, out_specs=P("shot", "rcv", None), check_vma=False)
```

time: 203 us -> 91.4 us (0.45)
  local copies, waits for them, and re-layouts: 69.9 us -> 5.47 us
  matrix products: 43.1 us -> 0 us
  Pallas kernels: 0 us -> 31.8 us
  waiting for transfers between devices: 46.8 us -> 23.1 us
  blocking collectives: 17.6 us -> 0 us
  starting transfers between devices: 0.01 us -> 17.2 us
  between operations: 16.3 us -> 2.53 us
  loops' own time: 0 us -> 2.82 us
    psum x1 -> x0, waiting for transfers between devices: 46.8 us -> none  [broadcast(): return lax.psum(jnp.where(mine, value, jnp.zeros_like(value)), axis)]
    dot_general x8 -> x0, matrix products: 43.1 us -> none  [the longest x4 25.6 us: band_matrices(): jnp.einsum('skt,ltio->lskio', panel_prim, shift_ones, preferred_element_t...]
    dot_general x4 -> x0, local copies, waits for them, and re-layouts: 37.1 us -> none  [band_matrices(): jnp.einsum('skt,ltio->lskio', panel_prim, shift_ones, preferred_element_t...]
    pallas_call x0 -> x3, Pallas kernels: none -> 31.8 us  [the longest x2 20.8 us: residual_of(): pl.pallas_call(residual_kernel, out_shape=(piece, piece), grid_spec=pltpu...]
    ppermute x0 -> x17, waiting for transfers between devices: none -> 23.1 us  [the longest x14 23.1 us: flip(): return lax.ppermute(value, 'shot', [(i, i ^ bit) for i in range(SQUARE)])]
    another operation x8 -> x0, local copies, waits for them, and re-layouts: 23 us -> none  [convolve(): stacked = jnp.stack([blocks, earlier])]
    psum x1 -> x0, blocking collectives: 17.6 us -> none  [broadcast(): return lax.psum(jnp.where(mine, value, jnp.zeros_like(value)), axis)]
    ppermute x0 -> x17, starting transfers between devices: none -> 17.2 us  [the longest x14 12.5 us: flip(): return lax.ppermute(value, 'shot', [(i, i ^ bit) for i in range(SQUARE)])]
  transfers between devices with their start and end apart: 1 -> 17, of which waited for: 1 -> 6; matrix products, arithmetic and copies ran while one was open for 32% -> 3% of each run, Pallas kernels for 0% -> 35%
where the time goes in v1:
time: 91.4 us; the launch traced here: 90.8 us
  Pallas kernels  31.8 us (35%)
  waiting for transfers between devices  23.1 us (25%)
  starting transfers between devices  17.2 us (19%)
  other arithmetic  7.89 us (9%)
  local copies, waits for them, and re-layouts  5.47 us (6%)
  loops' own time  2.82 us (3%)
  between operations  2.53 us (3%)
    ppermute x14, waiting for transfers between devices, flip(): return lax.ppermute(value, 'shot', [(i, i ^ bit) for i in range(SQUARE)])  23.1 us
    pallas_call x2, Pallas kernels, residual_of(): pl.pallas_call(residual_kernel, out_shape=(piece, piece), grid_spec=pltpu...  20.8 us
    ppermute x14, starting transfers between devices, flip(): return lax.ppermute(value, 'shot', [(i, i ^ bit) for i in range(SQUARE)])  12.5 us
    pallas_call x1, Pallas kernels, bands_of(): pl.pallas_call(band_kernel, out_shape=jax.ShapeDtypeStruct((panels * heig...  11 us
    ppermute x3, starting transfers between devices, run(): lax.ppermute(primaries, 'rcv', [(i, (i + j) % ring) for i in range(ring)])  4.67 us
    another operation x1, loops' own time, square_shards(): lax.cond(neighbours_full, functools.partial(run, True), functools.partial...  2.82 us
    select_n x2, other arithmetic, run(): own_b.append(jnp.where(mine_is_b, here, met))  2.74 us
    cond x34, local copies, waits for them, and re-layouts  2.72 us
  transfers between devices with their start and end apart: 17, of which 6 were waited for; matrix products, arithmetic and copies ran while one was open for 3% of the time, Pallas kernels for 35%

profile of v1, /device:TPU:1, one launch (start us, length us, event | category | flops | bytes accessed | tf_op | source)
XLA Modules:
  0.0 90.8 jit_solution(9998233162237186263)
XLA Ops:
  0.0 0.1 pad_add_fusion
  0.1 1.3 %compare_reduce_fusion = (pred[]{:T(512)}, pred[]{:T(512)}) fusion(s32[4]{0:T(128)} %param.9, s32[]{:T(128)S(6)} %add.60, s32[]{:T(128)S(6)} %mul.15), kind=kLoop, calls=%fused_computation.48 | loop fusion | flops 14 | bytes 26 | tf_op jit(solution)/shard_map/reduce_or | solution.py:211
  1.4 1.4 %fusion.23 = (s32[]{:T(128)}, s32[]{:T(128)}, s32[]{:T(128)}, s32[]{:T(128)}) fusion(s32[4]{0:T(128)} %param.9), kind=kLoop, calls=%fused_computation.61 | loop fusion | flops 104 | bytes 32 | tf_op jit(solution)/shard_map/reduce_sum | solution.py:215
  5.3 84.6 %conditional.1 = (bf16[6,256,256]{2,1,0:T(8,128)(2,1)S(1)}) conditional(s32[]{:T(128)} %convert_element_type.24, (s32[]{:T(128)}, pred[]{:T(512)}, bf16[16,256,256]{2,1,0:T(8,128)(2,1)}, pred[]{:T(512)}, pred[]{:T(512)}, /*index=5*/bf16[6,16,64]{2,1,0:T(8,128)(2,1)}, s32[3]{0:T(128)S(1)}, bf16[6,256,256]{2,1,0:T(8,128)(2,1)}, s32[4]{0:T(128)}, ...), branch_computations={%region_6.7_spmd, %region_7.8_spmd} | conditional | flops 6503211008 | bytes 125241032 | solution.py:252
  5.3 1.1 %constant_dynamic-slice_fusion.2 = bf16[16,64,256]{2,1,0:T(8,128)(2,1)S(1)} fusion(bf16[16,256,256]{2,1,0:T(8,128)(2,1)} %get-tuple-element.93, s32[]{:T(128)S(6)} %select_n.103), kind=kLoop, calls=%fused_computation.23 | loop fusion | bytes 1048580 | tf_op jit(solution)/shard_map/cond/branch_0_fun/dynamic_slice | solution.py:225
  6.4 0.1 collective-permute-start
  7.7 0.0 copy-start.33
  7.7 0.6 collective-permute-done
  8.4 1.5 %broadcast_select_fusion.5 = (bf16[16,64,256]{2,1,0:T(8,128)(2,1)S(1)}, bf16[16,64,256]{2,1,0:T(8,128)(2,1)S(1)}, bf16[16,64,256]{2,1,0:T(8,128)(2,1)S(1)}) fusion(bf16[16,64,256]{2,1,0:T(8,128)(2,1)S(1)} %collective-permute-done, pred[]{:T(512)S(6)} %eq.74, bf16[16,256,256]{2,1,0:T(8,128)(2,1)} %get-tuple-element.93, s32[]{:T(128)S(6)} %select_n.102, ...), kind=kLoop, calls=%fused_computation.6 | loop fusion | flops 524288 | bytes 3145738 | tf_op jit(solution)/shard_map/cond/branch_0_fun/jit(_where)/select_n | solution.py:228
  9.9 0.2 collective-permute-start.10
  10.1 2.6 %collective-permute-start.2 = (bf16[16,64,256]{2,1,0:T(8,128)(2,1)S(1)}, bf16[16,64,256]{2,1,0:T(8,128)(2,1)S(1)}, u32[]{:S(2)}, u32[]{:S(2)}) collective-permute-start(bf16[16,64,256]{2,1,0:T(8,128)(2,1)S(1)} %get-tuple-element.109.refs_1_), channel_id=1, source_target_pairs={{0,16},{4,20},{8,24},{12,28},{16,0},{20,4},{24,8},{28,12},{1,17},{... | collective-permute-start | bytes 1572872 | tf_op jit(solution)/shard_map/cond/branch_0_fun/ppermute | solution.py:56
  12.7 1.3 %collective-permute-start.5 = (bf16[6,16,64]{2,1,0:T(8,128)(2,1)S(1)}, bf16[6,16,64]{2,1,0:T(8,128)(2,1)S(1)}, u32[]{:S(2)}, u32[]{:S(2)}) collective-permute-start(bf16[6,16,64]{2,1,0:T(8,128)(2,1)S(1)} %copy-done.33), channel_id=1, source_target_pairs={{0,1},{1,2},{2,3},{3,0},{4,5},{5,6},{6,7},{7,4},{8,9},{9,10},{10,1... | collective-permute-start | bytes 36872 | tf_op jit(solution)/shard_map/cond/branch_0_fun/ppermute | solution.py:233
  14.0 2.3 %collective-permute-start.6 = (bf16[6,16,64]{2,1,0:T(8,128)(2,1)S(1)}, bf16[6,16,64]{2,1,0:T(8,128)(2,1)S(1)}, u32[]{:S(2)}, u32[]{:S(2)}) collective-permute-start(bf16[6,16,64]{2,1,0:T(8,128)(2,1)S(1)} %copy-done.33), channel_id=1, source_target_pairs={{0,2},{1,3},{2,0},{3,1},{4,6},{5,7},{6,4},{7,5},{8,10},{9,11},{10,... | collective-permute-start | bytes 36872 | tf_op jit(solution)/shard_map/cond/branch_0_fun/ppermute | solution.py:233
  16.3 1.1 %collective-permute-start.7 = (bf16[6,16,64]{2,1,0:T(8,128)(2,1)S(1)}, bf16[6,16,64]{2,1,0:T(8,128)(2,1)S(1)}, u32[]{:S(2)}, u32[]{:S(2)}) collective-permute-start(bf16[6,16,64]{2,1,0:T(8,128)(2,1)S(1)} %copy-done.33), channel_id=1, source_target_pairs={{0,3},{1,0},{2,1},{3,2},{4,7},{5,4},{6,5},{7,6},{8,11},{9,8},{10,9... | collective-permute-start | bytes 36872 | tf_op jit(solution)/shard_map/cond/branch_0_fun/ppermute | solution.py:233
  17.4 0.8 constant_dynamic-slice_fusion.1
  19.4 1.3 %collective-permute-start.9 = (bf16[6,128,256]{2,1,0:T(8,128)(2,1)}, bf16[6,128,256]{2,1,0:T(8,128)(2,1)S(1)}, u32[]{:S(2)}, u32[]{:S(2)}) collective-permute-start(bf16[6,128,256]{2,1,0:T(8,128)(2,1)} %constant_dynamic-slice_fusion.1), channel_id=1, source_target_pairs={{0,4},{4,0},{8,12},{12,8},{16,20},{20,16},{24,28},{28,24},{1,5},{5... | collective-permute-start | bytes 1179656 | tf_op jit(solution)/shard_map/cond/branch_0_fun/ppermute | solution.py:56
  20.8 0.5 collective-permute-start.8
  21.2 1.2 %collective-permute-start.1 = (bf16[16,64,256]{2,1,0:T(8,128)(2,1)S(1)}, bf16[16,64,256]{2,1,0:T(8,128)(2,1)S(1)}, u32[]{:S(2)}, u32[]{:S(2)}) collective-permute-start(bf16[16,64,256]{2,1,0:T(8,128)(2,1)S(1)} %get-tuple-element.110.refs_0_), channel_id=1, source_target_pairs={{0,8},{4,12},{8,0},{12,4},{16,24},{20,28},{24,16},{28,20},{1,9},{5... | collective-permute-start | bytes 1572872 | tf_op jit(solution)/shard_map/cond/branch_0_fun/ppermute | solution.py:56
  22.5 1.3 %broadcast_select_fusion.4 = (bf16[16,64,256]{2,1,0:T(8,128)(2,1)S(1)}, bf16[16,64,256]{2,1,0:T(8,128)(2,1)S(1)}) fusion(bf16[16,64,256]{2,1,0:T(8,128)(2,1)S(1)} %collective-permute-done.10, pred[]{:T(512)S(6)} %eq.74, bf16[16,256,256]{2,1,0:T(8,128)(2,1)} %get-tuple-element.93, s32[]{:T(128)S(6)} %select_n.110, pred[]{:T(512)S(6)} %eq.72), kind=kLoop, calls=%fused_computation.5 | loop fusion | flops 524288 | bytes 2097158 | tf_op jit(solution)/shard_map/cond/branch_0_fun/jit(_where)/select_n | solution.py:228
  23.7 0.0 copy-start.9
  23.8 0.3 collective-permute-start.11
  24.1 0.8 collective-permute-done.2.refs_3_
  24.9 0.1 broadcast_select_fusion.3
  25.0 1.3 %collective-permute-start.3 = (bf16[16,64,256]{2,1,0:T(8,128)(2,1)S(1)}, bf16[16,64,256]{2,1,0:T(8,128)(2,1)S(1)}, u32[]{:S(2)}, u32[]{:S(2)}) collective-permute-start(bf16[16,64,256]{2,1,0:T(8,128)(2,1)S(1)} %broadcast_select_fusion.3), channel_id=1, source_target_pairs={{0,8},{4,12},{8,0},{12,4},{16,24},{20,28},{24,16},{28,20},{1,9},{5... | collective-permute-start | bytes 1572872 | tf_op jit(solution)/shard_map/cond/branch_0_fun/ppermute | solution.py:56
  26.2 8.5 %collective-permute-done.1.refs_2_ = bf16[16,64,256]{2,1,0:T(8,128)(2,1)S(1)} collective-permute-done((bf16[16,64,256]{2,1,0:T(8,128)(2,1)S(1)}, bf16[16,64,256]{2,1,0:T(8,128)(2,1)S(1)}, u32[]{:S(2)}, u32[]{:S(2)}) %collective-permute-start.1) | collective-permute-done | bytes 524320 | tf_op jit(solution)/shard_map/cond/branch_0_fun/ppermute | solution.py:56
  34.7 0.2 collective-permute-start.12
  35.0 0.1 broadcast_select_fusion.2
  35.0 10.9 %collective-permute-done.11.refs_2_ = bf16[16,64,256]{2,1,0:T(8,128)(2,1)S(1)} collective-permute-done((bf16[16,64,256]{2,1,0:T(8,128)(2,1)S(1)}, bf16[16,64,256]{2,1,0:T(8,128)(2,1)S(1)}, u32[]{:S(2)}, u32[]{:S(2)}) %collective-permute-start.11) | collective-permute-done | bytes 524320 | tf_op jit(solution)/shard_map/cond/branch_0_fun/ppermute | solution.py:56
  46.0 0.2 collective-permute-start.4
  46.2 0.1 broadcast_select_fusion
  46.3 0.6 collective-permute-done.12.refs_3_
  46.8 0.8 collective-permute-start.14
  47.6 0.1 broadcast_select_fusion.1
  47.7 1.3 %collective-permute-start.13 = (bf16[16,64,256]{2,1,0:T(8,128)(2,1)S(1)}, bf16[16,64,256]{2,1,0:T(8,128)(2,1)S(1)}, u32[]{:S(2)}, u32[]{:S(2)}) collective-permute-start(bf16[16,64,256]{2,1,0:T(8,128)(2,1)S(1)} %broadcast_select_fusion.1), channel_id=1, source_target_pairs={{0,8},{4,12},{8,0},{12,4},{16,24},{20,28},{24,16},{28,20},{1,9},{5... | collective-permute-start | bytes 1572872 | tf_op jit(solution)/shard_map/cond/branch_0_fun/ppermute | solution.py:56
  49.0 0.8 fusion.9.taps_ref
  49.8 11.0 %bands.2.refs_6_ = bf16[4096,1536]{1,0:T(8,128)(2,1)} custom-call(s32[3]{0:T(128)S(1)} %get-tuple-element.46.place_ref, f32[4,12,16,128]{3,2,1,0:T(8,128)} %fusion.9.taps_ref), custom_call_target="tpu_custom_call" | custom-call | flops 50331648 | bytes 12582912 | tf_op jit(solution)/shard_map/cond/branch_0_fun/bands/pallas_call | solution.py:76
  60.8 0.7 copy-done.18
  61.5 0.2 copy-done.27
  61.7 0.2 copy-done.32
  61.9 10.4 %residual.4 = (bf16[6,64,256]{2,1,0:T(8,128)(2,1)}, bf16[6,64,256]{2,1,0:T(8,128)(2,1)}) custom-call(s32[4]{0:T(128)S(1)} %copy-done.37, s32[3]{0:T(128)S(1)} %get-tuple-element.46.place_ref, bf16[16,64,256]{2,1,0:T(8,128)(2,1)} %copy-done.7, bf16[16,64,256]{2,1,0:T(8,128)(2,1)} %copy-done.6, bf16[16,64,256]{2,1,0:T(8,128)(2,1)} %copy-done.16, ...), custom_call_target="tpu_custom_call" | custom-call | flops 3221225472 | bytes 12582912 | tf_op jit(solution)/shard_map/cond/branch_0_fun/residual/pallas_call | solution.py:175
  72.3 2.3 %collective-permute-start.15 = (bf16[6,64,256]{2,1,0:T(8,128)(2,1)}, bf16[6,64,256]{2,1,0:T(8,128)(2,1)S(1)}, u32[]{:S(2)}, u32[]{:S(2)}) collective-permute-start(bf16[6,64,256]{2,1,0:T(8,128)(2,1)} %get-tuple-element.55), channel_id=1, source_target_pairs={{0,4},{4,0},{8,12},{12,8},{16,20},{20,16},{24,28},{28,24},{1,5},{5... | collective-permute-start | bytes 589832 | tf_op jit(solution)/shard_map/cond/branch_0_fun/ppermute | solution.py:56
  74.7 0.8 copy-done.28
  75.5 0.8 copy-done.30
  76.3 10.4 %residual.5 = (bf16[6,64,256]{2,1,0:T(8,128)(2,1)}, bf16[6,64,256]{2,1,0:T(8,128)(2,1)}) custom-call(s32[4]{0:T(128)S(1)} %copy-done.37, s32[3]{0:T(128)S(1)} %get-tuple-element.46.place_ref, bf16[16,64,256]{2,1,0:T(8,128)(2,1)} %copy-done.9, bf16[16,64,256]{2,1,0:T(8,128)(2,1)} %copy-done.8, bf16[16,64,256]{2,1,0:T(8,128)(2,1)} %copy-done.15, ...), custom_call_target="tpu_custom_call" | custom-call | flops 3221225472 | bytes 12582912 | tf_op jit(solution)/shard_map/cond/branch_0_fun/residual/pallas_call | solution.py:175
  86.7 0.1 collective-permute-start.16
  86.8 1.6 %collective-permute-done.16 = bf16[6,64,256]{2,1,0:T(8,128)(2,1)S(1)} collective-permute-done((bf16[6,64,256]{2,1,0:T(8,128)(2,1)}, bf16[6,64,256]{2,1,0:T(8,128)(2,1)S(1)}, u32[]{:S(2)}, u32[]{:S(2)}) %collective-permute-start.16) | collective-permute-done | bytes 196640 | tf_op jit(solution)/shard_map/cond/branch_0_fun/ppermute | solution.py:56
  88.4 1.3 %maximum_select_fusion = bf16[6,256,256]{2,1,0:T(8,128)(2,1)S(1)} fusion(bf16[6,64,256]{2,1,0:T(8,128)(2,1)S(1)} %collective-permute-done.16, bf16[6,64,256]{2,1,0:T(8,128)(2,1)S(1)} %collective-permute-done.15, bf16[6,64,256]{2,1,0:T(8,128)(2,1)} %get-tuple-element.54, bf16[6,64,256]{2,1,0:T(8,128)(2,1)S(1)} %copy-done.36, pred[]{:T(512)S(6)} %eq.38), kind=kLoop, calls=%fused_computation | loop fusion | flops 6684672 | bytes 1572865 | tf_op jit(solution)/shard_map/cond/branch_0_fun/jit(_where)/select_n | solution.py:250
  89.9 0.9 copy-done.20
  (40 shorter events, 0.1 us)
Async XLA Ops:
  6.4 2.0 %collective-permute-start = (bf16[16,64,256]{2,1,0:T(8,128)(2,1)S(1)}, bf16[16,64,256]{2,1,0:T(8,128)(2,1)S(1)}, u32[]{:S(2)}, u32[]{:S(2)}) collective-permute-start(bf16[16,64,256]{2,1,0:T(8,128)(2,1)S(1)} %constant_dynamic-slice_fusion.2), channel_id=1, source_target_pairs={{0,4},{4,0},{8,12},{12,8},{16,20},{20,16},{24,28},{28,24},{1,5},{5... | collective-permute-start | bytes 1572872 | tf_op jit(solution)/shard_map/cond/branch_0_fun/ppermute | solution.py:56
  7.7 5.0 %copy-start.33 = (bf16[6,16,64]{2,1,0:T(8,128)(2,1)S(1)}, bf16[6,16,64]{2,1,0:T(8,128)(2,1)}, u32[]{:S(2)}) copy-start(bf16[6,16,64]{2,1,0:T(8,128)(2,1)} %get-tuple-element.99) | copy-start | bytes 36868 | tf_op jit(solution)/shard_map/cond
  7.7 9.7 %copy-start = (bf16[6,256,256]{2,1,0:T(8,128)(2,1)S(1)}, bf16[6,256,256]{2,1,0:T(8,128)(2,1)}, u32[]{:S(2)}) copy-start(bf16[6,256,256]{2,1,0:T(8,128)(2,1)} %get-tuple-element.101.refs_7_) | copy-start | bytes 2359300 | tf_op jit(solution)/shard_map/cond
  9.9 15.1 %copy-start.6 = (bf16[16,64,256]{2,1,0:T(8,128)(2,1)}, bf16[16,64,256]{2,1,0:T(8,128)(2,1)S(1)}, u32[]{:S(2)}) copy-start(bf16[16,64,256]{2,1,0:T(8,128)(2,1)S(1)} %get-tuple-element.109.refs_1_) | copy-start | bytes 1572868 | tf_op jit(solution)/shard_map/cond
  9.9 25.1 %copy-start.7 = (bf16[16,64,256]{2,1,0:T(8,128)(2,1)}, bf16[16,64,256]{2,1,0:T(8,128)(2,1)S(1)}, u32[]{:S(2)}) copy-start(bf16[16,64,256]{2,1,0:T(8,128)(2,1)S(1)} %get-tuple-element.110.refs_0_) | copy-start | bytes 1572868 | tf_op jit(solution)/shard_map/cond
  9.9 12.6 %collective-permute-start.10 = (bf16[16,64,256]{2,1,0:T(8,128)(2,1)S(1)}, bf16[16,64,256]{2,1,0:T(8,128)(2,1)S(1)}, u32[]{:S(2)}, u32[]{:S(2)}) collective-permute-start(bf16[16,64,256]{2,1,0:T(8,128)(2,1)S(1)} %get-tuple-element.113), channel_id=1, source_target_pairs={{0,4},{4,0},{8,12},{12,8},{16,20},{20,16},{24,28},{28,24},{1,5},{5... | collective-permute-start | bytes 1572872 | tf_op jit(solution)/shard_map/cond/branch_0_fun/ppermute | solution.py:56
  10.1 14.8 %collective-permute-start.2 = (bf16[16,64,256]{2,1,0:T(8,128)(2,1)S(1)}, bf16[16,64,256]{2,1,0:T(8,128)(2,1)S(1)}, u32[]{:S(2)}, u32[]{:S(2)}) collective-permute-start(bf16[16,64,256]{2,1,0:T(8,128)(2,1)S(1)} %get-tuple-element.109.refs_1_), channel_id=1, source_target_pairs={{0,16},{4,20},{8,24},{12,28},{16,0},{20,4},{24,8},{28,12},{1,17},{... | collective-permute-start | bytes 1572872 | tf_op jit(solution)/shard_map/cond/branch_0_fun/ppermute | solution.py:56
  12.7 6.6 %collective-permute-start.5 = (bf16[6,16,64]{2,1,0:T(8,128)(2,1)S(1)}, bf16[6,16,64]{2,1,0:T(8,128)(2,1)S(1)}, u32[]{:S(2)}, u32[]{:S(2)}) collective-permute-start(bf16[6,16,64]{2,1,0:T(8,128)(2,1)S(1)} %copy-done.33), channel_id=1, source_target_pairs={{0,1},{1,2},{2,3},{3,0},{4,5},{5,6},{6,7},{7,4},{8,9},{9,10},{10,1... | collective-permute-start | bytes 36872 | tf_op jit(solution)/shard_map/cond/branch_0_fun/ppermute | solution.py:233
  14.0 6.7 %collective-permute-start.6 = (bf16[6,16,64]{2,1,0:T(8,128)(2,1)S(1)}, bf16[6,16,64]{2,1,0:T(8,128)(2,1)S(1)}, u32[]{:S(2)}, u32[]{:S(2)}) collective-permute-start(bf16[6,16,64]{2,1,0:T(8,128)(2,1)S(1)} %copy-done.33), channel_id=1, source_target_pairs={{0,2},{1,3},{2,0},{3,1},{4,6},{5,7},{6,4},{7,5},{8,10},{9,11},{10,... | collective-permute-start | bytes 36872 | tf_op jit(solution)/shard_map/cond/branch_0_fun/ppermute | solution.py:233
  16.3 4.4 %collective-permute-start.7 = (bf16[6,16,64]{2,1,0:T(8,128)(2,1)S(1)}, bf16[6,16,64]{2,1,0:T(8,128)(2,1)S(1)}, u32[]{:S(2)}, u32[]{:S(2)}) collective-permute-start(bf16[6,16,64]{2,1,0:T(8,128)(2,1)S(1)} %copy-done.33), channel_id=1, source_target_pairs={{0,3},{1,0},{2,1},{3,2},{4,7},{5,4},{6,5},{7,6},{8,11},{9,8},{10,9... | collective-permute-start | bytes 36872 | tf_op jit(solution)/shard_map/cond/branch_0_fun/ppermute | solution.py:233
  19.4 41.4 %collective-permute-start.9 = (bf16[6,128,256]{2,1,0:T(8,128)(2,1)}, bf16[6,128,256]{2,1,0:T(8,128)(2,1)S(1)}, u32[]{:S(2)}, u32[]{:S(2)}) collective-permute-start(bf16[6,128,256]{2,1,0:T(8,128)(2,1)} %constant_dynamic-slice_fusion.1), channel_id=1, source_target_pairs={{0,4},{4,0},{8,12},{12,8},{16,20},{20,16},{24,28},{28,24},{1,5},{5... | collective-permute-start | bytes 1179656 | tf_op jit(solution)/shard_map/cond/branch_0_fun/ppermute | solution.py:56
  20.8 26.9 %collective-permute-start.8 = (bf16[4,6,16,64]{3,2,1,0:T(8,128)(2,1)S(1)}, bf16[4,6,16,64]{3,2,1,0:T(8,128)(2,1)S(1)}, u32[]{:S(2)}, u32[]{:S(2)}) collective-permute-start(bf16[4,6,16,64]{3,2,1,0:T(8,128)(2,1)S(1)} %pad_maximum_fusion), channel_id=1, source_target_pairs={{0,4},{4,0},{8,12},{12,8},{16,20},{20,16},{24,28},{28,24},{1,5},{5... | collective-permute-start | bytes 147464 | tf_op jit(solution)/shard_map/cond/branch_0_fun/ppermute | solution.py:56
  21.2 13.5 %collective-permute-start.1 = (bf16[16,64,256]{2,1,0:T(8,128)(2,1)S(1)}, bf16[16,64,256]{2,1,0:T(8,128)(2,1)S(1)}, u32[]{:S(2)}, u32[]{:S(2)}) collective-permute-start(bf16[16,64,256]{2,1,0:T(8,128)(2,1)S(1)} %get-tuple-element.110.refs_0_), channel_id=1, source_target_pairs={{0,8},{4,12},{8,0},{12,4},{16,24},{20,28},{24,16},{28,20},{1,9},{5... | collective-permute-start | bytes 1572872 | tf_op jit(solution)/shard_map/cond/branch_0_fun/ppermute | solution.py:56
  23.7 22.5 %copy-start.9 = (bf16[16,64,256]{2,1,0:T(8,128)(2,1)}, bf16[16,64,256]{2,1,0:T(8,128)(2,1)S(1)}, u32[]{:S(2)}) copy-start(bf16[16,64,256]{2,1,0:T(8,128)(2,1)S(1)} %get-tuple-element.112.refs_0_) | copy-start | bytes 1572868 | tf_op jit(solution)/shard_map/cond
  23.7 23.9 %copy-start.8 = (bf16[16,64,256]{2,1,0:T(8,128)(2,1)}, bf16[16,64,256]{2,1,0:T(8,128)(2,1)S(1)}, u32[]{:S(2)}) copy-start(bf16[16,64,256]{2,1,0:T(8,128)(2,1)S(1)} %get-tuple-element.111.refs_1_) | copy-start | bytes 1572868 | tf_op jit(solution)/shard_map/cond
  23.8 22.2 %collective-permute-start.11 = (bf16[16,64,256]{2,1,0:T(8,128)(2,1)S(1)}, bf16[16,64,256]{2,1,0:T(8,128)(2,1)S(1)}, u32[]{:S(2)}, u32[]{:S(2)}) collective-permute-start(bf16[16,64,256]{2,1,0:T(8,128)(2,1)S(1)} %get-tuple-element.112.refs_0_), channel_id=1, source_target_pairs={{0,8},{4,12},{8,0},{12,4},{16,24},{20,28},{24,16},{28,20},{1,9},{5... | collective-permute-start | bytes 1572872 | tf_op jit(solution)/shard_map/cond/branch_0_fun/ppermute | solution.py:56
  24.9 10.2 %copy-start.14 = (bf16[16,64,256]{2,1,0:T(8,128)(2,1)}, bf16[16,64,256]{2,1,0:T(8,128)(2,1)S(1)}, u32[]{:S(2)}) copy-start(bf16[16,64,256]{2,1,0:T(8,128)(2,1)S(1)} %collective-permute-done.2.refs_3_) | copy-start | bytes 1572868 | tf_op jit(solution)/shard_map/cond
  25.0 35.8 %collective-permute-start.3 = (bf16[16,64,256]{2,1,0:T(8,128)(2,1)S(1)}, bf16[16,64,256]{2,1,0:T(8,128)(2,1)S(1)}, u32[]{:S(2)}, u32[]{:S(2)}) collective-permute-start(bf16[16,64,256]{2,1,0:T(8,128)(2,1)S(1)} %broadcast_select_fusion.3), channel_id=1, source_target_pairs={{0,8},{4,12},{8,0},{12,4},{16,24},{20,28},{24,16},{28,20},{1,9},{5... | collective-permute-start | bytes 1572872 | tf_op jit(solution)/shard_map/cond/branch_0_fun/ppermute | solution.py:56
  34.7 11.5 %copy-start.16 = (bf16[16,64,256]{2,1,0:T(8,128)(2,1)}, bf16[16,64,256]{2,1,0:T(8,128)(2,1)S(1)}, u32[]{:S(2)}) copy-start(bf16[16,64,256]{2,1,0:T(8,128)(2,1)S(1)} %collective-permute-done.1.refs_2_) | copy-start | bytes 1572868 | tf_op jit(solution)/shard_map/cond
  34.7 12.1 %collective-permute-start.12 = (bf16[16,64,256]{2,1,0:T(8,128)(2,1)S(1)}, bf16[16,64,256]{2,1,0:T(8,128)(2,1)S(1)}, u32[]{:S(2)}, u32[]{:S(2)}) collective-permute-start(bf16[16,64,256]{2,1,0:T(8,128)(2,1)S(1)} %get-tuple-element.111.refs_1_), channel_id=1, source_target_pairs={{0,16},{4,20},{8,24},{12,28},{16,0},{20,4},{24,8},{28,12},{1,17},{... | collective-permute-start | bytes 1572872 | tf_op jit(solution)/shard_map/cond/branch_0_fun/ppermute | solution.py:56
  46.0 1.7 %copy-start.15 = (bf16[16,64,256]{2,1,0:T(8,128)(2,1)}, bf16[16,64,256]{2,1,0:T(8,128)(2,1)S(1)}, u32[]{:S(2)}) copy-start(bf16[16,64,256]{2,1,0:T(8,128)(2,1)S(1)} %collective-permute-done.11.refs_2_) | copy-start | bytes 1572868 | tf_op jit(solution)/shard_map/cond
  46.0 14.8 %collective-permute-start.4 = (bf16[16,64,256]{2,1,0:T(8,128)(2,1)S(1)}, bf16[16,64,256]{2,1,0:T(8,128)(2,1)S(1)}, u32[]{:S(2)}, u32[]{:S(2)}) collective-permute-start(bf16[16,64,256]{2,1,0:T(8,128)(2,1)S(1)} %broadcast_select_fusion.2), channel_id=1, source_target_pairs={{0,16},{4,20},{8,24},{12,28},{16,0},{20,4},{24,8},{28,12},{1,17},{... | collective-permute-start | bytes 1572872 | tf_op jit(solution)/shard_map/cond/branch_0_fun/ppermute | solution.py:56
  46.8 13.9 %copy-start.17 = (bf16[16,64,256]{2,1,0:T(8,128)(2,1)}, bf16[16,64,256]{2,1,0:T(8,128)(2,1)S(1)}, u32[]{:S(2)}) copy-start(bf16[16,64,256]{2,1,0:T(8,128)(2,1)S(1)} %collective-permute-done.12.refs_3_) | copy-start | bytes 1572868 | tf_op jit(solution)/shard_map/cond
  46.8 27.9 %collective-permute-start.14 = (bf16[16,64,256]{2,1,0:T(8,128)(2,1)S(1)}, bf16[16,64,256]{2,1,0:T(8,128)(2,1)S(1)}, u32[]{:S(2)}, u32[]{:S(2)}) collective-permute-start(bf16[16,64,256]{2,1,0:T(8,128)(2,1)S(1)} %broadcast_select_fusion), channel_id=1, source_target_pairs={{0,16},{4,20},{8,24},{12,28},{16,0},{20,4},{24,8},{28,12},{1,17},{... | collective-permute-start | bytes 1572872 | tf_op jit(solution)/shard_map/cond/branch_0_fun/ppermute | solution.py:56
  47.7 27.0 %collective-permute-start.13 = (bf16[16,64,256]{2,1,0:T(8,128)(2,1)S(1)}, bf16[16,64,256]{2,1,0:T(8,128)(2,1)S(1)}, u32[]{:S(2)}, u32[]{:S(2)}) collective-permute-start(bf16[16,64,256]{2,1,0:T(8,128)(2,1)S(1)} %broadcast_select_fusion.1), channel_id=1, source_target_pairs={{0,8},{4,12},{8,0},{12,4},{16,24},{20,28},{24,16},{28,20},{1,9},{5... | collective-permute-start | bytes 1572872 | tf_op jit(solution)/shard_map/cond/branch_0_fun/ppermute | solution.py:56
  49.8 12.1 %copy-start.37 = (s32[4]{0:T(128)S(1)}, s32[4]{0:T(128)}, u32[]{:S(2)}) copy-start(s32[4]{0:T(128)} %get-tuple-element.45.owner_ref) | copy-start | bytes 52 | tf_op jit(solution)/shard_map/cond
  60.8 0.8 copy-start.18
  60.8 0.9 %copy-start.27 = (bf16[16,64,256]{2,1,0:T(8,128)(2,1)}, bf16[16,64,256]{2,1,0:T(8,128)(2,1)S(1)}, u32[]{:S(2)}) copy-start(bf16[16,64,256]{2,1,0:T(8,128)(2,1)S(1)} %collective-permute-done.3.refs_4_) | copy-start | bytes 1572868 | tf_op jit(solution)/shard_map/cond
  60.8 1.1 %copy-start.32 = (bf16[16,64,256]{2,1,0:T(8,128)(2,1)}, bf16[16,64,256]{2,1,0:T(8,128)(2,1)S(1)}, u32[]{:S(2)}) copy-start(bf16[16,64,256]{2,1,0:T(8,128)(2,1)S(1)} %collective-permute-done.4.refs_5_) | copy-start | bytes 1572868 | tf_op jit(solution)/shard_map/cond
  72.3 16.1 %copy-start.36 = (bf16[6,64,256]{2,1,0:T(8,128)(2,1)S(1)}, bf16[6,64,256]{2,1,0:T(8,128)(2,1)}, u32[]{:S(2)}) copy-start(bf16[6,64,256]{2,1,0:T(8,128)(2,1)} %get-tuple-element.53) | copy-start | bytes 589828 | tf_op jit(solution)/shard_map/cond
  72.3 14.5 %collective-permute-start.15 = (bf16[6,64,256]{2,1,0:T(8,128)(2,1)}, bf16[6,64,256]{2,1,0:T(8,128)(2,1)S(1)}, u32[]{:S(2)}, u32[]{:S(2)}) collective-permute-start(bf16[6,64,256]{2,1,0:T(8,128)(2,1)} %get-tuple-element.55), channel_id=1, source_target_pairs={{0,4},{4,0},{8,12},{12,8},{16,20},{20,16},{24,28},{28,24},{1,5},{5... | collective-permute-start | bytes 589832 | tf_op jit(solution)/shard_map/cond/branch_0_fun/ppermute | solution.py:56
  74.7 0.8 copy-start.28
  75.5 0.8 copy-start.30
  86.7 1.7 %collective-permute-start.16 = (bf16[6,64,256]{2,1,0:T(8,128)(2,1)}, bf16[6,64,256]{2,1,0:T(8,128)(2,1)S(1)}, u32[]{:S(2)}, u32[]{:S(2)}) collective-permute-start(bf16[6,64,256]{2,1,0:T(8,128)(2,1)} %get-tuple-element.56), channel_id=1, source_target_pairs={{0,4},{4,0},{8,12},{12,8},{16,20},{20,16},{24,28},{28,24},{1,5},{5... | collective-permute-start | bytes 589832 | tf_op jit(solution)/shard_map/cond/branch_0_fun/ppermute | solution.py:56
  89.9 0.9 copy-start.20

commit v2 on v1

--- a/solution.py
+++ b/solution.py
@@ -10,7 +10,7 @@
 CORE, ACROSS, DOWN = 1, 2, 4
 SQUARE = 8
 CHUNKS = 2
-VMEM_BYTES = 56 * 1024 * 1024
+VMEM_BYTES = 20 * 1024 * 1024
 
 
 def broadcast(value, axis, root):
@@ -218,14 +218,15 @@
     )
     place = jnp.stack([chip, core, lax.axis_index("rcv")]).astype(jnp.int32)
 
+    met = flip(lax.dynamic_slice_in_dim(surface_traces, (1 - core) * side, side, axis=1), CORE)
+    own_a, own_b = [], []
+    for chunk in range(CHUNKS):
+        here = lax.dynamic_slice_in_dim(surface_traces, core * side + chunk * rows, rows, axis=1)
+        there = met[:, chunk * rows : (chunk + 1) * rows]
+        own_a.append(jnp.where(mine_is_a, here, there))
+        own_b.append(jnp.where(mine_is_b, here, there))
+
     def run(third):
-        own_a, own_b = [], []
-        for chunk in range(CHUNKS):
-            here = lax.dynamic_slice_in_dim(surface_traces, core * side + chunk * rows, rows, axis=1)
-            there = lax.dynamic_slice_in_dim(surface_traces, (1 - core) * side + chunk * rows, rows, axis=1)
-            met = flip(there, CORE)
-            own_a.append(jnp.where(mine_is_a, here, met))
-            own_b.append(jnp.where(mine_is_b, here, met))
         across = [flip(a, ACROSS) for a in own_a]
         down = [flip(b, DOWN) for b in own_b]
 
@@ -236,6 +237,8 @@
         blocks = jnp.pad(blocks.astype(jnp.float32), ((0, 0), (0, 0), (0, 0), (0, taps)))
         bands = bands_of(blocks, place)
         other_data = flip(lax.dynamic_slice_in_dim(data, (1 - core) * side, side, axis=1), CORE)
+
+        across[0], down[0], bands = lax.optimization_barrier((across[0], down[0], bands))
 
         kept, returned = [], []
         for chunk in range(CHUNKS):

time: 91.4 us -> 74 us (0.81)
  waiting for transfers between devices: 23.1 us -> 12 us
  Pallas kernels: 31.8 us -> 21.2 us
  starting transfers between devices: 17.2 us -> 22 us
  local copies, waits for them, and re-layouts: 5.47 us -> 3.99 us
    ppermute x14 -> x13, waiting for transfers between devices: 23.1 us -> 12 us  [flip(): return lax.ppermute(value, 'shot', [(i, i ^ bit) for i in range(SQUARE)])]
    pallas_call x2, Pallas kernels: 20.8 us -> 12.9 us  [residual_of(): pl.pallas_call(residual_kernel, out_shape=(piece, piece), grid_spec=pltpu...]
    ppermute x14 -> x13, starting transfers between devices: 12.5 us -> 15.8 us  [flip(): return lax.ppermute(value, 'shot', [(i, i ^ bit) for i in range(SQUARE)])]
    cond x34 -> x14, local copies, waits for them, and re-layouts: 2.72 us -> 0.03 us
    pallas_call x1, Pallas kernels: 11 us -> 8.34 us  [bands_of(): pl.pallas_call(band_kernel, out_shape=jax.ShapeDtypeStruct((panels * heig...]
    ppermute x3, starting transfers between devices: 4.67 us -> 6.17 us  [run(): lax.ppermute(primaries, 'rcv', [(i, (i + j) % ring) for i in range(ring)])]
    select_n x2, other arithmetic: 0.12 us -> 1.15 us  [run(): down_again = flip(jnp.where(both, own_a[chunk], across[chunk]), DOWN)]
    dynamic_slice x1, local copies, waits for them, and re-layouts: 0.78 us -> 1.77 us  [run(): lax.dynamic_slice_in_dim(data, (1 - core) * side, side, axis=1)]
  transfers between devices with their start and end apart: 17 -> 16, of which waited for: 6 -> 5; matrix products, arithmetic and copies ran while one was open for 3% -> 12% of each run, Pallas kernels for 35% -> 29%
where the time goes in v2:
time: 74 us; the launch traced here: 73.3 us
  starting transfers between devices  22 us (30%)
  Pallas kernels  21.2 us (29%)
  waiting for transfers between devices  12 us (16%)
  other arithmetic  8.63 us (12%)
  local copies, waits for them, and re-layouts  3.99 us (5%)
  loops' own time  3.01 us (4%)
  between operations  2.45 us (3%)
    ppermute x13, starting transfers between devices, flip(): return lax.ppermute(value, 'shot', [(i, i ^ bit) for i in range(SQUARE)])  15.8 us
    pallas_call x2, Pallas kernels, residual_of(): pl.pallas_call(residual_kernel, out_shape=(piece, piece), grid_spec=pltpu...  12.9 us
    ppermute x13, waiting for transfers between devices, flip(): return lax.ppermute(value, 'shot', [(i, i ^ bit) for i in range(SQUARE)])  12 us
    pallas_call x1, Pallas kernels, bands_of(): pl.pallas_call(band_kernel, out_shape=jax.ShapeDtypeStruct((panels * heig...  8.34 us
    ppermute x3, starting transfers between devices, run(): lax.ppermute(primaries, 'rcv', [(i, (i + j) % ring) for i in range(ring)])  6.17 us
    another operation x1, loops' own time, square_shards(): lax.cond(neighbours_full, functools.partial(run, True), functools.partial...  3.01 us
    select_n x2, other arithmetic, square_shards(): own_b.append(jnp.where(mine_is_b, here, there))  2.94 us
    dynamic_slice x1, local copies, waits for them, and re-layouts, run(): lax.dynamic_slice_in_dim(data, (1 - core) * side, side, axis=1)  1.77 us
  transfers between devices with their start and end apart: 16, of which 5 were waited for; matrix products, arithmetic and copies ran while one was open for 12% of the time, Pallas kernels for 29%

profile of v2, /device:TPU:1, one launch (start us, length us, event | category | flops | bytes accessed | tf_op | source)
XLA Modules:
  0.0 73.3 jit_solution(2763131870868429039)
XLA Ops:
  0.0 1.3 %constant_dynamic-slice_fusion.2 = bf16[16,128,256]{2,1,0:T(8,128)(2,1)S(1)} fusion(bf16[16,256,256]{2,1,0:T(8,128)(2,1)} %param.7, s32[]{:T(128)S(6)} %select_n.111), kind=kLoop, calls=%fused_computation.59 | loop fusion | bytes 2097156 | tf_op jit(solution)/shard_map/dynamic_slice | solution.py:221
  1.3 0.1 collective-permute-start.34
  1.4 0.7 %fusion.23 = (s32[]{:T(128)}, s32[]{:T(128)}, s32[]{:T(128)}, s32[]{:T(128)}) fusion(s32[4]{0:T(128)S(1)} %copy-done.15), kind=kLoop, calls=%fused_computation.57 | loop fusion | flops 104 | bytes 32 | tf_op jit(solution)/shard_map/reduce_sum | solution.py:215
  4.6 0.1 pad_add_fusion
  4.7 0.7 compare_reduce_fusion
  5.4 67.0 %conditional.1 = (bf16[6,256,256]{2,1,0:T(8,128)(2,1)S(1)}) conditional(s32[]{:T(128)} %convert_element_type.24, (s32[]{:T(128)}, pred[]{:T(512)}, pred[]{:T(512)}, bf16[6,16,64]{2,1,0:T(8,128)(2,1)S(1)}, s32[3]{0:T(128)S(1)}, /*index=5*/pred[]{:T(512)}, bf16[6,256,256]{2,1,0:T(8,128)(2,1)}, s32[4]{0:T(128)S(1)}, (), (), ...), branch_computations={%region_6.7_spmd, %region_7.8_spmd} | conditional | flops 6503211008 | bytes 187941984 | solution.py:255
  5.4 2.8 %collective-permute-start.2 = (bf16[6,16,64]{2,1,0:T(8,128)(2,1)S(1)}, bf16[6,16,64]{2,1,0:T(8,128)(2,1)S(1)}, u32[]{:S(2)}, u32[]{:S(2)}) collective-permute-start(bf16[6,16,64]{2,1,0:T(8,128)(2,1)S(1)} %get-tuple-element.117), channel_id=1, source_target_pairs={{0,1},{1,2},{2,3},{3,0},{4,5},{5,6},{6,7},{7,4},{8,9},{9,10},{10,1... | collective-permute-start | bytes 36872 | tf_op jit(solution)/shard_map/cond/branch_0_fun/ppermute | solution.py:234
  8.2 2.3 %collective-permute-start.3 = (bf16[6,16,64]{2,1,0:T(8,128)(2,1)S(1)}, bf16[6,16,64]{2,1,0:T(8,128)(2,1)S(1)}, u32[]{:S(2)}, u32[]{:S(2)}) collective-permute-start(bf16[6,16,64]{2,1,0:T(8,128)(2,1)S(1)} %get-tuple-element.117), channel_id=1, source_target_pairs={{0,2},{1,3},{2,0},{3,1},{4,6},{5,7},{6,4},{7,5},{8,10},{9,11},{10,... | collective-permute-start | bytes 36872 | tf_op jit(solution)/shard_map/cond/branch_0_fun/ppermute | solution.py:234
  10.5 1.1 %collective-permute-start.4 = (bf16[6,16,64]{2,1,0:T(8,128)(2,1)S(1)}, bf16[6,16,64]{2,1,0:T(8,128)(2,1)S(1)}, u32[]{:S(2)}, u32[]{:S(2)}) collective-permute-start(bf16[6,16,64]{2,1,0:T(8,128)(2,1)S(1)} %get-tuple-element.117), channel_id=1, source_target_pairs={{0,3},{1,0},{2,1},{3,2},{4,7},{5,4},{6,5},{7,6},{8,11},{9,8},{10,9... | collective-permute-start | bytes 36872 | tf_op jit(solution)/shard_map/cond/branch_0_fun/ppermute | solution.py:234
  12.9 1.4 %broadcast_select_fusion.3 = (bf16[16,64,256]{2,1,0:T(8,128)(2,1)S(1)}, bf16[16,64,256]{2,1,0:T(8,128)(2,1)S(1)}) fusion(pred[]{:T(512)S(6)} %eq.72, bf16[16,128,256]{2,1,0:T(8,128)(2,1)S(1)} %get-tuple-element.141, bf16[16,256,256]{2,1,0:T(8,128)(2,1)} %get-tuple-element.135, s32[]{:T(128)S(6)} %select_n.130, pred[]{:T(512)S(6)} %eq.74), kind=kLoop, calls=%fused_computation.4 | loop fusion | flops 524288 | bytes 2097158 | tf_op jit(solution)/shard_map/jit(_where)/select_n | solution.py:227
  14.3 1.3 %collective-permute-start = (bf16[16,64,256]{2,1,0:T(8,128)(2,1)S(1)}, bf16[16,64,256]{2,1,0:T(8,128)(2,1)S(1)}, u32[]{:S(2)}, u32[]{:S(2)}) collective-permute-start(bf16[16,64,256]{2,1,0:T(8,128)(2,1)S(1)} %get-tuple-element.190.refs_0_), channel_id=1, source_target_pairs={{0,8},{4,12},{8,0},{12,4},{16,24},{20,28},{24,16},{28,20},{1,9},{5... | collective-permute-start | bytes 1572872 | tf_op jit(solution)/shard_map/cond/branch_0_fun/ppermute | solution.py:56
  15.6 1.2 %collective-permute-start.1 = (bf16[16,64,256]{2,1,0:T(8,128)(2,1)S(1)}, bf16[16,64,256]{2,1,0:T(8,128)(2,1)S(1)}, u32[]{:S(2)}, u32[]{:S(2)}) collective-permute-start(bf16[16,64,256]{2,1,0:T(8,128)(2,1)S(1)} %get-tuple-element.189.refs_1_), channel_id=1, source_target_pairs={{0,16},{4,20},{8,24},{12,28},{16,0},{20,4},{24,8},{28,12},{1,17},{... | collective-permute-start | bytes 1572872 | tf_op jit(solution)/shard_map/cond/branch_0_fun/ppermute | solution.py:56
  16.8 1.8 %constant_dynamic-slice_fusion = bf16[6,128,256]{2,1,0:T(8,128)(2,1)} fusion(bf16[6,256,256]{2,1,0:T(8,128)(2,1)} %get-tuple-element.119.refs_7_, s32[]{:T(128)S(6)} %select_n.82), kind=kLoop, calls=%fused_computation.21 | loop fusion | bytes 786436 | tf_op jit(solution)/shard_map/cond/branch_0_fun/dynamic_slice | solution.py:239
  18.6 1.4 %collective-permute-start.8 = (bf16[6,128,256]{2,1,0:T(8,128)(2,1)}, bf16[6,128,256]{2,1,0:T(8,128)(2,1)S(1)}, u32[]{:S(2)}, u32[]{:S(2)}) collective-permute-start(bf16[6,128,256]{2,1,0:T(8,128)(2,1)} %constant_dynamic-slice_fusion), channel_id=1, source_target_pairs={{0,4},{4,0},{8,12},{12,8},{16,20},{20,16},{24,28},{28,24},{1,5},{5... | collective-permute-start | bytes 1179656 | tf_op jit(solution)/shard_map/cond/branch_0_fun/ppermute | solution.py:56
  20.0 0.0 collective-permute-done.3
  20.1 0.7 pad_maximum_fusion
  20.7 0.0 collective-permute-start.5
  20.8 1.5 %broadcast_select_fusion.2 = (bf16[16,64,256]{2,1,0:T(8,128)(2,1)S(1)}, bf16[16,64,256]{2,1,0:T(8,128)(2,1)S(1)}) fusion(pred[]{:T(512)S(6)} %eq.72, bf16[16,128,256]{2,1,0:T(8,128)(2,1)} %copy-done.5, bf16[16,256,256]{2,1,0:T(8,128)(2,1)} %get-tuple-element.135, s32[]{:T(128)S(6)} %select_n.132, pred[]{:T(512)S(6)} %eq.74), kind=kLoop, calls=%fused_computation.3 | loop fusion | flops 524288 | bytes 2097158 | tf_op jit(solution)/shard_map/jit(_where)/select_n | solution.py:227
  22.3 0.3 collective-permute-start.9
  23.9 0.0 collective-permute-done.5
  24.0 0.3 collective-permute-start.10
  24.2 1.0 %fusion.9.taps_ref = f32[4,12,16,128]{3,2,1,0:T(8,128)S(1)} fusion(bf16[4,6,16,64]{3,2,1,0:T(8,128)(2,1)} %collective-permute-done.5, bf16[1,6,16,64]{3,2,1,0:T(8,128)(2,1)} %bitcast.20, bf16[1,6,16,64]{3,2,1,0:T(8,128)(2,1)} %bitcast.18, bf16[1,6,16,64]{3,2,1,0:T(8,128)(2,1)} %bitcast.16, bf16[1,6,16,64]{3,2,1,0:T(8,128)(2,1)} %bitcast.12), kind=kLoop, calls=%fused_computation.19 | loop fusion | flops 1572864 | bytes 491520 | tf_op jit(solution)/shard_map/cond/branch_0_fun/jit(_pad)/pad | solution.py:237
  25.2 8.3 %bands.2.refs_6_ = bf16[4096,1536]{1,0:T(8,128)(2,1)S(1)} custom-call(s32[3]{0:T(128)S(1)} %get-tuple-element.50.place_ref, f32[4,12,16,128]{3,2,1,0:T(8,128)S(1)} %fusion.9.taps_ref), custom_call_target="tpu_custom_call" | custom-call | flops 50331648 | bytes 12582912 | tf_op jit(solution)/shard_map/cond/branch_0_fun/bands/pallas_call | solution.py:76
  33.6 0.0 collective-permute-done.1.refs_3_
  33.6 0.1 broadcast_select_fusion.7
  33.6 1.3 %collective-permute-start.6 = (bf16[16,64,256]{2,1,0:T(8,128)(2,1)S(1)}, bf16[16,64,256]{2,1,0:T(8,128)(2,1)S(1)}, u32[]{:S(2)}, u32[]{:S(2)}) collective-permute-start(bf16[16,64,256]{2,1,0:T(8,128)(2,1)S(1)} %broadcast_select_fusion.7), channel_id=1, source_target_pairs={{0,8},{4,12},{8,0},{12,4},{16,24},{20,28},{24,16},{28,20},{1,9},{5... | collective-permute-start | bytes 1572872 | tf_op jit(solution)/shard_map/cond/branch_0_fun/ppermute | solution.py:56
  34.9 0.1 broadcast_select_fusion.6
  35.0 0.0 copy-start.3
  35.0 1.3 %collective-permute-start.7 = (bf16[16,64,256]{2,1,0:T(8,128)(2,1)S(1)}, bf16[16,64,256]{2,1,0:T(8,128)(2,1)S(1)}, u32[]{:S(2)}, u32[]{:S(2)}) collective-permute-start(bf16[16,64,256]{2,1,0:T(8,128)(2,1)S(1)} %broadcast_select_fusion.6), channel_id=1, source_target_pairs={{0,16},{4,20},{8,24},{12,28},{16,0},{20,4},{24,8},{28,12},{1,17},{... | collective-permute-start | bytes 1572872 | tf_op jit(solution)/shard_map/cond/branch_0_fun/ppermute | solution.py:56
  36.3 2.0 %collective-permute-done.9.refs_2_ = bf16[16,64,256]{2,1,0:T(8,128)(2,1)} collective-permute-done((bf16[16,64,256]{2,1,0:T(8,128)(2,1)S(1)}, bf16[16,64,256]{2,1,0:T(8,128)(2,1)}, u32[]{:S(2)}, u32[]{:S(2)}) %collective-permute-start.9) | collective-permute-done | bytes 524320 | tf_op jit(solution)/shard_map/cond/branch_0_fun/ppermute | solution.py:56
  38.3 1.1 %broadcast_select_fusion.4 = bf16[16,64,256]{2,1,0:T(8,128)(2,1)S(1)} fusion(bf16[16,64,256]{2,1,0:T(8,128)(2,1)S(1)} %get-tuple-element.192.refs_0_, bf16[16,64,256]{2,1,0:T(8,128)(2,1)} %collective-permute-done.9.refs_2_, pred[]{:T(512)S(6)} %and.43), kind=kLoop, calls=%fused_computation.5 | loop fusion | flops 262144 | bytes 1572865 | tf_op jit(solution)/shard_map/cond/branch_0_fun/jit(_where)/select_n | solution.py:246
  39.4 1.3 %collective-permute-start.12 = (bf16[16,64,256]{2,1,0:T(8,128)(2,1)S(1)}, bf16[16,64,256]{2,1,0:T(8,128)(2,1)S(1)}, u32[]{:S(2)}, u32[]{:S(2)}) collective-permute-start(bf16[16,64,256]{2,1,0:T(8,128)(2,1)S(1)} %broadcast_select_fusion.4), channel_id=1, source_target_pairs={{0,16},{4,20},{8,24},{12,28},{16,0},{20,4},{24,8},{28,12},{1,17},{... | collective-permute-start | bytes 1572872 | tf_op jit(solution)/shard_map/cond/branch_0_fun/ppermute | solution.py:56
  40.7 0.0 collective-permute-done.10.refs_3_
  40.7 0.1 broadcast_select_fusion.5
  40.8 1.3 %collective-permute-start.11 = (bf16[16,64,256]{2,1,0:T(8,128)(2,1)S(1)}, bf16[16,64,256]{2,1,0:T(8,128)(2,1)S(1)}, u32[]{:S(2)}, u32[]{:S(2)}) collective-permute-start(bf16[16,64,256]{2,1,0:T(8,128)(2,1)S(1)} %broadcast_select_fusion.5), channel_id=1, source_target_pairs={{0,8},{4,12},{8,0},{12,4},{16,24},{20,28},{24,16},{28,20},{1,9},{5... | collective-permute-start | bytes 1572872 | tf_op jit(solution)/shard_map/cond/branch_0_fun/ppermute | solution.py:56
  42.0 0.0 collective-permute-done.8.refs_8_
  42.0 7.4 %collective-permute-done.6.refs_4_ = bf16[16,64,256]{2,1,0:T(8,128)(2,1)S(1)} collective-permute-done((bf16[16,64,256]{2,1,0:T(8,128)(2,1)S(1)}, bf16[16,64,256]{2,1,0:T(8,128)(2,1)S(1)}, u32[]{:S(2)}, u32[]{:S(2)}) %collective-permute-start.6) | collective-permute-done | bytes 524320 | tf_op jit(solution)/shard_map/cond/branch_0_fun/ppermute | solution.py:56
  49.4 0.9 %collective-permute-done.7.refs_5_ = bf16[16,64,256]{2,1,0:T(8,128)(2,1)S(1)} collective-permute-done((bf16[16,64,256]{2,1,0:T(8,128)(2,1)S(1)}, bf16[16,64,256]{2,1,0:T(8,128)(2,1)S(1)}, u32[]{:S(2)}, u32[]{:S(2)}) %collective-permute-start.7) | collective-permute-done | bytes 524320 | tf_op jit(solution)/shard_map/cond/branch_0_fun/ppermute | solution.py:56
  50.3 6.8 %residual.4 = (bf16[6,64,256]{2,1,0:T(8,128)(2,1)S(1)}, bf16[6,64,256]{2,1,0:T(8,128)(2,1)}) custom-call(s32[4]{0:T(128)S(1)} %get-tuple-element.49.owner_ref, s32[3]{0:T(128)S(1)} %get-tuple-element.50.place_ref, bf16[16,64,256]{2,1,0:T(8,128)(2,1)S(1)} %get-tuple-element.190.refs_0_, bf16[16,64,256]{2,1,0:T(8,128)(2,1)S(1)} %get-tuple-element.189.refs_1_, ...), custom_call_target="tpu_custom_call" | custom-call | flops 3221225472 | bytes 12582912 | tf_op jit(solution)/shard_map/cond/branch_0_fun/residual/pallas_call | solution.py:175
  57.2 3.8 %collective-permute-start.13 = (bf16[6,64,256]{2,1,0:T(8,128)(2,1)}, bf16[6,64,256]{2,1,0:T(8,128)(2,1)S(1)}, u32[]{:S(2)}, u32[]{:S(2)}) collective-permute-start(bf16[6,64,256]{2,1,0:T(8,128)(2,1)} %get-tuple-element.63), channel_id=1, source_target_pairs={{0,4},{4,0},{8,12},{12,8},{16,20},{20,16},{24,28},{28,24},{1,5},{5... | collective-permute-start | bytes 589832 | tf_op jit(solution)/shard_map/cond/branch_0_fun/ppermute | solution.py:56
  61.0 0.6 collective-permute-done.12.refs_5_
  61.6 0.0 collective-permute-done.11.refs_4_
  61.6 6.1 %residual.5 = (bf16[6,64,256]{2,1,0:T(8,128)(2,1)S(1)}, bf16[6,64,256]{2,1,0:T(8,128)(2,1)S(1)}) custom-call(s32[4]{0:T(128)S(1)} %get-tuple-element.49.owner_ref, s32[3]{0:T(128)S(1)} %get-tuple-element.50.place_ref, bf16[16,64,256]{2,1,0:T(8,128)(2,1)S(1)} %get-tuple-element.192.refs_0_, bf16[16,64,256]{2,1,0:T(8,128)(2,1)S(1)} %get-tuple-element.191.refs_1_, ...), custom_call_target="tpu_custom_call" | custom-call | flops 3221225472 | bytes 12582912 | tf_op jit(solution)/shard_map/cond/branch_0_fun/residual/pallas_call | solution.py:175
  67.7 2.1 %collective-permute-start.14 = (bf16[6,64,256]{2,1,0:T(8,128)(2,1)S(1)}, bf16[6,64,256]{2,1,0:T(8,128)(2,1)S(1)}, u32[]{:S(2)}, u32[]{:S(2)}) collective-permute-start(bf16[6,64,256]{2,1,0:T(8,128)(2,1)S(1)} %get-tuple-element.64), channel_id=1, source_target_pairs={{0,4},{4,0},{8,12},{12,8},{16,20},{20,16},{24,28},{28,24},{1,5},{5... | collective-permute-start | bytes 589832 | tf_op jit(solution)/shard_map/cond/branch_0_fun/ppermute | solution.py:56
  69.8 1.1 %collective-permute-done.14 = bf16[6,64,256]{2,1,0:T(8,128)(2,1)S(1)} collective-permute-done((bf16[6,64,256]{2,1,0:T(8,128)(2,1)S(1)}, bf16[6,64,256]{2,1,0:T(8,128)(2,1)S(1)}, u32[]{:S(2)}, u32[]{:S(2)}) %collective-permute-start.14) | collective-permute-done | bytes 196640 | tf_op jit(solution)/shard_map/cond/branch_0_fun/ppermute | solution.py:56
  70.9 1.3 %maximum_select_fusion = bf16[6,256,256]{2,1,0:T(8,128)(2,1)S(1)} fusion(bf16[6,64,256]{2,1,0:T(8,128)(2,1)S(1)} %collective-permute-done.14, bf16[6,64,256]{2,1,0:T(8,128)(2,1)S(1)} %collective-permute-done.13, bf16[6,64,256]{2,1,0:T(8,128)(2,1)S(1)} %get-tuple-element.62, bf16[6,64,256]{2,1,0:T(8,128)(2,1)} %copy-done.2, pred[]{:T(512)S(6)} %eq.38), kind=kLoop, calls=%fused_computation | loop fusion | flops 6684672 | bytes 1572865 | tf_op jit(solution)/shard_map/cond/branch_0_fun/jit(_where)/select_n | solution.py:253
  72.4 0.0 copy-start.7
  72.4 0.9 %copy-done.7 = bf16[6,256,256]{2,1,0:T(8,128)(2,1)} copy-done((bf16[6,256,256]{2,1,0:T(8,128)(2,1)}, bf16[6,256,256]{2,1,0:T(8,128)(2,1)S(1)}, u32[]{:S(2)}) %copy-start.7) | copy-done | bytes 786456
  (22 shorter events, 0.0 us)
Async XLA Ops:
  0.0 1.4 %copy-start.15 = (s32[4]{0:T(128)S(1)}, s32[4]{0:T(128)}, u32[]{:S(2)}) copy-start(s32[4]{0:T(128)} %param.9) | copy-start | bytes 52
  0.0 5.4 %copy-start.8 = (bf16[6,16,64]{2,1,0:T(8,128)(2,1)S(1)}, bf16[6,16,64]{2,1,0:T(8,128)(2,1)}, u32[]{:S(2)}) copy-start(bf16[6,16,64]{2,1,0:T(8,128)(2,1)} %param.8) | copy-start | bytes 36868
  1.3 4.1 %collective-permute-start.34 = (bf16[16,128,256]{2,1,0:T(8,128)(2,1)S(1)}, bf16[16,128,256]{2,1,0:T(8,128)(2,1)S(1)}, u32[]{:S(2)}, u32[]{:S(2)}) collective-permute-start(bf16[16,128,256]{2,1,0:T(8,128)(2,1)S(1)} %constant_dynamic-slice_fusion.2), channel_id=1, source_target_pairs={{0,4},{4,0},{8,12},{12,8},{16,20},{20,16},{24,28},{28,24},{1,5},{5... | collective-permute-start | bytes 3145736 | tf_op jit(solution)/shard_map/ppermute | solution.py:56
  5.4 8.9 %copy-start.5 = (bf16[16,128,256]{2,1,0:T(8,128)(2,1)}, bf16[16,128,256]{2,1,0:T(8,128)(2,1)S(1)}, u32[]{:S(2)}) copy-start(bf16[16,128,256]{2,1,0:T(8,128)(2,1)S(1)} %get-tuple-element.141) | copy-start | bytes 3145732 | tf_op jit(solution)/shard_map/cond
  5.4 15.3 %copy-start.9 = (bf16[6,16,64]{2,1,0:T(8,128)(2,1)}, bf16[6,16,64]{2,1,0:T(8,128)(2,1)S(1)}, u32[]{:S(2)}) copy-start(bf16[6,16,64]{2,1,0:T(8,128)(2,1)S(1)} %get-tuple-element.117) | copy-start | bytes 36868 | tf_op jit(solution)/shard_map/cond
  5.4 13.2 %collective-permute-start.2 = (bf16[6,16,64]{2,1,0:T(8,128)(2,1)S(1)}, bf16[6,16,64]{2,1,0:T(8,128)(2,1)S(1)}, u32[]{:S(2)}, u32[]{:S(2)}) collective-permute-start(bf16[6,16,64]{2,1,0:T(8,128)(2,1)S(1)} %get-tuple-element.117), channel_id=1, source_target_pairs={{0,1},{1,2},{2,3},{3,0},{4,5},{5,6},{6,7},{7,4},{8,9},{9,10},{10,1... | collective-permute-start | bytes 36872 | tf_op jit(solution)/shard_map/cond/branch_0_fun/ppermute | solution.py:234
  8.2 11.8 %collective-permute-start.3 = (bf16[6,16,64]{2,1,0:T(8,128)(2,1)S(1)}, bf16[6,16,64]{2,1,0:T(8,128)(2,1)S(1)}, u32[]{:S(2)}, u32[]{:S(2)}) collective-permute-start(bf16[6,16,64]{2,1,0:T(8,128)(2,1)S(1)} %get-tuple-element.117), channel_id=1, source_target_pairs={{0,2},{1,3},{2,0},{3,1},{4,6},{5,7},{6,4},{7,5},{8,10},{9,11},{10,... | collective-permute-start | bytes 36872 | tf_op jit(solution)/shard_map/cond/branch_0_fun/ppermute | solution.py:234
  10.5 9.5 %collective-permute-start.4 = (bf16[6,16,64]{2,1,0:T(8,128)(2,1)S(1)}, bf16[6,16,64]{2,1,0:T(8,128)(2,1)S(1)}, u32[]{:S(2)}, u32[]{:S(2)}) collective-permute-start(bf16[6,16,64]{2,1,0:T(8,128)(2,1)S(1)} %get-tuple-element.117), channel_id=1, source_target_pairs={{0,3},{1,0},{2,1},{3,2},{4,7},{5,4},{6,5},{7,6},{8,11},{9,8},{10,9... | collective-permute-start | bytes 36872 | tf_op jit(solution)/shard_map/cond/branch_0_fun/ppermute | solution.py:234
  14.3 19.2 %collective-permute-start = (bf16[16,64,256]{2,1,0:T(8,128)(2,1)S(1)}, bf16[16,64,256]{2,1,0:T(8,128)(2,1)S(1)}, u32[]{:S(2)}, u32[]{:S(2)}) collective-permute-start(bf16[16,64,256]{2,1,0:T(8,128)(2,1)S(1)} %get-tuple-element.190.refs_0_), channel_id=1, source_target_pairs={{0,8},{4,12},{8,0},{12,4},{16,24},{20,28},{24,16},{28,20},{1,9},{5... | collective-permute-start | bytes 1572872 | tf_op jit(solution)/shard_map/cond/branch_0_fun/ppermute | solution.py:56
  15.6 18.0 %collective-permute-start.1 = (bf16[16,64,256]{2,1,0:T(8,128)(2,1)S(1)}, bf16[16,64,256]{2,1,0:T(8,128)(2,1)S(1)}, u32[]{:S(2)}, u32[]{:S(2)}) collective-permute-start(bf16[16,64,256]{2,1,0:T(8,128)(2,1)S(1)} %get-tuple-element.189.refs_1_), channel_id=1, source_target_pairs={{0,16},{4,20},{8,24},{12,28},{16,0},{20,4},{24,8},{28,12},{1,17},{... | collective-permute-start | bytes 1572872 | tf_op jit(solution)/shard_map/cond/branch_0_fun/ppermute | solution.py:56
  18.6 2.2 %copy-start.12 = (bf16[6,16,64]{2,1,0:T(8,128)(2,1)}, bf16[6,16,64]{2,1,0:T(8,128)(2,1)S(1)}, u32[]{:S(2)}) copy-start(bf16[6,16,64]{2,1,0:T(8,128)(2,1)S(1)} %collective-permute-done.2) | copy-start | bytes 36868 | tf_op jit(solution)/shard_map/cond
  18.6 23.4 %collective-permute-start.8 = (bf16[6,128,256]{2,1,0:T(8,128)(2,1)}, bf16[6,128,256]{2,1,0:T(8,128)(2,1)S(1)}, u32[]{:S(2)}, u32[]{:S(2)}) collective-permute-start(bf16[6,128,256]{2,1,0:T(8,128)(2,1)} %constant_dynamic-slice_fusion), channel_id=1, source_target_pairs={{0,4},{4,0},{8,12},{12,8},{16,20},{20,16},{24,28},{28,24},{1,5},{5... | collective-permute-start | bytes 1179656 | tf_op jit(solution)/shard_map/cond/branch_0_fun/ppermute | solution.py:56
  20.0 0.7 copy-start.13
  20.1 0.7 copy-start.14
  20.7 3.2 %collective-permute-start.5 = (bf16[4,6,16,64]{3,2,1,0:T(8,128)(2,1)}, bf16[4,6,16,64]{3,2,1,0:T(8,128)(2,1)}, u32[]{:S(2)}, u32[]{:S(2)}) collective-permute-start(bf16[4,6,16,64]{3,2,1,0:T(8,128)(2,1)} %pad_maximum_fusion), channel_id=1, source_target_pairs={{0,4},{4,0},{8,12},{12,8},{16,20},{20,16},{24,28},{28,24},{1,5},{5... | collective-permute-start | bytes 147464 | tf_op jit(solution)/shard_map/cond/branch_0_fun/ppermute | solution.py:56
  22.3 16.0 %collective-permute-start.9 = (bf16[16,64,256]{2,1,0:T(8,128)(2,1)S(1)}, bf16[16,64,256]{2,1,0:T(8,128)(2,1)}, u32[]{:S(2)}, u32[]{:S(2)}) collective-permute-start(bf16[16,64,256]{2,1,0:T(8,128)(2,1)S(1)} %get-tuple-element.192.refs_0_), channel_id=1, source_target_pairs={{0,8},{4,12},{8,0},{12,4},{16,24},{20,28},{24,16},{28,20},{1,9},{5... | collective-permute-start | bytes 1572872 | tf_op jit(solution)/shard_map/cond/branch_0_fun/ppermute | solution.py:56
  24.0 16.7 %collective-permute-start.10 = (bf16[16,64,256]{2,1,0:T(8,128)(2,1)S(1)}, bf16[16,64,256]{2,1,0:T(8,128)(2,1)S(1)}, u32[]{:S(2)}, u32[]{:S(2)}) collective-permute-start(bf16[16,64,256]{2,1,0:T(8,128)(2,1)S(1)} %get-tuple-element.191.refs_1_), channel_id=1, source_target_pairs={{0,16},{4,20},{8,24},{12,28},{16,0},{20,4},{24,8},{28,12},{1,17},{... | collective-permute-start | bytes 1572872 | tf_op jit(solution)/shard_map/cond/branch_0_fun/ppermute | solution.py:56
  33.6 15.8 %collective-permute-start.6 = (bf16[16,64,256]{2,1,0:T(8,128)(2,1)S(1)}, bf16[16,64,256]{2,1,0:T(8,128)(2,1)S(1)}, u32[]{:S(2)}, u32[]{:S(2)}) collective-permute-start(bf16[16,64,256]{2,1,0:T(8,128)(2,1)S(1)} %broadcast_select_fusion.7), channel_id=1, source_target_pairs={{0,8},{4,12},{8,0},{12,4},{16,24},{20,28},{24,16},{28,20},{1,9},{5... | collective-permute-start | bytes 1572872 | tf_op jit(solution)/shard_map/cond/branch_0_fun/ppermute | solution.py:56
  35.0 15.4 %copy-start.3 = (bf16[6,256,256]{2,1,0:T(8,128)(2,1)S(1)}, bf16[6,256,256]{2,1,0:T(8,128)(2,1)}, u32[]{:S(2)}) copy-start(bf16[6,256,256]{2,1,0:T(8,128)(2,1)} %get-tuple-element.119.refs_7_) | copy-start | bytes 2359300 | tf_op jit(solution)/shard_map/cond
  35.0 15.3 %collective-permute-start.7 = (bf16[16,64,256]{2,1,0:T(8,128)(2,1)S(1)}, bf16[16,64,256]{2,1,0:T(8,128)(2,1)S(1)}, u32[]{:S(2)}, u32[]{:S(2)}) collective-permute-start(bf16[16,64,256]{2,1,0:T(8,128)(2,1)S(1)} %broadcast_select_fusion.6), channel_id=1, source_target_pairs={{0,16},{4,20},{8,24},{12,28},{16,0},{20,4},{24,8},{28,12},{1,17},{... | collective-permute-start | bytes 1572872 | tf_op jit(solution)/shard_map/cond/branch_0_fun/ppermute | solution.py:56
  39.4 22.2 %collective-permute-start.12 = (bf16[16,64,256]{2,1,0:T(8,128)(2,1)S(1)}, bf16[16,64,256]{2,1,0:T(8,128)(2,1)S(1)}, u32[]{:S(2)}, u32[]{:S(2)}) collective-permute-start(bf16[16,64,256]{2,1,0:T(8,128)(2,1)S(1)} %broadcast_select_fusion.4), channel_id=1, source_target_pairs={{0,16},{4,20},{8,24},{12,28},{16,0},{20,4},{24,8},{28,12},{1,17},{... | collective-permute-start | bytes 1572872 | tf_op jit(solution)/shard_map/cond/branch_0_fun/ppermute | solution.py:56
  40.8 20.8 %collective-permute-start.11 = (bf16[16,64,256]{2,1,0:T(8,128)(2,1)S(1)}, bf16[16,64,256]{2,1,0:T(8,128)(2,1)S(1)}, u32[]{:S(2)}, u32[]{:S(2)}) collective-permute-start(bf16[16,64,256]{2,1,0:T(8,128)(2,1)S(1)} %broadcast_select_fusion.5), channel_id=1, source_target_pairs={{0,8},{4,12},{8,0},{12,4},{16,24},{20,28},{24,16},{28,20},{1,9},{5... | collective-permute-start | bytes 1572872 | tf_op jit(solution)/shard_map/cond/branch_0_fun/ppermute | solution.py:56
  57.1 10.5 %copy-start.2 = (bf16[6,64,256]{2,1,0:T(8,128)(2,1)}, bf16[6,64,256]{2,1,0:T(8,128)(2,1)S(1)}, u32[]{:S(2)}) copy-start(bf16[6,64,256]{2,1,0:T(8,128)(2,1)S(1)} %get-tuple-element.59) | copy-start | bytes 589828 | tf_op jit(solution)/shard_map/cond
  57.2 12.7 %collective-permute-start.13 = (bf16[6,64,256]{2,1,0:T(8,128)(2,1)}, bf16[6,64,256]{2,1,0:T(8,128)(2,1)S(1)}, u32[]{:S(2)}, u32[]{:S(2)}) collective-permute-start(bf16[6,64,256]{2,1,0:T(8,128)(2,1)} %get-tuple-element.63), channel_id=1, source_target_pairs={{0,4},{4,0},{8,12},{12,8},{16,20},{20,16},{24,28},{28,24},{1,5},{5... | collective-permute-start | bytes 589832 | tf_op jit(solution)/shard_map/cond/branch_0_fun/ppermute | solution.py:56
  67.7 3.2 %collective-permute-start.14 = (bf16[6,64,256]{2,1,0:T(8,128)(2,1)S(1)}, bf16[6,64,256]{2,1,0:T(8,128)(2,1)S(1)}, u32[]{:S(2)}, u32[]{:S(2)}) collective-permute-start(bf16[6,64,256]{2,1,0:T(8,128)(2,1)S(1)} %get-tuple-element.64), channel_id=1, source_target_pairs={{0,4},{4,0},{8,12},{12,8},{16,20},{20,16},{24,28},{28,24},{1,5},{5... | collective-permute-start | bytes 589832 | tf_op jit(solution)/shard_map/cond/branch_0_fun/ppermute | solution.py:56
  72.4 0.9 %copy-start.7 = (bf16[6,256,256]{2,1,0:T(8,128)(2,1)}, bf16[6,256,256]{2,1,0:T(8,128)(2,1)S(1)}, u32[]{:S(2)}) copy-start(bf16[6,256,256]{2,1,0:T(8,128)(2,1)S(1)} %get-tuple-element.225) | copy-start | bytes 2359300

commit v3 on v2

v3 whole, which is shorter than its diff:
```python
import functools

import jax
import jax.numpy as jnp
from jax import lax
from jax.experimental import pallas as pl
from jax.experimental.pallas import tpu as pltpu
from jax.sharding import PartitionSpec as P

CORE, ACROSS, DOWN = 1, 2, 4
SQUARE = 8
CHUNKS = 2
FIRST_SOURCES = 4
VMEM_BYTES = 20 * 1024 * 1024
SMALL_VMEM_BYTES = 2 * 1024 * 1024


def broadcast(value, axis, root):
    mine = lax.axis_index(axis) == root
    return lax.psum(jnp.where(mine, value, jnp.zeros_like(value)), axis)


def shift_table(taps, block):
    shape = (2, taps, block, block)
    lag_index, tap_index, in_index, out_index = (lax.broadcasted_iota(jnp.int32, shape, dim) for dim in range(4))
    distance = out_index - in_index + lag_index * block
    return (distance == tap_index).astype(jnp.bfloat16)


def band_matrices(panel_prim, shift_ones):
    bands = jnp.einsum("skt,ltio->lskio", panel_prim, shift_ones, preferred_element_type=jnp.float32)
    return bands.astype(jnp.bfloat16)


def convolve(traces, bands, block):
    point_count, row_count, length = traces.shape
    blocks = traces.reshape(point_count, row_count, length // block, block)
    earlier = jnp.concatenate([jnp.zeros_like(blocks[:, :, :1]), blocks[:, :, :-1]], axis=2)
    stacked = jnp.stack([blocks, earlier])
    product = jnp.einsum("lkrbi,lskio->srbo", stacked, bands, preferred_element_type=jnp.float32)
    return product.reshape(bands.shape[1], row_count, length)


def summed_broadcasts(data, surface_traces, primaries, panel_owner):
    points, taps = surface_traces.shape[0], primaries.shape[2]
    shift_ones = shift_table(taps, 2 * taps)
    summed = jnp.zeros(data.shape, jnp.float32)
    panels_here = primaries.shape[1] // points
    for panel_id in range(panel_owner.shape[0]):
        first_point = panel_id % panels_here * points
        panel_prim = broadcast(primaries, "rcv", panel_id // panels_here)[:, first_point : first_point + points]
        traces = broadcast(surface_traces, "shot", panel_owner[panel_id])
        summed = summed + convolve(traces, band_matrices(panel_prim, shift_ones), 2 * taps)
    return (data.astype(jnp.float32) - summed).astype(jnp.bfloat16)


def flip(value, bit):
    return lax.ppermute(value, "shot", [(i, i ^ bit) for i in range(SQUARE)])


def band_kernel(place_ref, taps_ref, band_ref):
    shots, points, width = taps_ref.shape[1:]
    rows = width // 2

    def point(k, carry):
        for s in range(shots):
            row = taps_ref[0, s, pl.ds(k, 1), :]
            spread = pltpu.roll(jnp.broadcast_to(row, (rows, width)), 0, 1, stride=1, stride_axis=0)
            band_ref[pl.ds(pl.multiple_of(k * rows, rows), rows), s * width : (s + 1) * width] = spread.astype(jnp.bfloat16)
        return carry

    lax.fori_loop(0, points, point, 0)


def bands_of(blocks, place):
    panels, shots, points, width = blocks.shape
    height = points * width // 2
    return pl.pallas_call(
        band_kernel,
        out_shape=jax.ShapeDtypeStruct((panels * height, shots * width), jnp.bfloat16),
        grid_spec=pltpu.PrefetchScalarGridSpec(
            num_scalar_prefetch=1,
            grid=(panels,),
            in_specs=[pl.BlockSpec((1, shots, points, width), lambda p, place: (place[2] ^ p, 0, 0, 0))],
            out_specs=pl.BlockSpec((height, shots * width), lambda p, place: (p, 0)),
        ),
        compiler_params=pltpu.CompilerParams(vmem_limit_bytes=VMEM_BYTES),
        cost_estimate=pl.CostEstimate(flops=panels * height * shots * width * 8, bytes_accessed=panels * height * shots * width * 2, transcendentals=0),
        name="bands",
    )(place, blocks)


def source_of(panel, owner_ref, chip):
    panels = owner_ref.shape[0]

    def held(place):
        count = jnp.int32(0)
        for other in range(panels):
            count = count + (owner_ref[other] // 2 == place).astype(jnp.int32)
        return count

    owner = owner_ref[panel]
    there, second = owner // 2, lax.rem(owner, 2) == 1
    both = held(there) == 2
    across_full, down_full = held(chip ^ 1) == 2, held(chip ^ 2) == 2
    own = jnp.where(both & second, 1, 0)
    across = jnp.where(both & second, 4, 2)
    down = jnp.where(both & jnp.logical_not(second), 5, 3)
    single = jnp.where(down_full, 4, 5)
    double = jnp.where(second, jnp.where(across_full, 7, 4), jnp.where(down_full, 6, 5))
    diagonal = jnp.where(both, double, single)
    return jnp.where(there == chip, own, jnp.where(there == (chip ^ 1), across, jnp.where(there == (chip ^ 2), down, diagonal)))


def plan_kernel(owner_ref, place_ref, plan_ref):
    panels = owner_ref.shape[0]
    early, late = jnp.int32(0), jnp.int32(0)
    for entry in range(3 * panels):
        plan_ref[entry] = jnp.int32(0)
    for panel in range(panels):
        source = source_of(panel, owner_ref, place_ref[0])
        plan_ref[panel] = source
        plan_ref[panels + early] = jnp.int32(panel)
        plan_ref[2 * panels + late] = jnp.int32(panel)
        met_first = source < FIRST_SOURCES
        early = early + jnp.where(met_first, 1, 0)
        late = late + jnp.where(met_first, 0, 1)
    plan_ref[3 * panels] = early
    plan_ref[3 * panels + 1] = late


def plan_of(owner, place):
    return pl.pallas_call(
        plan_kernel,
        out_shape=jax.ShapeDtypeStruct((3 * owner.shape[0] + 2,), jnp.int32),
        in_specs=[pl.BlockSpec(memory_space=pltpu.SMEM)] * 2,
        out_specs=pl.BlockSpec(memory_space=pltpu.SMEM),
        name="plan",
    )(owner, place)


def pick_kernel(chunk, owner_ref, place_ref, slot_ref, met_ref, a_ref, b_ref, sems):
    chip, core = place_ref[0], place_ref[1]
    first_owns, second_owns = jnp.bool_(False), jnp.bool_(False)
    for panel in range(owner_ref.shape[0]):
        first_owns = first_owns | (owner_ref[panel] == 2 * chip)
        second_owns = second_owns | (owner_ref[panel] == 2 * chip + 1)
    rows = met_ref.shape[1]
    start = pl.multiple_of((core * CHUNKS + chunk) * rows, rows)
    here_ref = slot_ref.at[:, pl.ds(start, rows), :]
    for index, (out_ref, mine) in enumerate(((a_ref, first_owns == (core == 0)), (b_ref, second_owns == (core == 1)))):
        @pl.when(mine)
        def _():
            pltpu.make_async_copy(here_ref, out_ref, sems.at[index]).start()

        @pl.when(jnp.logical_not(mine))
        def _():
            pltpu.make_async_copy(met_ref, out_ref, sems.at[index]).start()

    for index, out_ref in enumerate((a_ref, b_ref)):
        pltpu.make_async_copy(met_ref, out_ref, sems.at[index]).wait()


def pick(chunk, owner, place, slot, met):
    piece = jax.ShapeDtypeStruct(met.shape, met.dtype)
    return pl.pallas_call(
        functools.partial(pick_kernel, chunk),
        out_shape=(piece, piece),
        in_specs=[pl.BlockSpec(memory_space=pltpu.SMEM)] * 2 + [pl.BlockSpec(memory_space=pl.ANY)] * 2,
        out_specs=[pl.BlockSpec(memory_space=pl.ANY)] * 2,
        scratch_shapes=[pltpu.SemaphoreType.DMA((2,))],
        compiler_params=pltpu.CompilerParams(vmem_limit_bytes=SMALL_VMEM_BYTES),
        name="pick",
    )(owner, place, slot, met)


def sum_kernel(last, plan_ref, place_ref, *refs):
    extra = 5 if last else 1
    count = len(refs) - extra - 5
    sources, band_ref = refs[:count], refs[count]
    window, spread, total, arrived = refs[-4:]
    step, steps = pl.program_id(0), pl.num_programs(0)
    slots, points, rows, length = window.shape
    panels = (plan_ref.shape[0] - 2) // 3
    entries = panels * (2 if last else 1)
    wanted = plan_ref[3 * panels + (1 if last else 0)]
    half = spread.shape[1] // points
    width = 2 * half

    @pl.when(step == 0)
    def _():
        for slot in range(slots):
            chosen = jnp.clip(plan_ref[plan_ref[entries + slot]] - (FIRST_SOURCES if last else 0), 0, count - 1)
            for index, source in enumerate(sources):
                @pl.when((slot < wanted) & (chosen == index))
                def _():
                    pltpu.make_async_copy(source, window.at[slot], arrived.at[slot]).start()

    low = lax.broadcasted_iota(jnp.int32, (rows, width), 1) < half

    @pl.when(step < wanted)
    def _():
        pltpu.make_async_copy(sources[0], window.at[step], arrived.at[step]).wait()
        for j in range(points // 2):
            for c in range(length // width):
                first = window[step, 2 * j, :, c * width : (c + 1) * width].astype(jnp.float32)
                second = window[step, 2 * j + 1, :, c * width : (c + 1) * width].astype(jnp.float32)
                even = jnp.where(low, first, pltpu.roll(second, half, 1))
                odd = jnp.where(low, pltpu.roll(first, half, 1), second)
                spread[2 * c * rows : (2 * c + 1) * rows, j * width : (j + 1) * width] = even.astype(jnp.bfloat16)
                spread[(2 * c + 1) * rows : (2 * c + 2) * rows, j * width : (j + 1) * width] = odd.astype(jnp.bfloat16)
        product = jnp.dot(spread[...], band_ref[...], preferred_element_type=jnp.float32)

        @pl.when(step == 0)
        def _():
            total[...] = product

        @pl.when(step > 0)
        def _():
            total[...] += product

    @pl.when((step == 0) & (wanted == 0))
    def _():
        total[...] = jnp.zeros_like(total)

    @pl.when(step == steps - 1)
    def _():
        for s in range(total.shape[1] // width):

            def part(b):
                return total[b * rows : (b + 1) * rows, s * width : (s + 1) * width]

            for c in range(length // width):
                before = part(2 * c - 1) if c > 0 else jnp.zeros((rows, width), jnp.float32)
                summed = part(2 * c) + pltpu.roll(jnp.where(low, part(2 * c + 1), before), half, 1)
                span = slice(c * width, (c + 1) * width)
                if last:
                    early_ref, mine_ref, other_ref, out_mine_ref, out_other_ref = refs[count + 1 : -4]
                    shots = mine_ref.shape[0]
                    data_ref, out_ref = (mine_ref, out_mine_ref) if s < shots else (other_ref, out_other_ref)
                    summed = summed + early_ref[s, :, span]
                    here = data_ref[s % shots, :, span].astype(jnp.float32)
                    out_ref[s % shots, :, span] = (here - summed).astype(jnp.bfloat16)
                else:
                    refs[count + 1][s, :, span] = summed


def sum_of(plan, place, sources, bands, steps, taps, late=None):
    points, rows, length = sources[0].shape
    panels = (plan.shape[0] - 2) // 3
    height, columns = bands.shape[0] // panels, bands.shape[1]
    shots = columns // (2 * taps)
    last = late is not None
    entries = panels * (2 if last else 1)

    def band_place(step, plan, place):
        wanted = plan[3 * panels + (1 if last else 0)]
        return (plan[entries + jnp.maximum(jnp.minimum(step, wanted - 1), 0)], 0)

    in_specs = [pl.BlockSpec(memory_space=pl.ANY)] * len(sources) + [pl.BlockSpec((height, columns), band_place)]
    operands = [*sources, bands]
    if last:
        chunk, early, data, other_data = late
        half = shots // 2
        piece = jax.ShapeDtypeStruct((half, rows, length), jnp.bfloat16)
        in_specs += [
            pl.BlockSpec((shots, rows, length), lambda step, plan, place: (0, 0, 0)),
            pl.BlockSpec((half, rows, length), lambda step, plan, place: (0, place[1] * CHUNKS + chunk, 0)),
            pl.BlockSpec((half, rows, length), lambda step, plan, place: (0, chunk, 0)),
        ]
        operands += [early, data, other_data]
        out_shape = (piece, piece)
        out_specs = [pl.BlockSpec((half, rows, length), lambda step, plan, place: (0, 0, 0))] * 2
    else:
        out_shape = jax.ShapeDtypeStruct((shots, rows, length), jnp.float32)
        out_specs = pl.BlockSpec((shots, rows, length), lambda step, plan, place: (0, 0, 0))
    tall = rows * length // taps
    return pl.pallas_call(
        functools.partial(sum_kernel, last),
        out_shape=out_shape,
        grid_spec=pltpu.PrefetchScalarGridSpec(
            num_scalar_prefetch=2,
            grid=(steps,),
            in_specs=in_specs,
            out_specs=out_specs,
            scratch_shapes=[
                pltpu.VMEM((steps, points, rows, length), jnp.bfloat16),
                pltpu.VMEM((tall, height), jnp.bfloat16),
                pltpu.VMEM((tall, columns), jnp.float32),
                pltpu.SemaphoreType.DMA((steps,)),
            ],
        ),
        compiler_params=pltpu.CompilerParams(vmem_limit_bytes=VMEM_BYTES),
        cost_estimate=pl.CostEstimate(flops=2 * tall * steps * height * columns, bytes_accessed=2 * steps * height * columns, transcendentals=0),
        name="residual" if last else "early_sum",
    )(plan, place, *operands)


def assemble_kernel(place_ref, *refs):
    pieces, out_ref, sems = refs[:-2], refs[-2], refs[-1]
    rows = pieces[0].shape[1]
    copies = []
    for index, piece in enumerate(pieces):
        side = place_ref[1] if index < CHUNKS else 1 - place_ref[1]
        start = pl.multiple_of((side * CHUNKS + index % CHUNKS) * rows, rows)
        copies.append(pltpu.make_async_copy(piece, out_ref.at[:, pl.ds(start, rows), :], sems.at[index]))
    for copy in copies:
        copy.start()
    for copy in copies:
        copy.wait()


def assemble(place, pieces, like):
    return pl.pallas_call(
        assemble_kernel,
        out_shape=jax.ShapeDtypeStruct(like.shape, like.dtype),
        in_specs=[pl.BlockSpec(memory_space=pltpu.SMEM)] + [pl.BlockSpec(memory_space=pl.ANY)] * len(pieces),
        out_specs=pl.BlockSpec(memory_space=pl.ANY),
        scratch_shapes=[pltpu.SemaphoreType.DMA((len(pieces),))],
        compiler_params=pltpu.CompilerParams(vmem_limit_bytes=SMALL_VMEM_BYTES),
        name="assemble",
    )(place, *pieces)


def square_shards(data, surface_traces, primaries, panel_owner):
    panels = panel_owner.shape[0]
    side = data.shape[1] // 2
    rows = side // CHUNKS
    taps = primaries.shape[2]
    me = lax.axis_index("shot")
    core, chip = me % 2, me // 2
    place = jnp.stack([chip, core, lax.axis_index("rcv")]).astype(jnp.int32)
    holds_two = [jnp.sum(panel_owner // 2 == other) == 2 for other in range(SQUARE // 2)]
    both = jnp.sum(panel_owner // 2 == chip) == 2
    neighbours_full = functools.reduce(
        jnp.logical_or, [holds_two[at] & holds_two[at ^ bit] for at in range(SQUARE // 2) for bit in (1, 2) if at < at ^ bit]
    )

    own_a, own_b, across, down = [], [], [], []
    for chunk in range(CHUNKS):
        there = lax.dynamic_slice_in_dim(surface_traces, (1 - core) * side + chunk * rows, rows, axis=1)
        a, b = pick(chunk, panel_owner, place, surface_traces, flip(there, CORE))
        own_a.append(a)
        own_b.append(b)
        across.append(flip(a, ACROSS))
        down.append(flip(b, DOWN))

    own_a[-1], primaries, data_there = lax.optimization_barrier((own_a[-1], primaries, data))
    ring = lax.axis_size("rcv")
    blocks, bit = primaries[None], 1
    while bit < ring:
        blocks = jnp.concatenate([blocks, lax.ppermute(blocks, "rcv", [(i, i ^ bit) for i in range(ring)])])
        bit *= 2
    blocks = jnp.concatenate([blocks, flip(blocks, CORE)], axis=1)
    blocks = jnp.pad(blocks.astype(jnp.float32), ((0, 0), (0, 0), (0, 0), (0, taps)))
    bands = bands_of(blocks, place)
    plan = plan_of(panel_owner, place)
    other_data = flip(lax.dynamic_slice_in_dim(data_there, (1 - core) * side, side, axis=1), CORE)
    across[0], down[0], bands = lax.optimization_barrier((across[0], down[0], bands))

    sources, early = [], []
    for chunk in range(CHUNKS):
        across_again = flip(jnp.where(both, own_b[chunk], down[chunk]), ACROSS)
        down_again = flip(jnp.where(both, own_a[chunk], across[chunk]), DOWN)
        first = [own_a[chunk], own_b[chunk], across[chunk], down[chunk]]
        early.append(sum_of(plan, place, first, bands, panels, taps))
        sources.append([across_again, down_again])

    def finish(sources, steps):
        kept, returned = [], []
        for chunk in range(CHUNKS):
            mine, others = sum_of(plan, place, sources[chunk], bands, steps, taps, (chunk, early[chunk], data, other_data))
            kept.append(mine)
            returned.append(flip(others, CORE))
        return assemble(place, kept + returned, data)

    def third_step():
        return finish([[a, d, flip(d, ACROSS), flip(a, DOWN)] for a, d in sources], panels - 1)

    residual = finish(sources, 2)
    return lax.cond(neighbours_full, third_step, lambda: residual)


def solution(mesh):
    placed = (P("shot", "rcv", None), P("shot", "rcv", None), P("shot", "rcv", None), P())
    shards = square_shards if mesh.shape["shot"] == SQUARE else summed_broadcasts
    return jax.shard_map(shards, mesh=mesh, in_specs=placed, out_specs=P("shot", "rcv", None), check_vma=False)
```

time: 74 us -> 72 us (0.973)
  other arithmetic: 8.63 us -> 1.91 us
  waiting for transfers between devices: 12 us -> 5.54 us
  Pallas kernels: 21.2 us -> 27.3 us
  starting transfers between devices: 22 us -> 26.7 us
  loops' own time: 3.01 us -> 0.19 us
  local copies, waits for them, and re-layouts: 3.99 us -> 6.06 us
  between operations: 2.45 us -> 3.47 us
    ppermute x13 -> x14, waiting for transfers between devices: 12 us -> 5.54 us  [flip(): return lax.ppermute(value, 'shot', [(i, i ^ bit) for i in range(SQUARE)])]
    pallas_call x2 -> x8, Pallas kernels: 12.9 us -> 19 us  [the longest x4 14.6 us: sum_of(): pl.pallas_call(functools.partial(sum_kernel, last), out_shape=out_shape,...]
    ppermute x13 -> x14, starting transfers between devices: 15.8 us -> 21.3 us  [flip(): return lax.ppermute(value, 'shot', [(i, i ^ bit) for i in range(SQUARE)])]
    select_n x7 -> x4, other arithmetic: 5.48 us -> 0.24 us  [the longest x2 0.13 us: square_shards(): down_again = flip(jnp.where(both, own_a[chunk], across[chunk]), DOWN)]
    another operation x1, loops' own time: 3.01 us -> 0.19 us  [square_shards(): return lax.cond(neighbours_full, third_step, lambda: residual)]
    unnamed x6 -> x40, local copies, waits for them, and re-layouts: 0.88 us -> 2.8 us
    ppermute x3 -> x2, starting transfers between devices: 6.17 us -> 5.46 us  [square_shards(): lax.ppermute(blocks, 'rcv', [(i, i ^ bit) for i in range(ring)])]
  transfers between devices with their start and end apart: 16 -> 16, of which waited for: 5 -> 4; matrix products, arithmetic and copies ran while one was open for 12% -> 4% of each run, Pallas kernels for 29% -> 37%
where the time goes in v3:
time: 72 us; the launch traced here: 71.2 us
  Pallas kernels  27.3 us (38%)
  starting transfers between devices  26.7 us (37%)
  local copies, waits for them, and re-layouts  6.06 us (8%)
  waiting for transfers between devices  5.54 us (8%)
  between operations  3.47 us (5%)
  other arithmetic  1.91 us (3%)
    ppermute x14, starting transfers between devices, flip(): return lax.ppermute(value, 'shot', [(i, i ^ bit) for i in range(SQUARE)])  21.3 us
    pallas_call x4, Pallas kernels, sum_of(): pl.pallas_call(functools.partial(sum_kernel, last), out_shape=out_shape,...  14.6 us
    pallas_call x1, Pallas kernels, bands_of(): pl.pallas_call(band_kernel, out_shape=jax.ShapeDtypeStruct((panels * heig...  8.32 us
    ppermute x14, waiting for transfers between devices, flip(): return lax.ppermute(value, 'shot', [(i, i ^ bit) for i in range(SQUARE)])  5.54 us
    ppermute x2, starting transfers between devices, square_shards(): lax.ppermute(blocks, 'rcv', [(i, i ^ bit) for i in range(ring)])  5.46 us
    unnamed x40, local copies, waits for them, and re-layouts  2.8 us
    pallas_call x2, Pallas kernels, pick(): pl.pallas_call(functools.partial(pick_kernel, chunk), out_shape=(piece, p...  2.27 us
    dynamic_slice x1, local copies, waits for them, and re-layouts, square_shards(): lax.dynamic_slice_in_dim(surface_traces, (1 - core) * side + chunk * rows...  2.24 us
  transfers between devices with their start and end apart: 16, of which 4 were waited for; matrix products, arithmetic and copies ran while one was open for 4% of the time, Pallas kernels for 37%

profile of v3, /device:TPU:1, one launch (start us, length us, event | category | flops | bytes accessed | tf_op | source)
XLA Modules:
  0.0 71.2 jit_solution(11959232324340095889)
XLA Ops:
  0.0 2.2 %constant_dynamic-slice_fusion.1 = (bf16[16,64,256]{2,1,0:T(8,128)(2,1)S(1)}, bf16[16,64,256]{2,1,0:T(8,128)(2,1)}) fusion(bf16[16,256,256]{2,1,0:T(8,128)(2,1)} %slot_ref.3, s32[]{:T(128)S(6)} %select_n.52, s32[]{:T(128)S(6)} %select_n.51), kind=kLoop, calls=%fused_computation.25 | loop fusion | bytes 2097160 | tf_op jit(solution)/shard_map/dynamic_slice | solution.py:341
  2.3 0.0 collective-permute-start.9
  2.3 0.5 collective-permute-start.6
  2.8 0.1 pad_add_fusion.place_ref
  2.8 1.6 %collective-permute-done.9.met_ref = bf16[16,64,256]{2,1,0:T(8,128)(2,1)S(1)} collective-permute-done((bf16[16,64,256]{2,1,0:T(8,128)(2,1)S(1)}, bf16[16,64,256]{2,1,0:T(8,128)(2,1)S(1)}, u32[]{:S(2)}, u32[]{:S(2)}) %collective-permute-start.9) | collective-permute-done | bytes 524320 | tf_op jit(solution)/shard_map/ppermute | solution.py:58
  4.5 0.8 %copy-done.1 = bf16[16,64,256]{2,1,0:T(8,128)(2,1)} copy-done((bf16[16,64,256]{2,1,0:T(8,128)(2,1)}, bf16[16,64,256]{2,1,0:T(8,128)(2,1)S(1)}, u32[]{:S(2)}) %copy-start.1) | copy-done | bytes 524312
  5.3 1.0 %copy-done.2 = bf16[16,64,256]{2,1,0:T(8,128)(2,1)S(1)} copy-done((bf16[16,64,256]{2,1,0:T(8,128)(2,1)S(1)}, bf16[16,64,256]{2,1,0:T(8,128)(2,1)}, u32[]{:S(2)}) %copy-start.2) | copy-done | bytes 524312
  6.3 0.7 pick.3
  7.0 2.9 %collective-permute-start.10 = (bf16[1,6,16,64]{3,2,1,0:T(8,128)(2,1)S(1)}, bf16[1,6,16,64]{3,2,1,0:T(8,128)(2,1)S(1)}, u32[]{:S(2)}, u32[]{:S(2)}) collective-permute-start(bf16[1,6,16,64]{3,2,1,0:T(8,128)(2,1)S(1)} %bitcast.5), channel_id=1, source_target_pairs={{0,1},{1,0},{2,3},{3,2},{4,5},{5,4},{6,7},{7,6},{8,9},{9,8},{10,11... | collective-permute-start | bytes 36872 | tf_op jit(solution)/shard_map/ppermute | solution.py:352
  9.9 1.2 %collective-permute-start.18 = (bf16[16,64,256]{2,1,0:T(8,128)(2,1)S(1)}, bf16[16,64,256]{2,1,0:T(8,128)(2,1)}, u32[]{:S(2)}, u32[]{:S(2)}) collective-permute-start(bf16[16,64,256]{2,1,0:T(8,128)(2,1)S(1)} %get-tuple-element.70.refs_0_), channel_id=1, source_target_pairs={{0,8},{4,12},{8,0},{12,4},{16,24},{20,28},{24,16},{28,20},{1,9},{5... | collective-permute-start | bytes 1572872 | tf_op jit(solution)/shard_map/ppermute | solution.py:58
  11.1 0.0 collective-permute-done.10
  11.1 2.5 %collective-permute-start.11 = (bf16[2,6,16,64]{3,2,1,0:T(8,128)(2,1)S(1)}, bf16[2,6,16,64]{3,2,1,0:T(8,128)(2,1)S(1)}, u32[]{:S(2)}, u32[]{:S(2)}) collective-permute-start(bf16[2,6,16,64]{3,2,1,0:T(8,128)(2,1)S(1)} %pad_maximum_fusion.1), channel_id=1, source_target_pairs={{0,2},{1,3},{2,0},{3,1},{4,6},{5,7},{6,4},{7,5},{8,10},{9,11},{10,... | collective-permute-start | bytes 73736 | tf_op jit(solution)/shard_map/ppermute | solution.py:352
  13.7 0.8 %fusion.12 = (s32[]{:T(128)}, s32[]{:T(128)}, s32[]{:T(128)}, s32[]{:T(128)}, s32[]{:T(128)}) fusion(s32[]{:T(128)} %select_n.48, s32[4]{0:T(128)S(1)} %copy-done.3), kind=kLoop, calls=%fused_computation.31 | loop fusion | flops 115 | bytes 40 | tf_op jit(solution)/shard_map/reduce_sum | solution.py:334
  14.4 1.3 %plan.1.plan_ref = s32[14]{0:T(128)S(1)} custom-call(s32[4]{0:T(128)} %owner_ref.5, s32[3]{0:T(128)S(1)} %pad_add_fusion.place_ref), custom_call_target="tpu_custom_call" | custom-call | tf_op jit(solution)/shard_map/plan/pallas_call | solution.py:133
  16.4 1.3 %collective-permute-start.16 = (bf16[16,64,256]{2,1,0:T(8,128)(2,1)S(1)}, bf16[16,64,256]{2,1,0:T(8,128)(2,1)S(1)}, u32[]{:S(2)}, u32[]{:S(2)}) collective-permute-start(bf16[16,64,256]{2,1,0:T(8,128)(2,1)S(1)} %get-tuple-element.69.refs_1_), channel_id=1, source_target_pairs={{0,16},{4,20},{8,24},{12,28},{16,0},{20,4},{24,8},{28,12},{1,17},{... | collective-permute-start | bytes 1572872 | tf_op jit(solution)/shard_map/ppermute | solution.py:58
  17.7 2.1 %collective-permute-start.12 = (bf16[4,6,16,64]{3,2,1,0:T(8,128)(2,1)S(1)}, bf16[4,6,16,64]{3,2,1,0:T(8,128)(2,1)S(1)}, u32[]{:S(2)}, u32[]{:S(2)}) collective-permute-start(bf16[4,6,16,64]{3,2,1,0:T(8,128)(2,1)S(1)} %pad_maximum_fusion), channel_id=1, source_target_pairs={{0,4},{4,0},{8,12},{12,8},{16,20},{20,16},{24,28},{28,24},{1,5},{5... | collective-permute-start | bytes 147464 | tf_op jit(solution)/shard_map/ppermute | solution.py:58
  19.9 1.0 %constant_dynamic-slice_fusion = bf16[6,128,256]{2,1,0:T(8,128)(2,1)S(1)} fusion(bf16[6,256,256]{2,1,0:T(8,128)(2,1)} %refs_4_.3, s32[]{:T(128)S(6)} %select_n.51), kind=kLoop, calls=%fused_computation.24 | loop fusion | bytes 786436 | tf_op jit(solution)/shard_map/dynamic_slice | solution.py:358
  20.9 0.6 collective-permute-start.15
  21.5 1.6 %pick.2 = (bf16[16,64,256]{2,1,0:T(8,128)(2,1)S(1)}, bf16[16,64,256]{2,1,0:T(8,128)(2,1)S(1)}) custom-call(s32[4]{0:T(128)S(1)} %copy-done.4, s32[3]{0:T(128)S(1)} %pad_add_fusion.place_ref, bf16[16,256,256]{2,1,0:T(8,128)(2,1)S(1)} %copy-done, bf16[16,64,256]{2,1,0:T(8,128)(2,1)} %collective-permute-done.6.met_ref), custom_call_target="tpu_custom_call" | custom-call | tf_op jit(solution)/shard_map/pick/pallas_call | solution.py:166
  23.2 0.3 collective-permute-start.8
  23.5 0.0 collective-permute-done.12
  23.5 1.2 %collective-permute-start.7 = (bf16[16,64,256]{2,1,0:T(8,128)(2,1)S(1)}, bf16[16,64,256]{2,1,0:T(8,128)(2,1)S(1)}, u32[]{:S(2)}, u32[]{:S(2)}) collective-permute-start(bf16[16,64,256]{2,1,0:T(8,128)(2,1)S(1)} %get-tuple-element.61.refs_0_), channel_id=1, source_target_pairs={{0,8},{4,12},{8,0},{12,4},{16,24},{20,28},{24,16},{28,20},{1,9},{5... | collective-permute-start | bytes 1572872 | tf_op jit(solution)/shard_map/ppermute | solution.py:58
  24.7 0.8 %fusion.7.taps_ref = f32[4,12,16,128]{3,2,1,0:T(8,128)S(1)} fusion(bf16[4,6,16,64]{3,2,1,0:T(8,128)(2,1)S(1)} %collective-permute-done.12, bf16[2,6,16,64]{3,2,1,0:T(8,128)(2,1)S(1)} %copy-done.22, bf16[1,6,16,64]{3,2,1,0:T(8,128)(2,1)S(1)} %copy-done.20, bf16[1,6,16,64]{3,2,1,0:T(8,128)(2,1)} %bitcast.4), kind=kLoop, calls=%fused_computation.12 | loop fusion | flops 1277952 | bytes 491520 | tf_op jit(solution)/shard_map/jit(_pad)/pad | solution.py:355
  25.5 8.3 %bands.1.refs_4_.refs_2_ = bf16[4096,1536]{1,0:T(8,128)(2,1)S(1)} custom-call(s32[3]{0:T(128)S(1)} %pad_add_fusion.place_ref, f32[4,12,16,128]{3,2,1,0:T(8,128)S(1)} %fusion.7.taps_ref), custom_call_target="tpu_custom_call" | custom-call | flops 50331648 | bytes 12582912 | tf_op jit(solution)/shard_map/bands/pallas_call | solution.py:78
  33.8 0.0 collective-permute-done.18.refs_2_
  33.8 0.1 broadcast_select_fusion
  33.9 2.9 %collective-permute-start.19 = (bf16[16,64,256]{2,1,0:T(8,128)(2,1)S(1)}, bf16[16,64,256]{2,1,0:T(8,128)(2,1)S(1)}, u32[]{:S(2)}, u32[]{:S(2)}) collective-permute-start(bf16[16,64,256]{2,1,0:T(8,128)(2,1)S(1)} %broadcast_select_fusion), channel_id=1, source_target_pairs={{0,16},{4,20},{8,24},{12,28},{16,0},{20,4},{24,8},{28,12},{1,17},{... | collective-permute-start | bytes 1572872 | tf_op jit(solution)/shard_map/ppermute | solution.py:58
  36.8 0.1 broadcast_select_fusion.1
  36.9 0.2 collective-permute-start.17
  37.0 2.3 %collective-permute-done.8.refs_3_ = bf16[16,64,256]{2,1,0:T(8,128)(2,1)S(1)} collective-permute-done((bf16[16,64,256]{2,1,0:T(8,128)(2,1)S(1)}, bf16[16,64,256]{2,1,0:T(8,128)(2,1)S(1)}, u32[]{:S(2)}, u32[]{:S(2)}) %collective-permute-start.8) | collective-permute-done | bytes 524320 | tf_op jit(solution)/shard_map/ppermute | solution.py:58
  39.3 0.1 broadcast_select_fusion.3
  39.4 0.1 broadcast_select_fusion.2
  39.5 1.3 %collective-permute-start.14 = (bf16[16,64,256]{2,1,0:T(8,128)(2,1)S(1)}, bf16[16,64,256]{2,1,0:T(8,128)(2,1)S(1)}, u32[]{:S(2)}, u32[]{:S(2)}) collective-permute-start(bf16[16,64,256]{2,1,0:T(8,128)(2,1)S(1)} %broadcast_select_fusion.2), channel_id=1, source_target_pairs={{0,16},{4,20},{8,24},{12,28},{16,0},{20,4},{24,8},{28,12},{1,17},{... | collective-permute-start | bytes 1572872 | tf_op jit(solution)/shard_map/ppermute | solution.py:58
  40.8 1.2 %collective-permute-start.13 = (bf16[16,64,256]{2,1,0:T(8,128)(2,1)S(1)}, bf16[16,64,256]{2,1,0:T(8,128)(2,1)S(1)}, u32[]{:S(2)}, u32[]{:S(2)}) collective-permute-start(bf16[16,64,256]{2,1,0:T(8,128)(2,1)S(1)} %broadcast_select_fusion.3), channel_id=1, source_target_pairs={{0,8},{4,12},{8,0},{12,4},{16,24},{20,28},{24,16},{28,20},{1,9},{5... | collective-permute-start | bytes 1572872 | tf_op jit(solution)/shard_map/ppermute | solution.py:58
  42.0 4.7 %early_sum.2.refs_3_ = f32[12,64,256]{2,1,0:T(8,128)S(1)} custom-call(s32[14]{0:T(128)S(1)} %plan.1.plan_ref, s32[3]{0:T(128)S(1)} %pad_add_fusion.place_ref, bf16[16,64,256]{2,1,0:T(8,128)(2,1)S(1)} %get-tuple-element.61.refs_0_, bf16[16,64,256]{2,1,0:T(8,128)(2,1)S(1)} %get-tuple-element.60.refs_1_, ...), custom_call_target="tpu_custom_call" | custom-call | flops 3221225472 | bytes 12582912 | tf_op jit(solution)/shard_map/early_sum/pallas_call | solution.py:278
  46.7 0.0 copy-start.8
  46.7 0.0 copy-start.7
  46.7 5.6 %early_sum.3.refs_3_ = f32[12,64,256]{2,1,0:T(8,128)S(1)} custom-call(s32[14]{0:T(128)S(1)} %plan.1.plan_ref, s32[3]{0:T(128)S(1)} %pad_add_fusion.place_ref, bf16[16,64,256]{2,1,0:T(8,128)(2,1)S(1)} %get-tuple-element.70.refs_0_, bf16[16,64,256]{2,1,0:T(8,128)(2,1)S(1)} %get-tuple-element.69.refs_1_, bf16[16,64,256]{2,1,0:T(8,128)(2,1)} %collective-permute-done.18.refs_2_, ...), custom_call_target="tpu_custom_call" | custom-call | flops 3221225472 | bytes 12582912 | tf_op jit(solution)/shard_map/early_sum/pallas_call | solution.py:278
  52.4 2.2 %residual.7 = (bf16[6,64,256]{2,1,0:T(8,128)(2,1)S(1)}, bf16[6,64,256]{2,1,0:T(8,128)(2,1)S(1)}) custom-call(s32[14]{0:T(128)S(1)} %plan.1.plan_ref, s32[3]{0:T(128)S(1)} %pad_add_fusion.place_ref, bf16[16,64,256]{2,1,0:T(8,128)(2,1)S(1)} %collective-permute-done.17.refs_0_, bf16[16,64,256]{2,1,0:T(8,128)(2,1)S(1)} %collective-permute-done.19.refs_1_, ...), custom_call_target="tpu_custom_call" | custom-call | flops 1610612736 | bytes 6291456 | tf_op jit(solution)/shard_map/residual/pallas_call | solution.py:278
  54.6 5.7 %collective-permute-start.21 = (bf16[6,64,256]{2,1,0:T(8,128)(2,1)S(1)}, bf16[6,64,256]{2,1,0:T(8,128)(2,1)S(1)}, u32[]{:S(2)}, u32[]{:S(2)}) collective-permute-start(bf16[6,64,256]{2,1,0:T(8,128)(2,1)S(1)} %get-tuple-element.73), channel_id=1, source_target_pairs={{0,4},{4,0},{8,12},{12,8},{16,20},{20,16},{24,28},{28,24},{1,5},{5... | collective-permute-start | bytes 589832 | tf_op jit(solution)/shard_map/ppermute | solution.py:58
  60.3 1.5 %collective-permute-done.14.refs_1_ = bf16[16,64,256]{2,1,0:T(8,128)(2,1)S(1)} collective-permute-done((bf16[16,64,256]{2,1,0:T(8,128)(2,1)S(1)}, bf16[16,64,256]{2,1,0:T(8,128)(2,1)S(1)}, u32[]{:S(2)}, u32[]{:S(2)}) %collective-permute-start.14) | collective-permute-done | bytes 524320 | tf_op jit(solution)/shard_map/ppermute | solution.py:58
  61.8 0.1 collective-permute-done.13.refs_0_
  61.9 2.2 %residual.6 = (bf16[6,64,256]{2,1,0:T(8,128)(2,1)S(1)}, bf16[6,64,256]{2,1,0:T(8,128)(2,1)S(1)}) custom-call(s32[14]{0:T(128)S(1)} %plan.1.plan_ref, s32[3]{0:T(128)S(1)} %pad_add_fusion.place_ref, bf16[16,64,256]{2,1,0:T(8,128)(2,1)S(1)} %collective-permute-done.13.refs_0_, bf16[16,64,256]{2,1,0:T(8,128)(2,1)S(1)} %collective-permute-done.14.refs_1_, ...), custom_call_target="tpu_custom_call" | custom-call | flops 1610612736 | bytes 6291456 | tf_op jit(solution)/shard_map/residual/pallas_call | solution.py:278
  64.1 2.7 %collective-permute-start.20 = (bf16[6,64,256]{2,1,0:T(8,128)(2,1)S(1)}, bf16[6,64,256]{2,1,0:T(8,128)(2,1)S(1)}, u32[]{:S(2)}, u32[]{:S(2)}) collective-permute-start(bf16[6,64,256]{2,1,0:T(8,128)(2,1)S(1)} %get-tuple-element.72), channel_id=1, source_target_pairs={{0,4},{4,0},{8,12},{12,8},{16,20},{20,16},{24,28},{28,24},{1,5},{5... | collective-permute-start | bytes 589832 | tf_op jit(solution)/shard_map/ppermute | solution.py:58
  69.4 0.8 %assemble.3 = bf16[6,256,256]{2,1,0:T(8,128)(2,1)S(1)} custom-call(s32[3]{0:T(128)S(1)} %pad_add_fusion.place_ref, bf16[6,64,256]{2,1,0:T(8,128)(2,1)S(1)} %get-tuple-element.68.refs_0_, bf16[6,64,256]{2,1,0:T(8,128)(2,1)S(1)} %get-tuple-element.71.refs_1_, bf16[6,64,256]{2,1,0:T(8,128)(2,1)S(1)} %collective-permute-done.20.refs_2_, ...), custom_call_target="tpu_custom_call" | custom-call | tf_op jit(solution)/shard_map/assemble/pallas_call | solution.py:314
  70.1 0.2 conditional.1
  70.3 0.0 copy-start.17
  70.3 0.9 %copy-done.17 = bf16[6,256,256]{2,1,0:T(8,128)(2,1)} copy-done((bf16[6,256,256]{2,1,0:T(8,128)(2,1)}, bf16[6,256,256]{2,1,0:T(8,128)(2,1)S(1)}, u32[]{:S(2)}) %copy-start.17) | copy-done | bytes 786456
  (45 shorter events, 0.1 us)
Async XLA Ops:
  0.0 5.3 %copy-start = (bf16[16,256,256]{2,1,0:T(8,128)(2,1)S(1)}, bf16[16,256,256]{2,1,0:T(8,128)(2,1)}, u32[]{:S(2)}) copy-start(bf16[16,256,256]{2,1,0:T(8,128)(2,1)} %slot_ref.3) | copy-start | bytes 6291460
  0.0 5.3 %copy-start.3 = (s32[4]{0:T(128)S(1)}, s32[4]{0:T(128)}, u32[]{:S(2)}) copy-start(s32[4]{0:T(128)} %owner_ref.5) | copy-start | bytes 52
  0.0 7.0 %copy-start.18 = (bf16[6,16,64]{2,1,0:T(8,128)(2,1)S(1)}, bf16[6,16,64]{2,1,0:T(8,128)(2,1)}, u32[]{:S(2)}) copy-start(bf16[6,16,64]{2,1,0:T(8,128)(2,1)} %param.8) | copy-start | bytes 36868
  2.3 19.3 %copy-start.4 = (s32[4]{0:T(128)S(1)}, s32[4]{0:T(128)}, u32[]{:S(2)}) copy-start(s32[4]{0:T(128)} %owner_ref.5) | copy-start | bytes 52
  2.3 2.2 %collective-permute-start.9 = (bf16[16,64,256]{2,1,0:T(8,128)(2,1)S(1)}, bf16[16,64,256]{2,1,0:T(8,128)(2,1)S(1)}, u32[]{:S(2)}, u32[]{:S(2)}) collective-permute-start(bf16[16,64,256]{2,1,0:T(8,128)(2,1)S(1)} %get-tuple-element.80), channel_id=1, source_target_pairs={{0,4},{4,0},{8,12},{12,8},{16,20},{20,16},{24,28},{28,24},{1,5},{5... | collective-permute-start | bytes 1572872 | tf_op jit(solution)/shard_map/ppermute | solution.py:58
  2.3 19.2 %collective-permute-start.6 = (bf16[16,64,256]{2,1,0:T(8,128)(2,1)}, bf16[16,64,256]{2,1,0:T(8,128)(2,1)}, u32[]{:S(2)}, u32[]{:S(2)}) collective-permute-start(bf16[16,64,256]{2,1,0:T(8,128)(2,1)} %get-tuple-element.81), channel_id=1, source_target_pairs={{0,4},{4,0},{8,12},{12,8},{16,20},{20,16},{24,28},{28,24},{1,5},{5... | collective-permute-start | bytes 1572872 | tf_op jit(solution)/shard_map/ppermute | solution.py:58
  4.5 0.8 %copy-start.1 = (bf16[16,64,256]{2,1,0:T(8,128)(2,1)}, bf16[16,64,256]{2,1,0:T(8,128)(2,1)S(1)}, u32[]{:S(2)}) copy-start(bf16[16,64,256]{2,1,0:T(8,128)(2,1)S(1)} %collective-permute-done.9.met_ref) | copy-start | bytes 1572868
  5.3 1.0 %copy-start.2 = (bf16[16,64,256]{2,1,0:T(8,128)(2,1)S(1)}, bf16[16,64,256]{2,1,0:T(8,128)(2,1)}, u32[]{:S(2)}) copy-start(bf16[16,64,256]{2,1,0:T(8,128)(2,1)} %copy-done.1) | copy-start | bytes 1572868
  7.0 4.1 %collective-permute-start.10 = (bf16[1,6,16,64]{3,2,1,0:T(8,128)(2,1)S(1)}, bf16[1,6,16,64]{3,2,1,0:T(8,128)(2,1)S(1)}, u32[]{:S(2)}, u32[]{:S(2)}) collective-permute-start(bf16[1,6,16,64]{3,2,1,0:T(8,128)(2,1)S(1)} %bitcast.5), channel_id=1, source_target_pairs={{0,1},{1,0},{2,3},{3,2},{4,5},{5,4},{6,7},{7,6},{8,9},{9,8},{10,11... | collective-permute-start | bytes 36872 | tf_op jit(solution)/shard_map/ppermute | solution.py:352
  9.9 23.9 %collective-permute-start.18 = (bf16[16,64,256]{2,1,0:T(8,128)(2,1)S(1)}, bf16[16,64,256]{2,1,0:T(8,128)(2,1)}, u32[]{:S(2)}, u32[]{:S(2)}) collective-permute-start(bf16[16,64,256]{2,1,0:T(8,128)(2,1)S(1)} %get-tuple-element.70.refs_0_), channel_id=1, source_target_pairs={{0,8},{4,12},{8,0},{12,4},{16,24},{20,28},{24,16},{28,20},{1,9},{5... | collective-permute-start | bytes 1572872 | tf_op jit(solution)/shard_map/ppermute | solution.py:58
  11.1 8.8 %copy-start.19 = (bf16[1,6,16,64]{3,2,1,0:T(8,128)(2,1)}, bf16[1,6,16,64]{3,2,1,0:T(8,128)(2,1)S(1)}, u32[]{:S(2)}) copy-start(bf16[1,6,16,64]{3,2,1,0:T(8,128)(2,1)S(1)} %collective-permute-done.10) | copy-start | bytes 36868
  11.1 6.6 %collective-permute-start.11 = (bf16[2,6,16,64]{3,2,1,0:T(8,128)(2,1)S(1)}, bf16[2,6,16,64]{3,2,1,0:T(8,128)(2,1)S(1)}, u32[]{:S(2)}, u32[]{:S(2)}) collective-permute-start(bf16[2,6,16,64]{3,2,1,0:T(8,128)(2,1)S(1)} %pad_maximum_fusion.1), channel_id=1, source_target_pairs={{0,2},{1,3},{2,0},{3,1},{4,6},{5,7},{6,4},{7,5},{8,10},{9,11},{10,... | collective-permute-start | bytes 73736 | tf_op jit(solution)/shard_map/ppermute | solution.py:352
  16.4 20.4 %collective-permute-start.16 = (bf16[16,64,256]{2,1,0:T(8,128)(2,1)S(1)}, bf16[16,64,256]{2,1,0:T(8,128)(2,1)S(1)}, u32[]{:S(2)}, u32[]{:S(2)}) collective-permute-start(bf16[16,64,256]{2,1,0:T(8,128)(2,1)S(1)} %get-tuple-element.69.refs_1_), channel_id=1, source_target_pairs={{0,16},{4,20},{8,24},{12,28},{16,0},{20,4},{24,8},{28,12},{1,17},{... | collective-permute-start | bytes 1572872 | tf_op jit(solution)/shard_map/ppermute | solution.py:58
  17.7 2.2 %copy-start.21 = (bf16[2,6,16,64]{3,2,1,0:T(8,128)(2,1)}, bf16[2,6,16,64]{3,2,1,0:T(8,128)(2,1)S(1)}, u32[]{:S(2)}) copy-start(bf16[2,6,16,64]{3,2,1,0:T(8,128)(2,1)S(1)} %collective-permute-done.11) | copy-start | bytes 73732
  17.7 5.7 %collective-permute-start.12 = (bf16[4,6,16,64]{3,2,1,0:T(8,128)(2,1)S(1)}, bf16[4,6,16,64]{3,2,1,0:T(8,128)(2,1)S(1)}, u32[]{:S(2)}, u32[]{:S(2)}) collective-permute-start(bf16[4,6,16,64]{3,2,1,0:T(8,128)(2,1)S(1)} %pad_maximum_fusion), channel_id=1, source_target_pairs={{0,4},{4,0},{8,12},{12,8},{16,20},{20,16},{24,28},{28,24},{1,5},{5... | collective-permute-start | bytes 147464 | tf_op jit(solution)/shard_map/ppermute | solution.py:58
  20.9 3.8 %copy-start.20 = (bf16[1,6,16,64]{3,2,1,0:T(8,128)(2,1)S(1)}, bf16[1,6,16,64]{3,2,1,0:T(8,128)(2,1)}, u32[]{:S(2)}) copy-start(bf16[1,6,16,64]{3,2,1,0:T(8,128)(2,1)} %copy-done.19) | copy-start | bytes 36868
  20.9 3.7 %copy-start.22 = (bf16[2,6,16,64]{3,2,1,0:T(8,128)(2,1)S(1)}, bf16[2,6,16,64]{3,2,1,0:T(8,128)(2,1)}, u32[]{:S(2)}) copy-start(bf16[2,6,16,64]{3,2,1,0:T(8,128)(2,1)} %copy-done.21) | copy-start | bytes 73732
  20.9 31.4 %collective-permute-start.15 = (bf16[6,128,256]{2,1,0:T(8,128)(2,1)S(1)}, bf16[6,128,256]{2,1,0:T(8,128)(2,1)S(1)}, u32[]{:S(2)}, u32[]{:S(2)}) collective-permute-start(bf16[6,128,256]{2,1,0:T(8,128)(2,1)S(1)} %constant_dynamic-slice_fusion), channel_id=1, source_target_pairs={{0,4},{4,0},{8,12},{12,8},{16,20},{20,16},{24,28},{28,24},{1,5},{5... | collective-permute-start | bytes 1179656 | tf_op jit(solution)/shard_map/ppermute | solution.py:58
  23.2 16.2 %collective-permute-start.8 = (bf16[16,64,256]{2,1,0:T(8,128)(2,1)S(1)}, bf16[16,64,256]{2,1,0:T(8,128)(2,1)S(1)}, u32[]{:S(2)}, u32[]{:S(2)}) collective-permute-start(bf16[16,64,256]{2,1,0:T(8,128)(2,1)S(1)} %get-tuple-element.60.refs_1_), channel_id=1, source_target_pairs={{0,16},{4,20},{8,24},{12,28},{16,0},{20,4},{24,8},{28,12},{1,17},{... | collective-permute-start | bytes 1572872 | tf_op jit(solution)/shard_map/ppermute | solution.py:58
  23.5 15.8 %collective-permute-start.7 = (bf16[16,64,256]{2,1,0:T(8,128)(2,1)S(1)}, bf16[16,64,256]{2,1,0:T(8,128)(2,1)S(1)}, u32[]{:S(2)}, u32[]{:S(2)}) collective-permute-start(bf16[16,64,256]{2,1,0:T(8,128)(2,1)S(1)} %get-tuple-element.61.refs_0_), channel_id=1, source_target_pairs={{0,8},{4,12},{8,0},{12,4},{16,24},{20,28},{24,16},{28,20},{1,9},{5... | collective-permute-start | bytes 1572872 | tf_op jit(solution)/shard_map/ppermute | solution.py:58
  33.8 28.1 %copy-start.5 = (bf16[4096,1536]{1,0:T(8,128)(2,1)}, bf16[4096,1536]{1,0:T(8,128)(2,1)S(1)}, u32[]{:S(2)}) copy-start(bf16[4096,1536]{1,0:T(8,128)(2,1)S(1)} %bands.1.refs_4_.refs_2_) | copy-start | bytes 37748740
  33.9 18.4 %collective-permute-start.19 = (bf16[16,64,256]{2,1,0:T(8,128)(2,1)S(1)}, bf16[16,64,256]{2,1,0:T(8,128)(2,1)S(1)}, u32[]{:S(2)}, u32[]{:S(2)}) collective-permute-start(bf16[16,64,256]{2,1,0:T(8,128)(2,1)S(1)} %broadcast_select_fusion), channel_id=1, source_target_pairs={{0,16},{4,20},{8,24},{12,28},{16,0},{20,4},{24,8},{28,12},{1,17},{... | collective-permute-start | bytes 1572872 | tf_op jit(solution)/shard_map/ppermute | solution.py:58
  36.9 15.5 %collective-permute-start.17 = (bf16[16,64,256]{2,1,0:T(8,128)(2,1)S(1)}, bf16[16,64,256]{2,1,0:T(8,128)(2,1)S(1)}, u32[]{:S(2)}, u32[]{:S(2)}) collective-permute-start(bf16[16,64,256]{2,1,0:T(8,128)(2,1)S(1)} %broadcast_select_fusion.1), channel_id=1, source_target_pairs={{0,8},{4,12},{8,0},{12,4},{16,24},{20,28},{24,16},{28,20},{1,9},{5... | collective-permute-start | bytes 1572872 | tf_op jit(solution)/shard_map/ppermute | solution.py:58
  39.5 22.3 %collective-permute-start.14 = (bf16[16,64,256]{2,1,0:T(8,128)(2,1)S(1)}, bf16[16,64,256]{2,1,0:T(8,128)(2,1)S(1)}, u32[]{:S(2)}, u32[]{:S(2)}) collective-permute-start(bf16[16,64,256]{2,1,0:T(8,128)(2,1)S(1)} %broadcast_select_fusion.2), channel_id=1, source_target_pairs={{0,16},{4,20},{8,24},{12,28},{16,0},{20,4},{24,8},{28,12},{1,17},{... | collective-permute-start | bytes 1572872 | tf_op jit(solution)/shard_map/ppermute | solution.py:58
  40.8 21.1 %collective-permute-start.13 = (bf16[16,64,256]{2,1,0:T(8,128)(2,1)S(1)}, bf16[16,64,256]{2,1,0:T(8,128)(2,1)S(1)}, u32[]{:S(2)}, u32[]{:S(2)}) collective-permute-start(bf16[16,64,256]{2,1,0:T(8,128)(2,1)S(1)} %broadcast_select_fusion.3), channel_id=1, source_target_pairs={{0,8},{4,12},{8,0},{12,4},{16,24},{20,28},{24,16},{28,20},{1,9},{5... | collective-permute-start | bytes 1572872 | tf_op jit(solution)/shard_map/ppermute | solution.py:58
  46.7 15.2 %copy-start.8 = (f32[12,64,256]{2,1,0:T(8,128)}, f32[12,64,256]{2,1,0:T(8,128)S(1)}, u32[]{:S(2)}) copy-start(f32[12,64,256]{2,1,0:T(8,128)S(1)} %early_sum.2.refs_3_) | copy-start | bytes 2359300
  46.7 5.6 %copy-start.7 = (bf16[6,256,256]{2,1,0:T(8,128)(2,1)S(1)}, bf16[6,256,256]{2,1,0:T(8,128)(2,1)}, u32[]{:S(2)}) copy-start(bf16[6,256,256]{2,1,0:T(8,128)(2,1)} %refs_4_.3) | copy-start | bytes 2359300
  52.3 2.2 %copy-start.9 = (f32[12,64,256]{2,1,0:T(8,128)}, f32[12,64,256]{2,1,0:T(8,128)S(1)}, u32[]{:S(2)}) copy-start(f32[12,64,256]{2,1,0:T(8,128)S(1)} %early_sum.3.refs_3_) | copy-start | bytes 2359300
  52.3 2.2 %copy-start.11 = (bf16[16,64,256]{2,1,0:T(8,128)(2,1)}, bf16[16,64,256]{2,1,0:T(8,128)(2,1)S(1)}, u32[]{:S(2)}) copy-start(bf16[16,64,256]{2,1,0:T(8,128)(2,1)S(1)} %collective-permute-done.19.refs_1_) | copy-start | bytes 1572868
  52.4 2.2 %copy-start.13 = (bf16[16,64,256]{2,1,0:T(8,128)(2,1)}, bf16[16,64,256]{2,1,0:T(8,128)(2,1)S(1)}, u32[]{:S(2)}) copy-start(bf16[16,64,256]{2,1,0:T(8,128)(2,1)S(1)} %collective-permute-done.17.refs_0_) | copy-start | bytes 1572868
  54.6 14.8 %copy-start.10 = (f32[12,64,256]{2,1,0:T(8,128)S(1)}, f32[12,64,256]{2,1,0:T(8,128)}, u32[]{:S(2)}) copy-start(f32[12,64,256]{2,1,0:T(8,128)} %copy-done.9) | copy-start | bytes 2359300
  54.6 14.8 %collective-permute-start.21 = (bf16[6,64,256]{2,1,0:T(8,128)(2,1)S(1)}, bf16[6,64,256]{2,1,0:T(8,128)(2,1)S(1)}, u32[]{:S(2)}, u32[]{:S(2)}) collective-permute-start(bf16[6,64,256]{2,1,0:T(8,128)(2,1)S(1)} %get-tuple-element.73), channel_id=1, source_target_pairs={{0,4},{4,0},{8,12},{12,8},{16,20},{20,16},{24,28},{28,24},{1,5},{5... | collective-permute-start | bytes 589832 | tf_op jit(solution)/shard_map/ppermute | solution.py:58
  61.8 2.3 %copy-start.15 = (bf16[16,64,256]{2,1,0:T(8,128)(2,1)}, bf16[16,64,256]{2,1,0:T(8,128)(2,1)S(1)}, u32[]{:S(2)}) copy-start(bf16[16,64,256]{2,1,0:T(8,128)(2,1)S(1)} %collective-permute-done.14.refs_1_) | copy-start | bytes 1572868
  61.9 2.2 %copy-start.16 = (bf16[16,64,256]{2,1,0:T(8,128)(2,1)}, bf16[16,64,256]{2,1,0:T(8,128)(2,1)S(1)}, u32[]{:S(2)}) copy-start(bf16[16,64,256]{2,1,0:T(8,128)(2,1)S(1)} %collective-permute-done.13.refs_0_) | copy-start | bytes 1572868
  64.1 5.3 %collective-permute-start.20 = (bf16[6,64,256]{2,1,0:T(8,128)(2,1)S(1)}, bf16[6,64,256]{2,1,0:T(8,128)(2,1)S(1)}, u32[]{:S(2)}, u32[]{:S(2)}) collective-permute-start(bf16[6,64,256]{2,1,0:T(8,128)(2,1)S(1)} %get-tuple-element.72), channel_id=1, source_target_pairs={{0,4},{4,0},{8,12},{12,8},{16,20},{20,16},{24,28},{28,24},{1,5},{5... | collective-permute-start | bytes 589832 | tf_op jit(solution)/shard_map/ppermute | solution.py:58
  70.3 0.9 %copy-start.17 = (bf16[6,256,256]{2,1,0:T(8,128)(2,1)}, bf16[6,256,256]{2,1,0:T(8,128)(2,1)S(1)}, u32[]{:S(2)}) copy-start(bf16[6,256,256]{2,1,0:T(8,128)(2,1)S(1)} %get-tuple-element.113) | copy-start | bytes 2359300

commit v4 on v3

--- a/solution.py
+++ b/solution.py
@@ -11,8 +11,11 @@
 SQUARE = 8
 CHUNKS = 2
 FIRST_SOURCES = 4
-VMEM_BYTES = 20 * 1024 * 1024
+VMEM_BYTES = 16 * 1024 * 1024
 SMALL_VMEM_BYTES = 2 * 1024 * 1024
+IN_SMEM = pl.BlockSpec(memory_space=pltpu.SMEM)
+ANYWHERE = pl.BlockSpec(memory_space=pl.ANY)
+NO_COST = pl.CostEstimate(flops=0, bytes_accessed=0, transcendentals=0)
 
 
 def broadcast(value, axis, root):
@@ -135,43 +138,58 @@
         out_shape=jax.ShapeDtypeStruct((3 * owner.shape[0] + 2,), jnp.int32),
         in_specs=[pl.BlockSpec(memory_space=pltpu.SMEM)] * 2,
         out_specs=pl.BlockSpec(memory_space=pltpu.SMEM),
+        cost_estimate=NO_COST,
         name="plan",
     )(owner, place)
 
 
-def pick_kernel(chunk, owner_ref, place_ref, slot_ref, met_ref, a_ref, b_ref, sems):
+def pick_kernel(passed, before, owner_ref, place_ref, slot_ref, met_ref, *refs):
     chip, core = place_ref[0], place_ref[1]
     first_owns, second_owns = jnp.bool_(False), jnp.bool_(False)
     for panel in range(owner_ref.shape[0]):
         first_owns = first_owns | (owner_ref[panel] == 2 * chip)
         second_owns = second_owns | (owner_ref[panel] == 2 * chip + 1)
-    rows = met_ref.shape[1]
-    start = pl.multiple_of((core * CHUNKS + chunk) * rows, rows)
-    here_ref = slot_ref.at[:, pl.ds(start, rows), :]
-    for index, (out_ref, mine) in enumerate(((a_ref, first_owns == (core == 0)), (b_ref, second_owns == (core == 1)))):
-        @pl.when(mine)
-        def _():
-            pltpu.make_async_copy(here_ref, out_ref, sems.at[index]).start()
-
-        @pl.when(jnp.logical_not(mine))
-        def _():
-            pltpu.make_async_copy(met_ref, out_ref, sems.at[index]).start()
-
-    for index, out_ref in enumerate((a_ref, b_ref)):
-        pltpu.make_async_copy(met_ref, out_ref, sems.at[index]).wait()
-
-
-def pick(chunk, owner, place, slot, met):
-    piece = jax.ShapeDtypeStruct(met.shape, met.dtype)
-    return pl.pallas_call(
-        functools.partial(pick_kernel, chunk),
-        out_shape=(piece, piece),
-        in_specs=[pl.BlockSpec(memory_space=pltpu.SMEM)] * 2 + [pl.BlockSpec(memory_space=pl.ANY)] * 2,
-        out_specs=[pl.BlockSpec(memory_space=pl.ANY)] * 2,
-        scratch_shapes=[pltpu.SemaphoreType.DMA((2,))],
+    outs, sems = refs[passed + before : -1], refs[-1]
+    points, rows, _ = outs[0].shape
+    shots = met_ref.shape[0] - points
+    for chunk in range(CHUNKS):
+        here_ref = slot_ref.at[:, pl.ds(pl.multiple_of((core * CHUNKS + chunk) * rows, rows), rows), :]
+        there_ref = met_ref.at[pl.ds(shots, points), pl.ds(chunk * rows, rows), :]
+        for which, mine in enumerate((first_owns == (core == 0), second_owns == (core == 1))):
+            index = 2 * chunk + which
+
+            @pl.when(mine)
+            def _():
+                pltpu.make_async_copy(here_ref, outs[index], sems.at[index]).start()
+
+            @pl.when(jnp.logical_not(mine))
+            def _():
+                pltpu.make_async_copy(there_ref, outs[index], sems.at[index]).start()
+
+    copies = [pltpu.make_async_copy(refs[index], outs[2 * CHUNKS + index], sems.at[2 * CHUNKS + index]) for index in range(passed)]
+    for copy in copies:
+        copy.start()
+    for index in range(2 * CHUNKS):
+        pltpu.make_async_copy(met_ref.at[pl.ds(shots, points), pl.ds(0, rows), :], outs[index], sems.at[index]).wait()
+    for copy in copies:
+        copy.wait()
+
+
+def pick(owner, place, slot, met, passed, before):
+    points, side, length = slot.shape[0], met.shape[1], met.shape[2]
+    outs = [jax.ShapeDtypeStruct((points, side // CHUNKS, length), met.dtype)] * (2 * CHUNKS)
+    outs += [jax.ShapeDtypeStruct(value.shape, value.dtype) for value in passed]
+    outs = pl.pallas_call(
+        functools.partial(pick_kernel, len(passed), len(before)),
+        out_shape=tuple(outs),
+        in_specs=[IN_SMEM] * 2 + [ANYWHERE] * (2 + len(passed) + len(before)),
+        out_specs=[ANYWHERE] * len(outs),
+        scratch_shapes=[pltpu.SemaphoreType.DMA((len(outs),))],
         compiler_params=pltpu.CompilerParams(vmem_limit_bytes=SMALL_VMEM_BYTES),
+        cost_estimate=NO_COST,
         name="pick",
-    )(owner, place, slot, met)
+    )(owner, place, slot, met, *passed, *before)
+    return outs[0 : 2 * CHUNKS : 2], outs[1 : 2 * CHUNKS : 2], *outs[2 * CHUNKS :]
 
 
 def sum_kernel(last, plan_ref, place_ref, *refs):
@@ -257,7 +275,7 @@
         wanted = plan[3 * panels + (1 if last else 0)]
         return (plan[entries + jnp.maximum(jnp.minimum(step, wanted - 1), 0)], 0)
 
-    in_specs = [pl.BlockSpec(memory_space=pl.ANY)] * len(sources) + [pl.BlockSpec((height, columns), band_place)]
+    in_specs = [ANYWHERE] * len(sources) + [pl.BlockSpec((height, columns), band_place)]
     operands = [*sources, bands]
     if last:
         chunk, early, data, other_data = late
@@ -314,71 +332,64 @@
     return pl.pallas_call(
         assemble_kernel,
         out_shape=jax.ShapeDtypeStruct(like.shape, like.dtype),
-        in_specs=[pl.BlockSpec(memory_space=pltpu.SMEM)] + [pl.BlockSpec(memory_space=pl.ANY)] * len(pieces),
-        out_specs=pl.BlockSpec(memory_space=pl.ANY),
+        in_specs=[IN_SMEM] + [pl.BlockSpec(memory_space=pl.ANY)] * len(pieces),
+        out_specs=ANYWHERE,
         scratch_shapes=[pltpu.SemaphoreType.DMA((len(pieces),))],
         compiler_params=pltpu.CompilerParams(vmem_limit_bytes=SMALL_VMEM_BYTES),
+        cost_estimate=NO_COST,
         name="assemble",
     )(place, *pieces)
 
 
-def square_shards(data, surface_traces, primaries, panel_owner):
+def any_of(flags):
+    return functools.reduce(jnp.logical_or, flags)
+
+
+def exchange(data, surface_traces, primaries, panel_owner, place, third):
     panels = panel_owner.shape[0]
     side = data.shape[1] // 2
     rows = side // CHUNKS
     taps = primaries.shape[2]
-    me = lax.axis_index("shot")
-    core, chip = me % 2, me // 2
-    place = jnp.stack([chip, core, lax.axis_index("rcv")]).astype(jnp.int32)
-    holds_two = [jnp.sum(panel_owner // 2 == other) == 2 for other in range(SQUARE // 2)]
-    both = jnp.sum(panel_owner // 2 == chip) == 2
-    neighbours_full = functools.reduce(
-        jnp.logical_or, [holds_two[at] & holds_two[at ^ bit] for at in range(SQUARE // 2) for bit in (1, 2) if at < at ^ bit]
-    )
-
-    own_a, own_b, across, down = [], [], [], []
-    for chunk in range(CHUNKS):
-        there = lax.dynamic_slice_in_dim(surface_traces, (1 - core) * side + chunk * rows, rows, axis=1)
-        a, b = pick(chunk, panel_owner, place, surface_traces, flip(there, CORE))
-        own_a.append(a)
-        own_b.append(b)
-        across.append(flip(a, ACROSS))
-        down.append(flip(b, DOWN))
-
-    own_a[-1], primaries, data_there = lax.optimization_barrier((own_a[-1], primaries, data))
+    core = lax.rem(lax.axis_index("shot"), 2)
+    plan = plan_of(panel_owner, place)
     ring = lax.axis_size("rcv")
-    blocks, bit = primaries[None], 1
+    there = jnp.concatenate([lax.dynamic_slice_in_dim(array, (1 - core) * side, side, axis=1) for array in (data, surface_traces)])
+    met = flip(there, CORE)
+    ahead = lax.ppermute(primaries, "rcv", [(i, i ^ 1) for i in range(ring)])
+    own_a, own_b, primaries = pick(panel_owner, place, surface_traces, met, (primaries,), (ahead,))
+    across, down = [flip(a, ACROSS) for a in own_a], [flip(b, DOWN) for b in own_b]
+    blocks, bit = jnp.stack([primaries, ahead]), 2
     while bit < ring:
         blocks = jnp.concatenate([blocks, lax.ppermute(blocks, "rcv", [(i, i ^ bit) for i in range(ring)])])
         bit *= 2
     blocks = jnp.concatenate([blocks, flip(blocks, CORE)], axis=1)
     blocks = jnp.pad(blocks.astype(jnp.float32), ((0, 0), (0, 0), (0, 0), (0, taps)))
     bands = bands_of(blocks, place)
-    plan = plan_of(panel_owner, place)
-    other_data = flip(lax.dynamic_slice_in_dim(data_there, (1 - core) * side, side, axis=1), CORE)
-    across[0], down[0], bands = lax.optimization_barrier((across[0], down[0], bands))
-
-    sources, early = [], []
+    both = jnp.sum(panel_owner // 2 == place[0]) == 2
+    for_across = [jnp.where(both, own_b[chunk], down[chunk]) for chunk in range(CHUNKS)]
+    for_down = [jnp.where(both, own_a[chunk], across[chunk]) for chunk in range(CHUNKS)]
+
+    kept, returned = [], []
     for chunk in range(CHUNKS):
-        across_again = flip(jnp.where(both, own_b[chunk], down[chunk]), ACROSS)
-        down_again = flip(jnp.where(both, own_a[chunk], across[chunk]), DOWN)
         first = [own_a[chunk], own_b[chunk], across[chunk], down[chunk]]
-        early.append(sum_of(plan, place, first, bands, panels, taps))
-        sources.append([across_again, down_again])
-
-    def finish(sources, steps):
-        kept, returned = [], []
-        for chunk in range(CHUNKS):
-            mine, others = sum_of(plan, place, sources[chunk], bands, steps, taps, (chunk, early[chunk], data, other_data))
-            kept.append(mine)
-            returned.append(flip(others, CORE))
-        return assemble(place, kept + returned, data)
-
-    def third_step():
-        return finish([[a, d, flip(d, ACROSS), flip(a, DOWN)] for a, d in sources], panels - 1)
-
-    residual = finish(sources, 2)
-    return lax.cond(neighbours_full, third_step, lambda: residual)
+        second = [flip(for_across[chunk], ACROSS), flip(for_down[chunk], DOWN)]
+        if third:
+            second += [flip(second[1], ACROSS), flip(second[0], DOWN)]
+        early = sum_of(plan, place, first, bands, panels, taps)
+        mine, others = sum_of(plan, place, second, bands, panels - 1 if third else 2, taps, (chunk, early, data, met))
+        kept.append(mine)
+        returned.append(flip(others, CORE))
+    return assemble(place, kept + returned, data)
+
+
+def square_shards(data, surface_traces, primaries, panel_owner):
+    me = lax.axis_index("shot")
+    place = jnp.stack([me // 2, me % 2, lax.axis_index("rcv")]).astype(jnp.int32)
+    holds_two = [jnp.sum(panel_owner // 2 == other) == 2 for other in range(SQUARE // 2)]
+    neighbours_full = any_of([holds_two[at] & holds_two[at ^ bit] for at in range(SQUARE // 2) for bit in (1, 2) if at < at ^ bit])
+    arguments = (data, surface_traces, primaries, panel_owner, place)
+    residual = exchange(*arguments, False)
+    return lax.while_loop(lambda state: state[0], lambda state: (jnp.bool_(False), exchange(*arguments, True)), (neighbours_full, residual))[1]
 
 
 def solution(mesh):

time: 72 us -> 68.7 us (0.954)
  starting transfers between devices: 26.7 us -> 23.2 us
  other arithmetic: 1.91 us -> 4.93 us
  local copies, waits for them, and re-layouts: 6.06 us -> 3.3 us
    ppermute x14 -> x12, starting transfers between devices: 21.3 us -> 18.5 us  [flip(): return lax.ppermute(value, 'shot', [(i, i ^ bit) for i in range(SQUARE)])]
    select_n x4, other arithmetic: 0.24 us -> 2.33 us  [the longest x2 1.16 us: exchange(): jnp.where(both, own_b[chunk], down[chunk])]
    dynamic_slice x2, local copies, waits for them, and re-layouts: 3.27 us -> 1.39 us  [exchange(): lax.dynamic_slice_in_dim(array, (1 - core) * side, side, axis=1)]
    ppermute x14 -> x12, waiting for transfers between devices: 5.54 us -> 4.07 us  [flip(): return lax.ppermute(value, 'shot', [(i, i ^ bit) for i in range(SQUARE)])]
    ppermute x2, waiting for transfers between devices: 0.01 us -> 1.46 us  [the longest x1 1.14 us: exchange(): ahead = lax.ppermute(primaries, 'rcv', [(i, i ^ 1) for i in range(ring)])]
    unnamed x40 -> x22, local copies, waits for them, and re-layouts: 2.8 us -> 1.91 us
    ppermute x2, starting transfers between devices: 5.46 us -> 4.66 us  [the longest x1 2.37 us: exchange(): lax.ppermute(blocks, 'rcv', [(i, i ^ bit) for i in range(ring)])]
    pallas_call x2 -> x1, Pallas kernels: 2.27 us -> 1.49 us  [pick(): pl.pallas_call(functools.partial(pick_kernel, len(passed), len(before)),...]
  transfers between devices with their start and end apart: 16 -> 14, of which waited for: 4 -> 5; matrix products, arithmetic and copies ran while one was open for 4% -> 7% of each run, Pallas kernels for 37% -> 36%
where the time goes in v4:
time: 68.7 us; the launch traced here: 67.7 us
  Pallas kernels  27 us (39%)
  starting transfers between devices  23.2 us (34%)
  waiting for transfers between devices  5.53 us (8%)
  other arithmetic  4.93 us (7%)
  between operations  3.52 us (5%)
  local copies, waits for them, and re-layouts  3.3 us (5%)
    ppermute x12, starting transfers between devices, flip(): return lax.ppermute(value, 'shot', [(i, i ^ bit) for i in range(SQUARE)])  18.5 us
    pallas_call x4, Pallas kernels, sum_of(): pl.pallas_call(functools.partial(sum_kernel, last), out_shape=out_shape,...  14.6 us
    pallas_call x1, Pallas kernels, bands_of(): pl.pallas_call(band_kernel, out_shape=jax.ShapeDtypeStruct((panels * heig...  8.32 us
    ppermute x12, waiting for transfers between devices, flip(): return lax.ppermute(value, 'shot', [(i, i ^ bit) for i in range(SQUARE)])  4.07 us
    ppermute x1, starting transfers between devices, exchange(): lax.ppermute(blocks, 'rcv', [(i, i ^ bit) for i in range(ring)])  2.37 us
    ppermute x1, starting transfers between devices, exchange(): ahead = lax.ppermute(primaries, 'rcv', [(i, i ^ 1) for i in range(ring)])  2.29 us
    unnamed x22, local copies, waits for them, and re-layouts  1.91 us
    pallas_call x1, Pallas kernels, pick(): pl.pallas_call(functools.partial(pick_kernel, len(passed), len(before)),...  1.49 us
  transfers between devices with their start and end apart: 14, of which 5 were waited for; matrix products, arithmetic and copies ran while one was open for 7% of the time, Pallas kernels for 36%

profile of v4, /device:TPU:1, one launch (start us, length us, event | category | flops | bytes accessed | tf_op | source)
XLA Modules:
  0.0 67.7 jit_solution(5304174624737584936)
XLA Ops:
  0.0 1.4 %constant_dynamic-slice_fusion.2 = bf16[16,128,256]{2,1,0:T(8,128)(2,1)S(1)} fusion(bf16[16,256,256]{2,1,0:T(8,128)(2,1)} %slot_ref.1, s32[]{:T(128)S(6)} %select_n.77), kind=kLoop, calls=%fused_computation.55 | loop fusion | bytes 2097156 | tf_op jit(solution)/shard_map/dynamic_slice | solution.py:356
  1.4 0.1 copy-done.14
  1.5 0.0 copy-start.19
  1.5 0.0 copy-start.23
  1.5 0.1 pad_maximum_fusion.3
  1.6 0.1 collective-permute-start.18
  1.8 0.5 copy-done.19
  2.2 2.3 %collective-permute-start.19 = (bf16[6,16,64]{2,1,0:T(8,128)(2,1)S(1)}, bf16[6,16,64]{2,1,0:T(8,128)(2,1)S(1)}, u32[]{:S(2)}, u32[]{:S(2)}) collective-permute-start(bf16[6,16,64]{2,1,0:T(8,128)(2,1)S(1)} %copy-done.19), channel_id=1, source_target_pairs={{0,1},{1,0},{2,3},{3,2},{4,5},{5,4},{6,7},{7,6},{8,9},{9,8},{10,11... | collective-permute-start | bytes 36872 | tf_op jit(solution)/shard_map/ppermute | solution.py:358
  4.5 0.1 pad_add_fusion.place_ref
  4.6 1.1 %collective-permute-done.19.refs_1_ = bf16[6,16,64]{2,1,0:T(8,128)(2,1)S(1)} collective-permute-done((bf16[6,16,64]{2,1,0:T(8,128)(2,1)S(1)}, bf16[6,16,64]{2,1,0:T(8,128)(2,1)S(1)}, u32[]{:S(2)}, u32[]{:S(2)}) %collective-permute-start.19) | collective-permute-done | bytes 12320 | tf_op jit(solution)/shard_map/ppermute | solution.py:358
  5.7 0.6 copy-done.8
  6.3 0.0 collective-permute-done.18.met_ref.refs_5_
  6.3 0.7 %copy-done.9 = bf16[6,16,64]{2,1,0:T(8,128)(2,1)S(1)} copy-done((bf16[6,16,64]{2,1,0:T(8,128)(2,1)S(1)}, bf16[6,16,64]{2,1,0:T(8,128)(2,1)}, u32[]{:S(2)}) %copy-start.9) | copy-done | bytes 12312
  7.1 1.5 %pick.3 = (bf16[16,64,256]{2,1,0:T(8,128)(2,1)S(1)}, bf16[16,64,256]{2,1,0:T(8,128)(2,1)S(1)}, bf16[16,64,256]{2,1,0:T(8,128)(2,1)S(1)}, bf16[16,64,256]{2,1,0:T(8,128)(2,1)S(1)}, bf16[6,16,64]{2,1,0:T(8,128)(2,1)S(1)}) custom-call(s32[4]{0:T(128)S(1)} %copy-done.23, s32[3]{0:T(128)S(1)} %pad_add_fusion.place_ref, bf16[16,256,256]{2,1,0:T(8,128)(2,1)} %slot_ref.1, ...), custom_call_target="tpu_custom_call" | custom-call | tf_op jit(solution)/shard_map/pick/pallas_call | solution.py:182
  8.6 2.1 %collective-permute-start.26 = (bf16[16,64,256]{2,1,0:T(8,128)(2,1)S(1)}, bf16[16,64,256]{2,1,0:T(8,128)(2,1)}, u32[]{:S(2)}, u32[]{:S(2)}) collective-permute-start(bf16[16,64,256]{2,1,0:T(8,128)(2,1)S(1)} %get-tuple-element.67.refs_1_), channel_id=1, source_target_pairs={{0,16},{4,20},{8,24},{12,28},{16,0},{20,4},{24,8},{28,12},{1,17},{... | collective-permute-start | bytes 1572872 | tf_op jit(solution)/shard_map/ppermute | solution.py:61
  10.7 2.4 %collective-permute-start.24 = (bf16[2,6,16,64]{3,2,1,0:T(8,128)(2,1)S(1)}, bf16[2,6,16,64]{3,2,1,0:T(8,128)(2,1)S(1)}, u32[]{:S(2)}, u32[]{:S(2)}) collective-permute-start(bf16[2,6,16,64]{3,2,1,0:T(8,128)(2,1)S(1)} %pad_maximum_fusion.5), channel_id=1, source_target_pairs={{0,2},{1,3},{2,0},{3,1},{4,6},{5,7},{6,4},{7,5},{8,10},{9,11},{10,... | collective-permute-start | bytes 73736 | tf_op jit(solution)/shard_map/ppermute | solution.py:363
  13.1 1.2 %collective-permute-start.28 = (bf16[16,64,256]{2,1,0:T(8,128)(2,1)S(1)}, bf16[16,64,256]{2,1,0:T(8,128)(2,1)}, u32[]{:S(2)}, u32[]{:S(2)}) collective-permute-start(bf16[16,64,256]{2,1,0:T(8,128)(2,1)S(1)} %get-tuple-element.68.refs_0_), channel_id=1, source_target_pairs={{0,8},{4,12},{8,0},{12,4},{16,24},{20,28},{24,16},{28,20},{1,9},{5... | collective-permute-start | bytes 1572872 | tf_op jit(solution)/shard_map/ppermute | solution.py:61
  14.3 0.3 collective-permute-done.24
  14.6 0.7 pad_maximum_fusion.4
  15.3 2.5 %collective-permute-start.25 = (bf16[4,6,16,64]{3,2,1,0:T(8,128)(2,1)}, bf16[4,6,16,64]{3,2,1,0:T(8,128)(2,1)}, u32[]{:S(2)}, u32[]{:S(2)}) collective-permute-start(bf16[4,6,16,64]{3,2,1,0:T(8,128)(2,1)} %pad_maximum_fusion.4), channel_id=1, source_target_pairs={{0,4},{4,0},{8,12},{12,8},{16,20},{20,16},{24,28},{28,24},{1,5},{5... | collective-permute-start | bytes 147464 | tf_op jit(solution)/shard_map/ppermute | solution.py:61
  17.7 0.8 %fusion.21 = (s32[]{:T(128)}, s32[]{:T(128)}, s32[]{:T(128)}, s32[]{:T(128)}, s32[]{:T(128)}) fusion(s32[]{:T(128)} %select_n.74, s32[4]{0:T(128)S(1)} %copy-done.23), kind=kLoop, calls=%fused_computation.53 | loop fusion | flops 115 | bytes 40 | tf_op jit(solution)/shard_map/reduce_sum | solution.py:368
  18.5 1.1 %plan.3.plan_ref = s32[14]{0:T(128)} custom-call(s32[4]{0:T(128)S(1)} %copy-done.23, s32[3]{0:T(128)S(1)} %pad_add_fusion.place_ref), custom_call_target="tpu_custom_call" | custom-call | tf_op jit(solution)/shard_map/plan/pallas_call | solution.py:136
  20.3 0.7 %collective-permute-start.20 = (bf16[16,64,256]{2,1,0:T(8,128)(2,1)S(1)}, bf16[16,64,256]{2,1,0:T(8,128)(2,1)S(1)}, u32[]{:S(2)}, u32[]{:S(2)}) collective-permute-start(bf16[16,64,256]{2,1,0:T(8,128)(2,1)S(1)} %get-tuple-element.63.refs_1_), channel_id=1, source_target_pairs={{0,16},{4,20},{8,24},{12,28},{16,0},{20,4},{24,8},{28,12},{1,17},{... | collective-permute-start | bytes 1572872 | tf_op jit(solution)/shard_map/ppermute | solution.py:61
  21.0 1.5 %collective-permute-start.22 = (bf16[16,64,256]{2,1,0:T(8,128)(2,1)S(1)}, bf16[16,64,256]{2,1,0:T(8,128)(2,1)S(1)}, u32[]{:S(2)}, u32[]{:S(2)}) collective-permute-start(bf16[16,64,256]{2,1,0:T(8,128)(2,1)S(1)} %get-tuple-element.64.refs_0_), channel_id=1, source_target_pairs={{0,8},{4,12},{8,0},{12,4},{16,24},{20,28},{24,16},{28,20},{1,9},{5... | collective-permute-start | bytes 1572872 | tf_op jit(solution)/shard_map/ppermute | solution.py:61
  22.5 1.0 %fusion.16.taps_ref = f32[4,12,16,128]{3,2,1,0:T(8,128)S(1)} fusion(bf16[4,6,16,64]{3,2,1,0:T(8,128)(2,1)} %collective-permute-done.25, bf16[2,6,16,64]{3,2,1,0:T(8,128)(2,1)} %copy-done.22, bf16[1,6,16,64]{3,2,1,0:T(8,128)(2,1)} %bitcast.13, bf16[1,6,16,64]{3,2,1,0:T(8,128)(2,1)} %bitcast.18), kind=kLoop, calls=%fused_computation.37 | loop fusion | flops 1277952 | bytes 491520 | tf_op jit(solution)/shard_map/jit(_pad)/pad | solution.py:366
  23.5 8.3 %bands.3.refs_4_.refs_2_ = bf16[4096,1536]{1,0:T(8,128)(2,1)S(1)} custom-call(s32[3]{0:T(128)S(1)} %pad_add_fusion.place_ref, f32[4,12,16,128]{3,2,1,0:T(8,128)S(1)} %fusion.16.taps_ref), custom_call_target="tpu_custom_call" | custom-call | flops 50331648 | bytes 12582912 | tf_op jit(solution)/shard_map/bands/pallas_call | solution.py:81
  31.8 0.0 collective-permute-done.26.refs_3_
  31.8 1.1 %broadcast_select_fusion.5 = bf16[16,64,256]{2,1,0:T(8,128)(2,1)S(1)} fusion(bf16[16,64,256]{2,1,0:T(8,128)(2,1)S(1)} %get-tuple-element.67.refs_1_, bf16[16,64,256]{2,1,0:T(8,128)(2,1)} %collective-permute-done.26.refs_3_, pred[]{:T(512)S(6)} %eq.54), kind=kLoop, calls=%fused_computation.26 | loop fusion | flops 262144 | bytes 1572865 | tf_op jit(solution)/shard_map/jit(_where)/select_n | solution.py:369
  32.9 0.1 collective-permute-start.27
  33.0 1.1 %broadcast_select_fusion.4 = bf16[16,64,256]{2,1,0:T(8,128)(2,1)S(1)} fusion(bf16[16,64,256]{2,1,0:T(8,128)(2,1)S(1)} %get-tuple-element.68.refs_0_, bf16[16,64,256]{2,1,0:T(8,128)(2,1)} %collective-permute-done.28.refs_2_, pred[]{:T(512)S(6)} %eq.54), kind=kLoop, calls=%fused_computation.25 | loop fusion | flops 262144 | bytes 1572865 | tf_op jit(solution)/shard_map/jit(_where)/select_n | solution.py:370
  34.1 0.8 %collective-permute-start.29 = (bf16[16,64,256]{2,1,0:T(8,128)(2,1)S(1)}, bf16[16,64,256]{2,1,0:T(8,128)(2,1)S(1)}, u32[]{:S(2)}, u32[]{:S(2)}) collective-permute-start(bf16[16,64,256]{2,1,0:T(8,128)(2,1)S(1)} %broadcast_select_fusion.4), channel_id=1, source_target_pairs={{0,16},{4,20},{8,24},{12,28},{16,0},{20,4},{24,8},{28,12},{1,17},{... | collective-permute-start | bytes 1572872 | tf_op jit(solution)/shard_map/ppermute | solution.py:61
  34.9 1.2 %collective-permute-done.22.refs_2_ = bf16[16,64,256]{2,1,0:T(8,128)(2,1)S(1)} collective-permute-done((bf16[16,64,256]{2,1,0:T(8,128)(2,1)S(1)}, bf16[16,64,256]{2,1,0:T(8,128)(2,1)S(1)}, u32[]{:S(2)}, u32[]{:S(2)}) %collective-permute-start.22) | collective-permute-done | bytes 524320 | tf_op jit(solution)/shard_map/ppermute | solution.py:61
  36.1 0.1 broadcast_select_fusion.6
  36.2 0.1 collective-permute-start.23
  36.3 0.1 broadcast_select_fusion.7
  36.4 1.3 %collective-permute-start.21 = (bf16[16,64,256]{2,1,0:T(8,128)(2,1)S(1)}, bf16[16,64,256]{2,1,0:T(8,128)(2,1)S(1)}, u32[]{:S(2)}, u32[]{:S(2)}) collective-permute-start(bf16[16,64,256]{2,1,0:T(8,128)(2,1)S(1)} %broadcast_select_fusion.7), channel_id=1, source_target_pairs={{0,8},{4,12},{8,0},{12,4},{16,24},{20,28},{24,16},{28,20},{1,9},{5... | collective-permute-start | bytes 1572872 | tf_op jit(solution)/shard_map/ppermute | solution.py:61
  37.6 5.6 %early_sum.7.refs_3_ = f32[12,64,256]{2,1,0:T(8,128)S(1)} custom-call(s32[14]{0:T(128)S(1)} %copy-done.13, s32[3]{0:T(128)S(1)} %pad_add_fusion.place_ref, bf16[16,64,256]{2,1,0:T(8,128)(2,1)S(1)} %get-tuple-element.68.refs_0_, bf16[16,64,256]{2,1,0:T(8,128)(2,1)S(1)} %get-tuple-element.67.refs_1_, bf16[16,64,256]{2,1,0:T(8,128)(2,1)} %collective-permute-done.28.refs_2_, ...), custom_call_target="tpu_custom_call" | custom-call | flops 3221225472 | bytes 12582912 | tf_op jit(solution)/shard_map/early_sum/pallas_call | solution.py:296
  43.2 0.0 copy-start.15
  43.2 4.7 %early_sum.6.refs_3_ = f32[12,64,256]{2,1,0:T(8,128)S(1)} custom-call(s32[14]{0:T(128)S(1)} %copy-done.13, s32[3]{0:T(128)S(1)} %pad_add_fusion.place_ref, bf16[16,64,256]{2,1,0:T(8,128)(2,1)S(1)} %get-tuple-element.64.refs_0_, bf16[16,64,256]{2,1,0:T(8,128)(2,1)S(1)} %get-tuple-element.63.refs_1_, bf16[16,64,256]{2,1,0:T(8,128)(2,1)S(1)} %collective-permute-done.22.refs_2_, ...), custom_call_target="tpu_custom_call" | custom-call | flops 3221225472 | bytes 12582912 | tf_op jit(solution)/shard_map/early_sum/pallas_call | solution.py:296
  48.0 2.2 %residual.7 = (bf16[6,64,256]{2,1,0:T(8,128)(2,1)S(1)}, bf16[6,64,256]{2,1,0:T(8,128)(2,1)S(1)}) custom-call(s32[14]{0:T(128)S(1)} %copy-done.13, s32[3]{0:T(128)S(1)} %pad_add_fusion.place_ref, bf16[16,64,256]{2,1,0:T(8,128)(2,1)S(1)} %collective-permute-done.27.refs_0_, bf16[16,64,256]{2,1,0:T(8,128)(2,1)S(1)} %collective-permute-done.29.refs_1_, ...), custom_call_target="tpu_custom_call" | custom-call | flops 1610612736 | bytes 6291456 | tf_op jit(solution)/shard_map/residual/pallas_call | solution.py:296
  50.2 5.6 %collective-permute-start.31 = (bf16[6,64,256]{2,1,0:T(8,128)(2,1)S(1)}, bf16[6,64,256]{2,1,0:T(8,128)(2,1)S(1)}, u32[]{:S(2)}, u32[]{:S(2)}) collective-permute-start(bf16[6,64,256]{2,1,0:T(8,128)(2,1)S(1)} %get-tuple-element.71), channel_id=1, source_target_pairs={{0,4},{4,0},{8,12},{12,8},{16,20},{20,16},{24,28},{28,24},{1,5},{5... | collective-permute-start | bytes 589832 | tf_op jit(solution)/shard_map/ppermute | solution.py:61
  55.8 2.4 %collective-permute-done.23.refs_1_ = bf16[16,64,256]{2,1,0:T(8,128)(2,1)S(1)} collective-permute-done((bf16[16,64,256]{2,1,0:T(8,128)(2,1)S(1)}, bf16[16,64,256]{2,1,0:T(8,128)(2,1)S(1)}, u32[]{:S(2)}, u32[]{:S(2)}) %collective-permute-start.23) | collective-permute-done | bytes 524320 | tf_op jit(solution)/shard_map/ppermute | solution.py:61
  58.1 0.5 collective-permute-done.21.refs_0_
  58.6 2.2 %residual.6 = (bf16[6,64,256]{2,1,0:T(8,128)(2,1)S(1)}, bf16[6,64,256]{2,1,0:T(8,128)(2,1)S(1)}) custom-call(s32[14]{0:T(128)S(1)} %copy-done.13, s32[3]{0:T(128)S(1)} %pad_add_fusion.place_ref, bf16[16,64,256]{2,1,0:T(8,128)(2,1)S(1)} %collective-permute-done.21.refs_0_, bf16[16,64,256]{2,1,0:T(8,128)(2,1)S(1)} %collective-permute-done.23.refs_1_, ...), custom_call_target="tpu_custom_call" | custom-call | flops 1610612736 | bytes 6291456 | tf_op jit(solution)/shard_map/residual/pallas_call | solution.py:296
  60.8 0.0 copy-start.20
  60.8 2.6 %collective-permute-start.30 = (bf16[6,64,256]{2,1,0:T(8,128)(2,1)S(1)}, bf16[6,64,256]{2,1,0:T(8,128)(2,1)S(1)}, u32[]{:S(2)}, u32[]{:S(2)}) collective-permute-start(bf16[6,64,256]{2,1,0:T(8,128)(2,1)S(1)} %get-tuple-element.70), channel_id=1, source_target_pairs={{0,4},{4,0},{8,12},{12,8},{16,20},{20,16},{24,28},{28,24},{1,5},{5... | collective-permute-start | bytes 589832 | tf_op jit(solution)/shard_map/ppermute | solution.py:61
  65.9 1.5 %assemble.3 = bf16[6,256,256]{2,1,0:T(8,128)(2,1)} custom-call(s32[3]{0:T(128)S(1)} %pad_add_fusion.place_ref, bf16[6,64,256]{2,1,0:T(8,128)(2,1)S(1)} %get-tuple-element.66.refs_0_, bf16[6,64,256]{2,1,0:T(8,128)(2,1)S(1)} %get-tuple-element.69.refs_1_, bf16[6,64,256]{2,1,0:T(8,128)(2,1)S(1)} %collective-permute-done.30.refs_2_, ...), custom_call_target="tpu_custom_call" | custom-call | tf_op jit(solution)/shard_map/assemble/pallas_call | solution.py:332
  67.3 0.2 while.9
  (23 shorter events, 0.1 us)
Async XLA Ops:
  0.0 1.4 %copy-start.14 = (bf16[6,256,256]{2,1,0:T(8,128)(2,1)S(1)}, bf16[6,256,256]{2,1,0:T(8,128)(2,1)}, u32[]{:S(2)}) copy-start(bf16[6,256,256]{2,1,0:T(8,128)(2,1)} %refs_4_.3) | copy-start | bytes 2359300
  1.5 0.7 %copy-start.19 = (bf16[6,16,64]{2,1,0:T(8,128)(2,1)S(1)}, bf16[6,16,64]{2,1,0:T(8,128)(2,1)}, u32[]{:S(2)}) copy-start(bf16[6,16,64]{2,1,0:T(8,128)(2,1)} %refs_0_.1) | copy-start | bytes 36868
  1.5 4.8 %copy-start.23 = (s32[4]{0:T(128)S(1)}, s32[4]{0:T(128)}, u32[]{:S(2)}) copy-start(s32[4]{0:T(128)} %owner_ref.3) | copy-start | bytes 52
  1.6 4.7 %collective-permute-start.18 = (bf16[22,128,256]{2,1,0:T(8,128)(2,1)S(1)}, bf16[22,128,256]{2,1,0:T(8,128)(2,1)S(1)}, u32[]{:S(2)}, u32[]{:S(2)}) collective-permute-start(bf16[22,128,256]{2,1,0:T(8,128)(2,1)S(1)} %pad_maximum_fusion.3), channel_id=1, source_target_pairs={{0,4},{4,0},{8,12},{12,8},{16,20},{20,16},{24,28},{28,24},{1,5},{5... | collective-permute-start | bytes 4325384 | tf_op jit(solution)/shard_map/ppermute | solution.py:61
  2.2 3.5 %collective-permute-start.19 = (bf16[6,16,64]{2,1,0:T(8,128)(2,1)S(1)}, bf16[6,16,64]{2,1,0:T(8,128)(2,1)S(1)}, u32[]{:S(2)}, u32[]{:S(2)}) collective-permute-start(bf16[6,16,64]{2,1,0:T(8,128)(2,1)S(1)} %copy-done.19), channel_id=1, source_target_pairs={{0,1},{1,0},{2,3},{3,2},{4,5},{5,4},{6,7},{7,6},{8,9},{9,8},{10,11... | collective-permute-start | bytes 36872 | tf_op jit(solution)/shard_map/ppermute | solution.py:358
  5.7 0.6 copy-start.8
  6.3 0.7 %copy-start.9 = (bf16[6,16,64]{2,1,0:T(8,128)(2,1)S(1)}, bf16[6,16,64]{2,1,0:T(8,128)(2,1)}, u32[]{:S(2)}) copy-start(bf16[6,16,64]{2,1,0:T(8,128)(2,1)} %copy-done.8) | copy-start | bytes 36868
  7.1 3.6 %copy-start.10 = (bf16[6,16,64]{2,1,0:T(8,128)(2,1)S(1)}, bf16[6,16,64]{2,1,0:T(8,128)(2,1)}, u32[]{:S(2)}) copy-start(bf16[6,16,64]{2,1,0:T(8,128)(2,1)} %copy-done.8) | copy-start | bytes 36868
  8.6 6.7 %copy-start.11 = (bf16[6,16,64]{2,1,0:T(8,128)(2,1)}, bf16[6,16,64]{2,1,0:T(8,128)(2,1)S(1)}, u32[]{:S(2)}) copy-start(bf16[6,16,64]{2,1,0:T(8,128)(2,1)S(1)} %get-tuple-element.65) | copy-start | bytes 36868
  8.6 23.2 %collective-permute-start.26 = (bf16[16,64,256]{2,1,0:T(8,128)(2,1)S(1)}, bf16[16,64,256]{2,1,0:T(8,128)(2,1)}, u32[]{:S(2)}, u32[]{:S(2)}) collective-permute-start(bf16[16,64,256]{2,1,0:T(8,128)(2,1)S(1)} %get-tuple-element.67.refs_1_), channel_id=1, source_target_pairs={{0,16},{4,20},{8,24},{12,28},{16,0},{20,4},{24,8},{28,12},{1,17},{... | collective-permute-start | bytes 1572872 | tf_op jit(solution)/shard_map/ppermute | solution.py:61
  10.7 3.9 %collective-permute-start.24 = (bf16[2,6,16,64]{3,2,1,0:T(8,128)(2,1)S(1)}, bf16[2,6,16,64]{3,2,1,0:T(8,128)(2,1)S(1)}, u32[]{:S(2)}, u32[]{:S(2)}) collective-permute-start(bf16[2,6,16,64]{3,2,1,0:T(8,128)(2,1)S(1)} %pad_maximum_fusion.5), channel_id=1, source_target_pairs={{0,2},{1,3},{2,0},{3,1},{4,6},{5,7},{6,4},{7,5},{8,10},{9,11},{10,... | collective-permute-start | bytes 73736 | tf_op jit(solution)/shard_map/ppermute | solution.py:363
  13.1 19.9 %collective-permute-start.28 = (bf16[16,64,256]{2,1,0:T(8,128)(2,1)S(1)}, bf16[16,64,256]{2,1,0:T(8,128)(2,1)}, u32[]{:S(2)}, u32[]{:S(2)}) collective-permute-start(bf16[16,64,256]{2,1,0:T(8,128)(2,1)S(1)} %get-tuple-element.68.refs_0_), channel_id=1, source_target_pairs={{0,8},{4,12},{8,0},{12,4},{16,24},{20,28},{24,16},{28,20},{1,9},{5... | collective-permute-start | bytes 1572872 | tf_op jit(solution)/shard_map/ppermute | solution.py:61
  14.6 3.1 %copy-start.22 = (bf16[2,6,16,64]{3,2,1,0:T(8,128)(2,1)}, bf16[2,6,16,64]{3,2,1,0:T(8,128)(2,1)S(1)}, u32[]{:S(2)}) copy-start(bf16[2,6,16,64]{3,2,1,0:T(8,128)(2,1)S(1)} %collective-permute-done.24) | copy-start | bytes 73732
  15.3 7.2 %collective-permute-start.25 = (bf16[4,6,16,64]{3,2,1,0:T(8,128)(2,1)}, bf16[4,6,16,64]{3,2,1,0:T(8,128)(2,1)}, u32[]{:S(2)}, u32[]{:S(2)}) collective-permute-start(bf16[4,6,16,64]{3,2,1,0:T(8,128)(2,1)} %pad_maximum_fusion.4), channel_id=1, source_target_pairs={{0,4},{4,0},{8,12},{12,8},{16,20},{20,16},{24,28},{28,24},{1,5},{5... | collective-permute-start | bytes 147464 | tf_op jit(solution)/shard_map/ppermute | solution.py:61
  20.3 16.0 %collective-permute-start.20 = (bf16[16,64,256]{2,1,0:T(8,128)(2,1)S(1)}, bf16[16,64,256]{2,1,0:T(8,128)(2,1)S(1)}, u32[]{:S(2)}, u32[]{:S(2)}) collective-permute-start(bf16[16,64,256]{2,1,0:T(8,128)(2,1)S(1)} %get-tuple-element.63.refs_1_), channel_id=1, source_target_pairs={{0,16},{4,20},{8,24},{12,28},{16,0},{20,4},{24,8},{28,12},{1,17},{... | collective-permute-start | bytes 1572872 | tf_op jit(solution)/shard_map/ppermute | solution.py:61
  21.0 15.2 %collective-permute-start.22 = (bf16[16,64,256]{2,1,0:T(8,128)(2,1)S(1)}, bf16[16,64,256]{2,1,0:T(8,128)(2,1)S(1)}, u32[]{:S(2)}, u32[]{:S(2)}) collective-permute-start(bf16[16,64,256]{2,1,0:T(8,128)(2,1)S(1)} %get-tuple-element.64.refs_0_), channel_id=1, source_target_pairs={{0,8},{4,12},{8,0},{12,4},{16,24},{20,28},{24,16},{28,20},{1,9},{5... | collective-permute-start | bytes 1572872 | tf_op jit(solution)/shard_map/ppermute | solution.py:61
  32.9 15.0 %collective-permute-start.27 = (bf16[16,64,256]{2,1,0:T(8,128)(2,1)S(1)}, bf16[16,64,256]{2,1,0:T(8,128)(2,1)S(1)}, u32[]{:S(2)}, u32[]{:S(2)}) collective-permute-start(bf16[16,64,256]{2,1,0:T(8,128)(2,1)S(1)} %broadcast_select_fusion.5), channel_id=1, source_target_pairs={{0,8},{4,12},{8,0},{12,4},{16,24},{20,28},{24,16},{28,20},{1,9},{5... | collective-permute-start | bytes 1572872 | tf_op jit(solution)/shard_map/ppermute | solution.py:61
  34.1 3.5 %copy-start.13 = (s32[14]{0:T(128)S(1)}, s32[14]{0:T(128)}, u32[]{:S(2)}) copy-start(s32[14]{0:T(128)} %plan.3.plan_ref) | copy-start | bytes 172
  34.1 13.8 %collective-permute-start.29 = (bf16[16,64,256]{2,1,0:T(8,128)(2,1)S(1)}, bf16[16,64,256]{2,1,0:T(8,128)(2,1)S(1)}, u32[]{:S(2)}, u32[]{:S(2)}) collective-permute-start(bf16[16,64,256]{2,1,0:T(8,128)(2,1)S(1)} %broadcast_select_fusion.4), channel_id=1, source_target_pairs={{0,16},{4,20},{8,24},{12,28},{16,0},{20,4},{24,8},{28,12},{1,17},{... | collective-permute-start | bytes 1572872 | tf_op jit(solution)/shard_map/ppermute | solution.py:61
  36.2 21.9 %collective-permute-start.23 = (bf16[16,64,256]{2,1,0:T(8,128)(2,1)S(1)}, bf16[16,64,256]{2,1,0:T(8,128)(2,1)S(1)}, u32[]{:S(2)}, u32[]{:S(2)}) collective-permute-start(bf16[16,64,256]{2,1,0:T(8,128)(2,1)S(1)} %broadcast_select_fusion.6), channel_id=1, source_target_pairs={{0,16},{4,20},{8,24},{12,28},{16,0},{20,4},{24,8},{28,12},{1,17},{... | collective-permute-start | bytes 1572872 | tf_op jit(solution)/shard_map/ppermute | solution.py:61
  36.4 22.3 %collective-permute-start.21 = (bf16[16,64,256]{2,1,0:T(8,128)(2,1)S(1)}, bf16[16,64,256]{2,1,0:T(8,128)(2,1)S(1)}, u32[]{:S(2)}, u32[]{:S(2)}) collective-permute-start(bf16[16,64,256]{2,1,0:T(8,128)(2,1)S(1)} %broadcast_select_fusion.7), channel_id=1, source_target_pairs={{0,8},{4,12},{8,0},{12,4},{16,24},{20,28},{24,16},{28,20},{1,9},{5... | collective-permute-start | bytes 1572872 | tf_op jit(solution)/shard_map/ppermute | solution.py:61
  43.2 4.8 %copy-start.15 = (bf16[6,256,256]{2,1,0:T(8,128)(2,1)S(1)}, bf16[6,256,256]{2,1,0:T(8,128)(2,1)}, u32[]{:S(2)}) copy-start(bf16[6,256,256]{2,1,0:T(8,128)(2,1)} %refs_4_.3) | copy-start | bytes 2359300
  50.2 15.7 %collective-permute-start.31 = (bf16[6,64,256]{2,1,0:T(8,128)(2,1)S(1)}, bf16[6,64,256]{2,1,0:T(8,128)(2,1)S(1)}, u32[]{:S(2)}, u32[]{:S(2)}) collective-permute-start(bf16[6,64,256]{2,1,0:T(8,128)(2,1)S(1)} %get-tuple-element.71), channel_id=1, source_target_pairs={{0,4},{4,0},{8,12},{12,8},{16,20},{20,16},{24,28},{28,24},{1,5},{5... | collective-permute-start | bytes 589832 | tf_op jit(solution)/shard_map/ppermute | solution.py:61
  60.8 6.6 %copy-start.20 = (bf16[6,16,64]{2,1,0:T(8,128)(2,1)S(1)}, bf16[6,16,64]{2,1,0:T(8,128)(2,1)}, u32[]{:S(2)}) copy-start(bf16[6,16,64]{2,1,0:T(8,128)(2,1)} %refs_0_.1) | copy-start | bytes 36868
  60.8 5.1 %collective-permute-start.30 = (bf16[6,64,256]{2,1,0:T(8,128)(2,1)S(1)}, bf16[6,64,256]{2,1,0:T(8,128)(2,1)S(1)}, u32[]{:S(2)}, u32[]{:S(2)}) collective-permute-start(bf16[6,64,256]{2,1,0:T(8,128)(2,1)S(1)} %get-tuple-element.70), channel_id=1, source_target_pairs={{0,4},{4,0},{8,12},{12,8},{16,20},{20,16},{24,28},{28,24},{1,5},{5... | collective-permute-start | bytes 589832 | tf_op jit(solution)/shard_map/ppermute | solution.py:61

commit v5 on v4

--- a/solution.py
+++ b/solution.py
@@ -61,7 +61,7 @@
     return lax.ppermute(value, "shot", [(i, i ^ bit) for i in range(SQUARE)])
 
 
-def band_kernel(place_ref, taps_ref, band_ref):
+def band_kernel(place_ref, taps_ref, full_ref, band_ref, full_out_ref):
     shots, points, width = taps_ref.shape[1:]
     rows = width // 2
 
@@ -73,24 +73,26 @@
         return carry
 
     lax.fori_loop(0, points, point, 0)
-
-
-def bands_of(blocks, place):
+    full_out_ref[...] = full_ref[...]
+
+
+def bands_of(blocks, place, full):
     panels, shots, points, width = blocks.shape
     height = points * width // 2
+    row = pl.BlockSpec(full.shape, lambda p, place: (0, 0))
     return pl.pallas_call(
         band_kernel,
-        out_shape=jax.ShapeDtypeStruct((panels * height, shots * width), jnp.bfloat16),
+        out_shape=(jax.ShapeDtypeStruct((panels * height, shots * width), jnp.bfloat16), jax.ShapeDtypeStruct(full.shape, full.dtype)),
         grid_spec=pltpu.PrefetchScalarGridSpec(
             num_scalar_prefetch=1,
             grid=(panels,),
-            in_specs=[pl.BlockSpec((1, shots, points, width), lambda p, place: (place[2] ^ p, 0, 0, 0))],
-            out_specs=pl.BlockSpec((height, shots * width), lambda p, place: (p, 0)),
+            in_specs=[pl.BlockSpec((1, shots, points, width), lambda p, place: (place[2] ^ p, 0, 0, 0)), row],
+            out_specs=[pl.BlockSpec((height, shots * width), lambda p, place: (p, 0)), row],
         ),
         compiler_params=pltpu.CompilerParams(vmem_limit_bytes=VMEM_BYTES),
         cost_estimate=pl.CostEstimate(flops=panels * height * shots * width * 8, bytes_accessed=panels * height * shots * width * 2, transcendentals=0),
         name="bands",
-    )(place, blocks)
+    )(place, blocks, full)
 
 
 def source_of(panel, owner_ref, chip):
@@ -115,7 +117,7 @@
     return jnp.where(there == chip, own, jnp.where(there == (chip ^ 1), across, jnp.where(there == (chip ^ 2), down, diagonal)))
 
 
-def plan_kernel(owner_ref, place_ref, plan_ref):
+def plan_kernel(owner_ref, place_ref, plan_ref, full_ref):
     panels = owner_ref.shape[0]
     early, late = jnp.int32(0), jnp.int32(0)
     for entry in range(3 * panels):
@@ -130,66 +132,75 @@
         late = late + jnp.where(met_first, 0, 1)
     plan_ref[3 * panels] = early
     plan_ref[3 * panels + 1] = late
-
-
-def plan_of(owner, place):
+    here = jnp.int32(0)
+    for panel in range(panels):
+        here = here + (owner_ref[panel] // 2 == place_ref[0]).astype(jnp.int32)
+    full_ref[...] = jnp.full(full_ref.shape, jnp.where(here == 2, 1.0, 0.0), jnp.float32)
+
+
+def plan_of(owner, place, length):
     return pl.pallas_call(
         plan_kernel,
-        out_shape=jax.ShapeDtypeStruct((3 * owner.shape[0] + 2,), jnp.int32),
-        in_specs=[pl.BlockSpec(memory_space=pltpu.SMEM)] * 2,
-        out_specs=pl.BlockSpec(memory_space=pltpu.SMEM),
+        out_shape=(jax.ShapeDtypeStruct((3 * owner.shape[0] + 2,), jnp.int32), jax.ShapeDtypeStruct((1, length), jnp.float32)),
+        in_specs=[IN_SMEM] * 2,
+        out_specs=[IN_SMEM, pl.BlockSpec(memory_space=pltpu.VMEM)],
         cost_estimate=NO_COST,
         name="plan",
     )(owner, place)
 
 
-def pick_kernel(passed, before, owner_ref, place_ref, slot_ref, met_ref, *refs):
+def pick_kernel(chunk, owner_ref, place_ref, slot_ref, met_ref, *refs):
     chip, core = place_ref[0], place_ref[1]
     first_owns, second_owns = jnp.bool_(False), jnp.bool_(False)
     for panel in range(owner_ref.shape[0]):
         first_owns = first_owns | (owner_ref[panel] == 2 * chip)
         second_owns = second_owns | (owner_ref[panel] == 2 * chip + 1)
-    outs, sems = refs[passed + before : -1], refs[-1]
+    outs, sems = refs[-3:-1], refs[-1]
     points, rows, _ = outs[0].shape
-    shots = met_ref.shape[0] - points
-    for chunk in range(CHUNKS):
-        here_ref = slot_ref.at[:, pl.ds(pl.multiple_of((core * CHUNKS + chunk) * rows, rows), rows), :]
-        there_ref = met_ref.at[pl.ds(shots, points), pl.ds(chunk * rows, rows), :]
-        for which, mine in enumerate((first_owns == (core == 0), second_owns == (core == 1))):
-            index = 2 * chunk + which
-
-            @pl.when(mine)
-            def _():
-                pltpu.make_async_copy(here_ref, outs[index], sems.at[index]).start()
-
-            @pl.when(jnp.logical_not(mine))
-            def _():
-                pltpu.make_async_copy(there_ref, outs[index], sems.at[index]).start()
-
-    copies = [pltpu.make_async_copy(refs[index], outs[2 * CHUNKS + index], sems.at[2 * CHUNKS + index]) for index in range(passed)]
-    for copy in copies:
-        copy.start()
-    for index in range(2 * CHUNKS):
-        pltpu.make_async_copy(met_ref.at[pl.ds(shots, points), pl.ds(0, rows), :], outs[index], sems.at[index]).wait()
-    for copy in copies:
-        copy.wait()
-
-
-def pick(owner, place, slot, met, passed, before):
-    points, side, length = slot.shape[0], met.shape[1], met.shape[2]
-    outs = [jax.ShapeDtypeStruct((points, side // CHUNKS, length), met.dtype)] * (2 * CHUNKS)
-    outs += [jax.ShapeDtypeStruct(value.shape, value.dtype) for value in passed]
-    outs = pl.pallas_call(
-        functools.partial(pick_kernel, len(passed), len(before)),
-        out_shape=tuple(outs),
-        in_specs=[IN_SMEM] * 2 + [ANYWHERE] * (2 + len(passed) + len(before)),
-        out_specs=[ANYWHERE] * len(outs),
-        scratch_shapes=[pltpu.SemaphoreType.DMA((len(outs),))],
+    here_ref = slot_ref.at[:, pl.ds(pl.multiple_of((core * CHUNKS + chunk) * rows, rows), rows), :]
+    there_ref = met_ref.at[pl.ds(0, points), pl.ds(chunk * rows, rows), :]
+    for index, mine in enumerate((first_owns == (core == 0), second_owns == (core == 1))):
+        @pl.when(mine)
+        def _():
+            pltpu.make_async_copy(here_ref, outs[index], sems.at[index]).start()
+
+        @pl.when(jnp.logical_not(mine))
+        def _():
+            pltpu.make_async_copy(there_ref, outs[index], sems.at[index]).start()
+
+    for index in range(2):
+        pltpu.make_async_copy(there_ref, outs[index], sems.at[index]).wait()
+
+
+def pick(chunk, owner, place, slot, met, before):
+    piece = jax.ShapeDtypeStruct((slot.shape[0], met.shape[1] // CHUNKS, slot.shape[2]), slot.dtype)
+    return pl.pallas_call(
+        functools.partial(pick_kernel, chunk),
+        out_shape=(piece, piece),
+        in_specs=[IN_SMEM] * 2 + [ANYWHERE] * (2 + len(before)),
+        out_specs=[pl.BlockSpec(memory_space=pltpu.VMEM)] * 2,
+        scratch_shapes=[pltpu.SemaphoreType.DMA((2,))],
+        compiler_params=pltpu.CompilerParams(vmem_limit_bytes=2 * SMALL_VMEM_BYTES),
+        cost_estimate=NO_COST,
+        name="pick",
+    )(owner, place, slot, met, *before)
+
+
+def hand_on_kernel(value_ref, *refs):
+    refs[-1][...] = value_ref[...]
+
+
+def hand_on(value, before):
+    whole = pl.BlockSpec(memory_space=pltpu.VMEM)
+    return pl.pallas_call(
+        hand_on_kernel,
+        out_shape=jax.ShapeDtypeStruct(value.shape, value.dtype),
+        in_specs=[whole] + [ANYWHERE] * len(before),
+        out_specs=whole,
         compiler_params=pltpu.CompilerParams(vmem_limit_bytes=SMALL_VMEM_BYTES),
         cost_estimate=NO_COST,
-        name="pick",
-    )(owner, place, slot, met, *passed, *before)
-    return outs[0 : 2 * CHUNKS : 2], outs[1 : 2 * CHUNKS : 2], *outs[2 * CHUNKS :]
+        name="hand_on",
+    )(value, *before)
 
 
 def sum_kernel(last, plan_ref, place_ref, *refs):
@@ -351,23 +362,29 @@
     rows = side // CHUNKS
     taps = primaries.shape[2]
     core = lax.rem(lax.axis_index("shot"), 2)
-    plan = plan_of(panel_owner, place)
+    plan, full = plan_of(panel_owner, place, data.shape[2])
     ring = lax.axis_size("rcv")
-    there = jnp.concatenate([lax.dynamic_slice_in_dim(array, (1 - core) * side, side, axis=1) for array in (data, surface_traces)])
+    there = jnp.concatenate([lax.dynamic_slice_in_dim(array, (1 - core) * side, side, axis=1) for array in (surface_traces, data)])
     met = flip(there, CORE)
+    other_data = met[surface_traces.shape[0] :]
     ahead = lax.ppermute(primaries, "rcv", [(i, i ^ 1) for i in range(ring)])
-    own_a, own_b, primaries = pick(panel_owner, place, surface_traces, met, (primaries,), (ahead,))
+    blocks, bit = jnp.stack([primaries, ahead]), 2
+    blocks = jnp.concatenate([blocks, flip(blocks, CORE)], axis=1)
+    own_a, own_b = [], []
+    for chunk in range(CHUNKS):
+        a, b = pick(chunk, panel_owner, place, surface_traces, met, [ahead] + own_a if own_a else [plan])
+        own_a.append(a)
+        own_b.append(b)
     across, down = [flip(a, ACROSS) for a in own_a], [flip(b, DOWN) for b in own_b]
-    blocks, bit = jnp.stack([primaries, ahead]), 2
+    blocks = hand_on(blocks, [across[0], down[0]])
     while bit < ring:
         blocks = jnp.concatenate([blocks, lax.ppermute(blocks, "rcv", [(i, i ^ bit) for i in range(ring)])])
         bit *= 2
-    blocks = jnp.concatenate([blocks, flip(blocks, CORE)], axis=1)
     blocks = jnp.pad(blocks.astype(jnp.float32), ((0, 0), (0, 0), (0, 0), (0, taps)))
-    bands = bands_of(blocks, place)
-    both = jnp.sum(panel_owner // 2 == place[0]) == 2
-    for_across = [jnp.where(both, own_b[chunk], down[chunk]) for chunk in range(CHUNKS)]
-    for_down = [jnp.where(both, own_a[chunk], across[chunk]) for chunk in range(CHUNKS)]
+    bands, full_later = bands_of(blocks, place, full)
+    rows_full = [full] + [full_later] * (CHUNKS - 1)
+    for_across = [jnp.where(row[0] > 0, own, met) for row, own, met in zip(rows_full, own_b, down)]
+    for_down = [jnp.where(row[0] > 0, own, met) for row, own, met in zip(rows_full, own_a, across)]
 
     kept, returned = [], []
     for chunk in range(CHUNKS):
@@ -376,7 +393,7 @@
         if third:
             second += [flip(second[1], ACROSS), flip(second[0], DOWN)]
         early = sum_of(plan, place, first, bands, panels, taps)
-        mine, others = sum_of(plan, place, second, bands, panels - 1 if third else 2, taps, (chunk, early, data, met))
+        mine, others = sum_of(plan, place, second, bands, panels - 1 if third else 2, taps, (chunk, early, data, other_data))
         kept.append(mine)
         returned.append(flip(others, CORE))
     return assemble(place, kept + returned, data)

time: 68.7 us -> 66.5 us (0.968)
  waiting for transfers between devices: 5.53 us -> 12.7 us
  starting transfers between devices: 23.2 us -> 18.8 us
  other arithmetic: 4.93 us -> 2.44 us
  Pallas kernels: 27 us -> 26.1 us
    ppermute x12, waiting for transfers between devices: 4.07 us -> 10.7 us  [flip(): return lax.ppermute(value, 'shot', [(i, i ^ bit) for i in range(SQUARE)])]
    ppermute x12, starting transfers between devices: 18.5 us -> 15.1 us  [flip(): return lax.ppermute(value, 'shot', [(i, i ^ bit) for i in range(SQUARE)])]
    select_n x4 -> x2, other arithmetic: 2.33 us -> 0.21 us  [exchange(): jnp.where(row[0] > 0, own, met)]
    unnamed x22 -> x14, local copies, waits for them, and re-layouts: 1.91 us -> 0.63 us
    concatenate x1, other arithmetic: 0.13 us -> 1.29 us  [exchange(): jnp.concatenate([lax.dynamic_slice_in_dim(array, (1 - core) * side, side,...]
    ppermute x1, starting transfers between devices: 2.29 us -> 1.3 us  [exchange(): ahead = lax.ppermute(primaries, 'rcv', [(i, i ^ 1) for i in range(ring)])]
    dynamic_slice x2, local copies, waits for them, and re-layouts: 1.39 us -> 2.33 us  [exchange(): lax.dynamic_slice_in_dim(array, (1 - core) * side, side, axis=1)]
    pad x1, other arithmetic: 0.96 us -> 0.05 us  [exchange(): jnp.pad(blocks.astype(jnp.float32), ((0, 0), (0, 0), (0, 0), (0, taps)))]
  transfers between devices with their start and end apart: 14 -> 14, of which waited for: 5 -> 8; matrix products, arithmetic and copies ran while one was open for 7% -> 2% of each run, Pallas kernels for 36% -> 36%
where the time goes in v5:
time: 66.5 us; the launch traced here: 66.1 us
  Pallas kernels  26.1 us (39%)
  starting transfers between devices  18.8 us (28%)
  waiting for transfers between devices  12.7 us (19%)
  local copies, waits for them, and re-layouts  2.98 us (4%)
  between operations  2.84 us (4%)
  other arithmetic  2.44 us (4%)
    ppermute x12, starting transfers between devices, flip(): return lax.ppermute(value, 'shot', [(i, i ^ bit) for i in range(SQUARE)])  15.1 us
    pallas_call x4, Pallas kernels, sum_of(): pl.pallas_call(functools.partial(sum_kernel, last), out_shape=out_shape,...  13.8 us
    ppermute x12, waiting for transfers between devices, flip(): return lax.ppermute(value, 'shot', [(i, i ^ bit) for i in range(SQUARE)])  10.7 us
    pallas_call x1, Pallas kernels, bands_of(): pl.pallas_call(band_kernel, out_shape=(jax.ShapeDtypeStruct((panels * hei...  8.32 us
    ppermute x1, starting transfers between devices, exchange(): lax.ppermute(blocks, 'rcv', [(i, i ^ bit) for i in range(ring)])  2.37 us
    dynamic_slice x2, local copies, waits for them, and re-layouts, exchange(): lax.dynamic_slice_in_dim(array, (1 - core) * side, side, axis=1)  2.33 us
    ppermute x1, waiting for transfers between devices, exchange(): ahead = lax.ppermute(primaries, 'rcv', [(i, i ^ 1) for i in range(ring)])  1.68 us
    pallas_call x1, Pallas kernels, assemble(): pl.pallas_call(assemble_kernel, out_shape=jax.ShapeDtypeStruct(like.shape...  1.45 us
  transfers between devices with their start and end apart: 14, of which 8 were waited for; matrix products, arithmetic and copies ran while one was open for 2% of the time, Pallas kernels for 36%

profile of v5, /device:TPU:1, one launch (start us, length us, event | category | flops | bytes accessed | tf_op | source)
XLA Modules:
  0.0 66.1 jit_solution(11661634094729497892)
XLA Ops:
  0.0 1.0 %constant_dynamic-slice_fusion.2 = bf16[6,128,256]{2,1,0:T(8,128)(2,1)S(1)} fusion(bf16[6,256,256]{2,1,0:T(8,128)(2,1)} %refs_4_.3, s32[]{:T(128)S(6)} %select_n.56), kind=kLoop, calls=%fused_computation.43 | loop fusion | bytes 786436 | tf_op jit(solution)/shard_map/dynamic_slice | solution.py:367
  1.0 1.3 %constant_dynamic-slice_fusion.3 = bf16[16,128,256]{2,1,0:T(8,128)(2,1)S(1)} fusion(bf16[16,256,256]{2,1,0:T(8,128)(2,1)} %slot_ref.3, s32[]{:T(128)S(6)} %select_n.56), kind=kLoop, calls=%fused_computation.44 | loop fusion | bytes 2097156 | tf_op jit(solution)/shard_map/dynamic_slice | solution.py:367
  2.3 0.0 copy-start.11
  2.3 0.0 copy-start.6
  2.4 1.3 %pad_maximum_fusion.3 = bf16[22,128,256]{2,1,0:T(8,128)(2,1)} fusion(bf16[6,128,256]{2,1,0:T(8,128)(2,1)S(1)} %constant_dynamic-slice_fusion.2, bf16[16,128,256]{2,1,0:T(8,128)(2,1)S(1)} %constant_dynamic-slice_fusion.3), kind=kLoop, calls=%fused_computation.16 | loop fusion | flops 720896 | bytes 2883584 | tf_op jit(solution)/shard_map/concatenate | solution.py:367
  3.6 0.1 collective-permute-start.18
  3.7 0.1 pad_add_fusion.place_ref
  3.8 1.2 %plan.3 = (s32[14]{0:T(128)}, f32[1,256]{1,0:T(1,128)}) custom-call(s32[4]{0:T(128)S(1)} %copy-done.11, s32[3]{0:T(128)S(1)} %pad_add_fusion.place_ref), custom_call_target="tpu_custom_call" | custom-call | tf_op jit(solution)/shard_map/plan/pallas_call | solution.py:142
  5.0 2.1 %collective-permute-done.18.met_ref = bf16[22,128,256]{2,1,0:T(8,128)(2,1)S(1)} collective-permute-done((bf16[22,128,256]{2,1,0:T(8,128)(2,1)}, bf16[22,128,256]{2,1,0:T(8,128)(2,1)S(1)}, u32[]{:S(2)}, u32[]{:S(2)}) %collective-permute-start.18) | collective-permute-done | bytes 1441824 | tf_op jit(solution)/shard_map/ppermute | solution.py:61
  7.1 0.6 copy-done.3
  7.7 0.7 pick.6
  8.4 2.4 %collective-permute-start.21 = (bf16[16,64,256]{2,1,0:T(8,128)(2,1)S(1)}, bf16[16,64,256]{2,1,0:T(8,128)(2,1)S(1)}, u32[]{:S(2)}, u32[]{:S(2)}) collective-permute-start(bf16[16,64,256]{2,1,0:T(8,128)(2,1)S(1)} %get-tuple-element.67.refs_0_.refs_1_), channel_id=1, source_target_pairs={{0,8},{4,12},{8,0},{12,4},{16,24},{20,28},{24,16},{28,20},{1,9},{5... | collective-permute-start | bytes 1572872 | tf_op jit(solution)/shard_map/ppermute | solution.py:61
  10.8 1.2 %collective-permute-start.19 = (bf16[16,64,256]{2,1,0:T(8,128)(2,1)S(1)}, bf16[16,64,256]{2,1,0:T(8,128)(2,1)S(1)}, u32[]{:S(2)}, u32[]{:S(2)}) collective-permute-start(bf16[16,64,256]{2,1,0:T(8,128)(2,1)S(1)} %get-tuple-element.66.refs_1_), channel_id=1, source_target_pairs={{0,16},{4,20},{8,24},{12,28},{16,0},{20,4},{24,8},{28,12},{1,17},{... | collective-permute-start | bytes 1572872 | tf_op jit(solution)/shard_map/ppermute | solution.py:61
  12.0 1.3 %collective-permute-start.23 = (bf16[6,16,64]{2,1,0:T(8,128)(2,1)S(1)}, bf16[6,16,64]{2,1,0:T(8,128)(2,1)S(1)}, u32[]{:S(2)}, u32[]{:S(2)}) collective-permute-start(bf16[6,16,64]{2,1,0:T(8,128)(2,1)S(1)} %copy-done.9), channel_id=1, source_target_pairs={{0,1},{1,0},{2,3},{3,2},{4,5},{5,4},{6,7},{7,6},{8,9},{9,8},{10,11... | collective-permute-start | bytes 36872 | tf_op jit(solution)/shard_map/ppermute | solution.py:370
  13.3 1.7 %collective-permute-done.23.refs_0_ = bf16[6,16,64]{2,1,0:T(8,128)(2,1)S(1)} collective-permute-done((bf16[6,16,64]{2,1,0:T(8,128)(2,1)S(1)}, bf16[6,16,64]{2,1,0:T(8,128)(2,1)S(1)}, u32[]{:S(2)}, u32[]{:S(2)}) %collective-permute-start.23) | collective-permute-done | bytes 12320 | tf_op jit(solution)/shard_map/ppermute | solution.py:370
  15.0 1.9 %collective-permute-start.24 = (bf16[2,6,16,64]{3,2,1,0:T(8,128)(2,1)S(1)}, bf16[2,6,16,64]{3,2,1,0:T(8,128)(2,1)S(1)}, u32[]{:S(2)}, u32[]{:S(2)}) collective-permute-start(bf16[2,6,16,64]{3,2,1,0:T(8,128)(2,1)S(1)} %pad_maximum_fusion.5), channel_id=1, source_target_pairs={{0,4},{4,0},{8,12},{12,8},{16,20},{20,16},{24,28},{28,24},{1,5},{5... | collective-permute-start | bytes 73736 | tf_op jit(solution)/shard_map/ppermute | solution.py:61
  16.9 0.9 %collective-permute-done.24 = bf16[2,6,16,64]{3,2,1,0:T(8,128)(2,1)S(1)} collective-permute-done((bf16[2,6,16,64]{3,2,1,0:T(8,128)(2,1)S(1)}, bf16[2,6,16,64]{3,2,1,0:T(8,128)(2,1)S(1)}, u32[]{:S(2)}, u32[]{:S(2)}) %collective-permute-start.24) | collective-permute-done | bytes 24608 | tf_op jit(solution)/shard_map/ppermute | solution.py:61
  17.8 0.7 %pick.7 = (bf16[16,64,256]{2,1,0:T(8,128)(2,1)S(1)}, bf16[16,64,256]{2,1,0:T(8,128)(2,1)S(1)}) custom-call(s32[4]{0:T(128)S(1)} %copy-done.11, s32[3]{0:T(128)S(1)} %pad_add_fusion.place_ref, bf16[16,256,256]{2,1,0:T(8,128)(2,1)S(1)} %copy-done.6, bf16[22,128,256]{2,1,0:T(8,128)(2,1)S(1)} %collective-permute-done.18.met_ref, ...), custom_call_target="tpu_custom_call" | custom-call | tf_op jit(solution)/shard_map/pick/pallas_call | solution.py:177
  18.4 0.3 collective-permute-start.28
  18.7 0.1 collective-permute-start.26
  18.8 3.9 %collective-permute-done.21.refs_0_.refs_2_ = bf16[16,64,256]{2,1,0:T(8,128)(2,1)S(1)} collective-permute-done((bf16[16,64,256]{2,1,0:T(8,128)(2,1)S(1)}, bf16[16,64,256]{2,1,0:T(8,128)(2,1)S(1)}, u32[]{:S(2)}, u32[]{:S(2)}) %collective-permute-start.21) | collective-permute-done | bytes 524320 | tf_op jit(solution)/shard_map/ppermute | solution.py:61
  22.8 0.8 %collective-permute-done.19.refs_1_.refs_3_ = bf16[16,64,256]{2,1,0:T(8,128)(2,1)S(1)} collective-permute-done((bf16[16,64,256]{2,1,0:T(8,128)(2,1)S(1)}, bf16[16,64,256]{2,1,0:T(8,128)(2,1)S(1)}, u32[]{:S(2)}, u32[]{:S(2)}) %collective-permute-start.19) | collective-permute-done | bytes 524320 | tf_op jit(solution)/shard_map/ppermute | solution.py:61
  23.6 2.4 %collective-permute-start.25 = (bf16[2,12,16,64]{3,2,1,0:T(8,128)(2,1)S(1)}, bf16[2,12,16,64]{3,2,1,0:T(8,128)(2,1)S(1)}, u32[]{:S(2)}, u32[]{:S(2)}) collective-permute-start(bf16[2,12,16,64]{3,2,1,0:T(8,128)(2,1)S(1)} %hand_on.3), channel_id=1, source_target_pairs={{0,2},{1,3},{2,0},{3,1},{4,6},{5,7},{6,4},{7,5},{8,10},{9,11},{10,... | collective-permute-start | bytes 147464 | tf_op jit(solution)/shard_map/ppermute | solution.py:381
  26.0 0.1 broadcast_select_fusion.6
  26.1 0.4 collective-permute-start.20
  26.5 1.2 %collective-permute-start.22 = (bf16[16,64,256]{2,1,0:T(8,128)(2,1)S(1)}, bf16[16,64,256]{2,1,0:T(8,128)(2,1)S(1)}, u32[]{:S(2)}, u32[]{:S(2)}) collective-permute-start(bf16[16,64,256]{2,1,0:T(8,128)(2,1)S(1)} %get-tuple-element.101), channel_id=1, source_target_pairs={{0,16},{4,20},{8,24},{12,28},{16,0},{20,4},{24,8},{28,12},{1,17},{... | collective-permute-start | bytes 1572872 | tf_op jit(solution)/shard_map/ppermute | solution.py:61
  27.7 0.3 collective-permute-done.25
  28.0 0.1 fusion.7.taps_ref
  28.1 8.3 %bands.3 = (bf16[4096,1536]{1,0:T(8,128)(2,1)S(1)}, f32[1,256]{1,0:T(1,128)S(1)}) custom-call(s32[3]{0:T(128)S(1)} %pad_add_fusion.place_ref, f32[4,12,16,128]{3,2,1,0:T(8,128)S(1)} %fusion.7.taps_ref, f32[1,256]{1,0:T(1,128)S(1)} %copy-done.5), custom_call_target="tpu_custom_call" | custom-call | flops 50331648 | bytes 12582912 | tf_op jit(solution)/shard_map/bands/pallas_call | solution.py:83
  36.5 0.0 collective-permute-done.26.refs_3_
  36.5 0.1 broadcast_select_fusion.4
  36.6 1.5 %collective-permute-start.27 = (bf16[16,64,256]{2,1,0:T(8,128)(2,1)S(1)}, bf16[16,64,256]{2,1,0:T(8,128)(2,1)S(1)}, u32[]{:S(2)}, u32[]{:S(2)}) collective-permute-start(bf16[16,64,256]{2,1,0:T(8,128)(2,1)S(1)} %get-tuple-element.100), channel_id=1, source_target_pairs={{0,8},{4,12},{8,0},{12,4},{16,24},{20,28},{24,16},{28,20},{1,9},{5... | collective-permute-start | bytes 1572872 | tf_op jit(solution)/shard_map/ppermute | solution.py:61
  38.1 0.1 collective-permute-start.29
  38.2 4.7 %early_sum.6.refs_3_ = f32[12,64,256]{2,1,0:T(8,128)S(1)} custom-call(s32[14]{0:T(128)S(1)} %copy-done.4, s32[3]{0:T(128)S(1)} %pad_add_fusion.place_ref, bf16[16,64,256]{2,1,0:T(8,128)(2,1)S(1)} %get-tuple-element.67.refs_0_.refs_1_, bf16[16,64,256]{2,1,0:T(8,128)(2,1)S(1)} %get-tuple-element.66.refs_1_, ...), custom_call_target="tpu_custom_call" | custom-call | flops 3221225472 | bytes 12582912 | tf_op jit(solution)/shard_map/early_sum/pallas_call | solution.py:307
  43.0 0.0 copy-start.7
  43.0 4.7 %early_sum.7.refs_3_ = f32[12,64,256]{2,1,0:T(8,128)S(1)} custom-call(s32[14]{0:T(128)S(1)} %copy-done.4, s32[3]{0:T(128)S(1)} %pad_add_fusion.place_ref, bf16[16,64,256]{2,1,0:T(8,128)(2,1)S(1)} %get-tuple-element.72.refs_0_, bf16[16,64,256]{2,1,0:T(8,128)(2,1)S(1)} %get-tuple-element.71.refs_1_, bf16[16,64,256]{2,1,0:T(8,128)(2,1)S(1)} %collective-permute-done.28.refs_2_, ...), custom_call_target="tpu_custom_call" | custom-call | flops 3221225472 | bytes 12582912 | tf_op jit(solution)/shard_map/early_sum/pallas_call | solution.py:307
  47.7 0.0 collective-permute-done.20.refs_0_
  47.7 2.2 %residual.6 = (bf16[6,64,256]{2,1,0:T(8,128)(2,1)S(1)}, bf16[6,64,256]{2,1,0:T(8,128)(2,1)S(1)}) custom-call(s32[14]{0:T(128)S(1)} %copy-done.4, s32[3]{0:T(128)S(1)} %pad_add_fusion.place_ref, bf16[16,64,256]{2,1,0:T(8,128)(2,1)S(1)} %collective-permute-done.20.refs_0_, bf16[16,64,256]{2,1,0:T(8,128)(2,1)S(1)} %collective-permute-done.22.refs_1_, ...), custom_call_target="tpu_custom_call" | custom-call | flops 1610612736 | bytes 6291456 | tf_op jit(solution)/shard_map/residual/pallas_call | solution.py:307
  49.9 4.4 %collective-permute-start.30 = (bf16[6,64,256]{2,1,0:T(8,128)(2,1)S(1)}, bf16[6,64,256]{2,1,0:T(8,128)(2,1)S(1)}, u32[]{:S(2)}, u32[]{:S(2)}) collective-permute-start(bf16[6,64,256]{2,1,0:T(8,128)(2,1)S(1)} %get-tuple-element.74), channel_id=1, source_target_pairs={{0,4},{4,0},{8,12},{12,8},{16,20},{20,16},{24,28},{28,24},{1,5},{5... | collective-permute-start | bytes 589832 | tf_op jit(solution)/shard_map/ppermute | solution.py:61
  54.3 2.2 %collective-permute-done.27.refs_0_ = bf16[16,64,256]{2,1,0:T(8,128)(2,1)S(1)} collective-permute-done((bf16[16,64,256]{2,1,0:T(8,128)(2,1)S(1)}, bf16[16,64,256]{2,1,0:T(8,128)(2,1)S(1)}, u32[]{:S(2)}, u32[]{:S(2)}) %collective-permute-start.27) | collective-permute-done | bytes 524320 | tf_op jit(solution)/shard_map/ppermute | solution.py:61
  56.5 0.8 %collective-permute-done.29.refs_1_ = bf16[16,64,256]{2,1,0:T(8,128)(2,1)S(1)} collective-permute-done((bf16[16,64,256]{2,1,0:T(8,128)(2,1)S(1)}, bf16[16,64,256]{2,1,0:T(8,128)(2,1)S(1)}, u32[]{:S(2)}, u32[]{:S(2)}) %collective-permute-start.29) | collective-permute-done | bytes 524320 | tf_op jit(solution)/shard_map/ppermute | solution.py:61
  57.3 2.2 %residual.7 = (bf16[6,64,256]{2,1,0:T(8,128)(2,1)S(1)}, bf16[6,64,256]{2,1,0:T(8,128)(2,1)S(1)}) custom-call(s32[14]{0:T(128)S(1)} %copy-done.4, s32[3]{0:T(128)S(1)} %pad_add_fusion.place_ref, bf16[16,64,256]{2,1,0:T(8,128)(2,1)S(1)} %collective-permute-done.27.refs_0_, bf16[16,64,256]{2,1,0:T(8,128)(2,1)S(1)} %collective-permute-done.29.refs_1_, ...), custom_call_target="tpu_custom_call" | custom-call | flops 1610612736 | bytes 6291456 | tf_op jit(solution)/shard_map/residual/pallas_call | solution.py:307
  59.5 1.6 %collective-permute-start.31 = (bf16[6,64,256]{2,1,0:T(8,128)(2,1)S(1)}, bf16[6,64,256]{2,1,0:T(8,128)(2,1)S(1)}, u32[]{:S(2)}, u32[]{:S(2)}) collective-permute-start(bf16[6,64,256]{2,1,0:T(8,128)(2,1)S(1)} %get-tuple-element.75), channel_id=1, source_target_pairs={{0,4},{4,0},{8,12},{12,8},{16,20},{20,16},{24,28},{28,24},{1,5},{5... | collective-permute-start | bytes 589832 | tf_op jit(solution)/shard_map/ppermute | solution.py:61
  61.0 0.7 %fusion.11 = (s32[]{:T(128)}, s32[]{:T(128)}, s32[]{:T(128)}, s32[]{:T(128)}) fusion(s32[4]{0:T(128)S(1)} %copy-done.11), kind=kLoop, calls=%fused_computation.41 | loop fusion | flops 104 | bytes 32 | tf_op jit(solution)/shard_map/reduce_sum | solution.py:405
  64.3 0.0 collective-permute-done.30.refs_2_
  64.3 0.0 collective-permute-done.31.refs_3_
  64.3 1.5 %assemble.3 = bf16[6,256,256]{2,1,0:T(8,128)(2,1)} custom-call(s32[3]{0:T(128)S(1)} %pad_add_fusion.place_ref, bf16[6,64,256]{2,1,0:T(8,128)(2,1)S(1)} %get-tuple-element.69.refs_0_, bf16[6,64,256]{2,1,0:T(8,128)(2,1)S(1)} %get-tuple-element.73.refs_1_, bf16[6,64,256]{2,1,0:T(8,128)(2,1)S(1)} %collective-permute-done.30.refs_2_, ...), custom_call_target="tpu_custom_call" | custom-call | tf_op jit(solution)/shard_map/assemble/pallas_call | solution.py:343
  65.7 0.2 while.9
  (18 shorter events, 0.1 us)
Async XLA Ops:
  2.3 1.4 %copy-start.11 = (s32[4]{0:T(128)S(1)}, s32[4]{0:T(128)}, u32[]{:S(2)}) copy-start(s32[4]{0:T(128)} %owner_ref.5) | copy-start | bytes 52
  2.3 4.7 %copy-start.6 = (bf16[16,256,256]{2,1,0:T(8,128)(2,1)S(1)}, bf16[16,256,256]{2,1,0:T(8,128)(2,1)}, u32[]{:S(2)}) copy-start(bf16[16,256,256]{2,1,0:T(8,128)(2,1)} %slot_ref.3) | copy-start | bytes 6291460
  3.6 3.4 %collective-permute-start.18 = (bf16[22,128,256]{2,1,0:T(8,128)(2,1)}, bf16[22,128,256]{2,1,0:T(8,128)(2,1)S(1)}, u32[]{:S(2)}, u32[]{:S(2)}) collective-permute-start(bf16[22,128,256]{2,1,0:T(8,128)(2,1)} %pad_maximum_fusion.3), channel_id=1, source_target_pairs={{0,4},{4,0},{8,12},{12,8},{16,20},{20,16},{24,28},{28,24},{1,5},{5... | collective-permute-start | bytes 4325384 | tf_op jit(solution)/shard_map/ppermute | solution.py:61
  7.1 0.6 copy-start.3
  7.7 4.3 %copy-start.9 = (bf16[6,16,64]{2,1,0:T(8,128)(2,1)S(1)}, bf16[6,16,64]{2,1,0:T(8,128)(2,1)}, u32[]{:S(2)}) copy-start(bf16[6,16,64]{2,1,0:T(8,128)(2,1)} %param.8) | copy-start | bytes 36868
  7.7 9.2 %copy-start.5 = (f32[1,256]{1,0:T(1,128)S(1)}, f32[1,256]{1,0:T(1,128)}, u32[]{:S(2)}) copy-start(f32[1,256]{1,0:T(1,128)} %get-tuple-element.65.full_ref) | copy-start | bytes 3076
  8.4 14.4 %collective-permute-start.21 = (bf16[16,64,256]{2,1,0:T(8,128)(2,1)S(1)}, bf16[16,64,256]{2,1,0:T(8,128)(2,1)S(1)}, u32[]{:S(2)}, u32[]{:S(2)}) collective-permute-start(bf16[16,64,256]{2,1,0:T(8,128)(2,1)S(1)} %get-tuple-element.67.refs_0_.refs_1_), channel_id=1, source_target_pairs={{0,8},{4,12},{8,0},{12,4},{16,24},{20,28},{24,16},{28,20},{1,9},{5... | collective-permute-start | bytes 1572872 | tf_op jit(solution)/shard_map/ppermute | solution.py:61
  10.8 12.8 %collective-permute-start.19 = (bf16[16,64,256]{2,1,0:T(8,128)(2,1)S(1)}, bf16[16,64,256]{2,1,0:T(8,128)(2,1)S(1)}, u32[]{:S(2)}, u32[]{:S(2)}) collective-permute-start(bf16[16,64,256]{2,1,0:T(8,128)(2,1)S(1)} %get-tuple-element.66.refs_1_), channel_id=1, source_target_pairs={{0,16},{4,20},{8,24},{12,28},{16,0},{20,4},{24,8},{28,12},{1,17},{... | collective-permute-start | bytes 1572872 | tf_op jit(solution)/shard_map/ppermute | solution.py:61
  12.0 3.0 %collective-permute-start.23 = (bf16[6,16,64]{2,1,0:T(8,128)(2,1)S(1)}, bf16[6,16,64]{2,1,0:T(8,128)(2,1)S(1)}, u32[]{:S(2)}, u32[]{:S(2)}) collective-permute-start(bf16[6,16,64]{2,1,0:T(8,128)(2,1)S(1)} %copy-done.9), channel_id=1, source_target_pairs={{0,1},{1,0},{2,3},{3,2},{4,5},{5,4},{6,7},{7,6},{8,9},{9,8},{10,11... | collective-permute-start | bytes 36872 | tf_op jit(solution)/shard_map/ppermute | solution.py:370
  15.0 2.7 %collective-permute-start.24 = (bf16[2,6,16,64]{3,2,1,0:T(8,128)(2,1)S(1)}, bf16[2,6,16,64]{3,2,1,0:T(8,128)(2,1)S(1)}, u32[]{:S(2)}, u32[]{:S(2)}) collective-permute-start(bf16[2,6,16,64]{3,2,1,0:T(8,128)(2,1)S(1)} %pad_maximum_fusion.5), channel_id=1, source_target_pairs={{0,4},{4,0},{8,12},{12,8},{16,20},{20,16},{24,28},{28,24},{1,5},{5... | collective-permute-start | bytes 73736 | tf_op jit(solution)/shard_map/ppermute | solution.py:61
  18.4 18.0 %collective-permute-start.28 = (bf16[16,64,256]{2,1,0:T(8,128)(2,1)S(1)}, bf16[16,64,256]{2,1,0:T(8,128)(2,1)S(1)}, u32[]{:S(2)}, u32[]{:S(2)}) collective-permute-start(bf16[16,64,256]{2,1,0:T(8,128)(2,1)S(1)} %get-tuple-element.72.refs_0_), channel_id=1, source_target_pairs={{0,8},{4,12},{8,0},{12,4},{16,24},{20,28},{24,16},{28,20},{1,9},{5... | collective-permute-start | bytes 1572872 | tf_op jit(solution)/shard_map/ppermute | solution.py:61
  18.7 17.7 %collective-permute-start.26 = (bf16[16,64,256]{2,1,0:T(8,128)(2,1)S(1)}, bf16[16,64,256]{2,1,0:T(8,128)(2,1)S(1)}, u32[]{:S(2)}, u32[]{:S(2)}) collective-permute-start(bf16[16,64,256]{2,1,0:T(8,128)(2,1)S(1)} %get-tuple-element.71.refs_1_), channel_id=1, source_target_pairs={{0,16},{4,20},{8,24},{12,28},{16,0},{20,4},{24,8},{28,12},{1,17},{... | collective-permute-start | bytes 1572872 | tf_op jit(solution)/shard_map/ppermute | solution.py:61
  23.6 4.4 %collective-permute-start.25 = (bf16[2,12,16,64]{3,2,1,0:T(8,128)(2,1)S(1)}, bf16[2,12,16,64]{3,2,1,0:T(8,128)(2,1)S(1)}, u32[]{:S(2)}, u32[]{:S(2)}) collective-permute-start(bf16[2,12,16,64]{3,2,1,0:T(8,128)(2,1)S(1)} %hand_on.3), channel_id=1, source_target_pairs={{0,2},{1,3},{2,0},{3,1},{4,6},{5,7},{6,4},{7,5},{8,10},{9,11},{10,... | collective-permute-start | bytes 147464 | tf_op jit(solution)/shard_map/ppermute | solution.py:381
  26.1 21.6 %collective-permute-start.20 = (bf16[16,64,256]{2,1,0:T(8,128)(2,1)S(1)}, bf16[16,64,256]{2,1,0:T(8,128)(2,1)S(1)}, u32[]{:S(2)}, u32[]{:S(2)}) collective-permute-start(bf16[16,64,256]{2,1,0:T(8,128)(2,1)S(1)} %get-tuple-element.102), channel_id=1, source_target_pairs={{0,8},{4,12},{8,0},{12,4},{16,24},{20,28},{24,16},{28,20},{1,9},{5... | collective-permute-start | bytes 1572872 | tf_op jit(solution)/shard_map/ppermute | solution.py:61
  26.5 21.3 %collective-permute-start.22 = (bf16[16,64,256]{2,1,0:T(8,128)(2,1)S(1)}, bf16[16,64,256]{2,1,0:T(8,128)(2,1)S(1)}, u32[]{:S(2)}, u32[]{:S(2)}) collective-permute-start(bf16[16,64,256]{2,1,0:T(8,128)(2,1)S(1)} %get-tuple-element.101), channel_id=1, source_target_pairs={{0,16},{4,20},{8,24},{12,28},{16,0},{20,4},{24,8},{28,12},{1,17},{... | collective-permute-start | bytes 1572872 | tf_op jit(solution)/shard_map/ppermute | solution.py:61
  36.5 1.8 %copy-start.4 = (s32[14]{0:T(128)S(1)}, s32[14]{0:T(128)}, u32[]{:S(2)}) copy-start(s32[14]{0:T(128)} %get-tuple-element.64.refs_0_.plan_ref) | copy-start | bytes 172
  36.6 19.9 %collective-permute-start.27 = (bf16[16,64,256]{2,1,0:T(8,128)(2,1)S(1)}, bf16[16,64,256]{2,1,0:T(8,128)(2,1)S(1)}, u32[]{:S(2)}, u32[]{:S(2)}) collective-permute-start(bf16[16,64,256]{2,1,0:T(8,128)(2,1)S(1)} %get-tuple-element.100), channel_id=1, source_target_pairs={{0,8},{4,12},{8,0},{12,4},{16,24},{20,28},{24,16},{28,20},{1,9},{5... | collective-permute-start | bytes 1572872 | tf_op jit(solution)/shard_map/ppermute | solution.py:61
  38.1 19.2 %collective-permute-start.29 = (bf16[16,64,256]{2,1,0:T(8,128)(2,1)S(1)}, bf16[16,64,256]{2,1,0:T(8,128)(2,1)S(1)}, u32[]{:S(2)}, u32[]{:S(2)}) collective-permute-start(bf16[16,64,256]{2,1,0:T(8,128)(2,1)S(1)} %get-tuple-element.99), channel_id=1, source_target_pairs={{0,16},{4,20},{8,24},{12,28},{16,0},{20,4},{24,8},{28,12},{1,17},{... | collective-permute-start | bytes 1572872 | tf_op jit(solution)/shard_map/ppermute | solution.py:61
  43.0 4.8 %copy-start.7 = (bf16[6,256,256]{2,1,0:T(8,128)(2,1)S(1)}, bf16[6,256,256]{2,1,0:T(8,128)(2,1)}, u32[]{:S(2)}) copy-start(bf16[6,256,256]{2,1,0:T(8,128)(2,1)} %refs_4_.3) | copy-start | bytes 2359300
  49.9 14.3 %collective-permute-start.30 = (bf16[6,64,256]{2,1,0:T(8,128)(2,1)S(1)}, bf16[6,64,256]{2,1,0:T(8,128)(2,1)S(1)}, u32[]{:S(2)}, u32[]{:S(2)}) collective-permute-start(bf16[6,64,256]{2,1,0:T(8,128)(2,1)S(1)} %get-tuple-element.74), channel_id=1, source_target_pairs={{0,4},{4,0},{8,12},{12,8},{16,20},{20,16},{24,28},{28,24},{1,5},{5... | collective-permute-start | bytes 589832 | tf_op jit(solution)/shard_map/ppermute | solution.py:61
  59.5 4.8 %collective-permute-start.31 = (bf16[6,64,256]{2,1,0:T(8,128)(2,1)S(1)}, bf16[6,64,256]{2,1,0:T(8,128)(2,1)S(1)}, u32[]{:S(2)}, u32[]{:S(2)}) collective-permute-start(bf16[6,64,256]{2,1,0:T(8,128)(2,1)S(1)} %get-tuple-element.75), channel_id=1, source_target_pairs={{0,4},{4,0},{8,12},{12,8},{16,20},{20,16},{24,28},{28,24},{1,5},{5... | collective-permute-start | bytes 589832 | tf_op jit(solution)/shard_map/ppermute | solution.py:61

commit v6 on v5

--- a/solution.py
+++ b/solution.py
@@ -117,7 +117,7 @@
     return jnp.where(there == chip, own, jnp.where(there == (chip ^ 1), across, jnp.where(there == (chip ^ 2), down, diagonal)))
 
 
-def plan_kernel(owner_ref, place_ref, plan_ref, full_ref):
+def write_plan(owner_ref, place_ref, plan_ref):
     panels = owner_ref.shape[0]
     early, late = jnp.int32(0), jnp.int32(0)
     for entry in range(3 * panels):
@@ -132,21 +132,6 @@
         late = late + jnp.where(met_first, 0, 1)
     plan_ref[3 * panels] = early
     plan_ref[3 * panels + 1] = late
-    here = jnp.int32(0)
-    for panel in range(panels):
-        here = here + (owner_ref[panel] // 2 == place_ref[0]).astype(jnp.int32)
-    full_ref[...] = jnp.full(full_ref.shape, jnp.where(here == 2, 1.0, 0.0), jnp.float32)
-
-
-def plan_of(owner, place, length):
-    return pl.pallas_call(
-        plan_kernel,
-        out_shape=(jax.ShapeDtypeStruct((3 * owner.shape[0] + 2,), jnp.int32), jax.ShapeDtypeStruct((1, length), jnp.float32)),
-        in_specs=[IN_SMEM] * 2,
-        out_specs=[IN_SMEM, pl.BlockSpec(memory_space=pltpu.VMEM)],
-        cost_estimate=NO_COST,
-        name="plan",
-    )(owner, place)
 
 
 def pick_kernel(chunk, owner_ref, place_ref, slot_ref, met_ref, *refs):
@@ -155,10 +140,11 @@
     for panel in range(owner_ref.shape[0]):
         first_owns = first_owns | (owner_ref[panel] == 2 * chip)
         second_owns = second_owns | (owner_ref[panel] == 2 * chip + 1)
-    outs, sems = refs[-3:-1], refs[-1]
-    points, rows, _ = outs[0].shape
+    *others, a_ref, b_ref, sems = refs
+    outs = (a_ref, b_ref)
+    points, rows, _ = a_ref.shape
     here_ref = slot_ref.at[:, pl.ds(pl.multiple_of((core * CHUNKS + chunk) * rows, rows), rows), :]
-    there_ref = met_ref.at[pl.ds(0, points), pl.ds(chunk * rows, rows), :]
+    there_ref = met_ref.at[:, pl.ds(chunk * rows, rows), :]
     for index, mine in enumerate((first_owns == (core == 0), second_owns == (core == 1))):
         @pl.when(mine)
         def _():
@@ -168,22 +154,53 @@
         def _():
             pltpu.make_async_copy(there_ref, outs[index], sems.at[index]).start()
 
+    if chunk == 1:
+        plan_ref, full_ref = others[-2:]
+        write_plan(owner_ref, place_ref, plan_ref)
+        full_ref[...] = jnp.full(full_ref.shape, jnp.where(first_owns & second_owns, 1.0, 0.0), jnp.float32)
     for index in range(2):
         pltpu.make_async_copy(there_ref, outs[index], sems.at[index]).wait()
 
 
 def pick(chunk, owner, place, slot, met, before):
-    piece = jax.ShapeDtypeStruct((slot.shape[0], met.shape[1] // CHUNKS, slot.shape[2]), slot.dtype)
+    points, length = slot.shape[0], slot.shape[2]
+    in_vmem = pl.BlockSpec(memory_space=pltpu.VMEM)
+    outs = [jax.ShapeDtypeStruct((points, met.shape[1] // CHUNKS, length), slot.dtype)] * 2
+    specs = [in_vmem] * 2
+    if chunk == 1:
+        outs = [jax.ShapeDtypeStruct((3 * owner.shape[0] + 2,), jnp.int32), jax.ShapeDtypeStruct((1, length), jnp.float32)] + outs
+        specs = [IN_SMEM, in_vmem] + specs
     return pl.pallas_call(
         functools.partial(pick_kernel, chunk),
-        out_shape=(piece, piece),
+        out_shape=tuple(outs),
         in_specs=[IN_SMEM] * 2 + [ANYWHERE] * (2 + len(before)),
-        out_specs=[pl.BlockSpec(memory_space=pltpu.VMEM)] * 2,
+        out_specs=specs,
         scratch_shapes=[pltpu.SemaphoreType.DMA((2,))],
         compiler_params=pltpu.CompilerParams(vmem_limit_bytes=2 * SMALL_VMEM_BYTES),
         cost_estimate=NO_COST,
         name="pick",
     )(owner, place, slot, met, *before)
+
+
+def cut_kernel(place_ref, array_ref, *refs):
+    refs[-1][...] = array_ref[...]
+
+
+def cut(array, place, before):
+    block = (array.shape[0], array.shape[1] // 2, array.shape[2])
+    return pl.pallas_call(
+        cut_kernel,
+        out_shape=jax.ShapeDtypeStruct(block, array.dtype),
+        grid_spec=pltpu.PrefetchScalarGridSpec(
+            num_scalar_prefetch=1,
+            grid=(1,),
+            in_specs=[pl.BlockSpec(block, lambda step, place: (0, 1 - place[1], 0))] + [ANYWHERE] * len(before),
+            out_specs=pl.BlockSpec(block, lambda step, place: (0, 0, 0)),
+        ),
+        compiler_params=pltpu.CompilerParams(vmem_limit_bytes=2 * SMALL_VMEM_BYTES),
+        cost_estimate=NO_COST,
+        name="cut",
+    )(place, array, *before)
 
 
 def hand_on_kernel(value_ref, *refs):
@@ -325,13 +342,14 @@
     )(plan, place, *operands)
 
 
-def assemble_kernel(place_ref, *refs):
-    pieces, out_ref, sems = refs[:-2], refs[-2], refs[-1]
+def assemble_kernel(at, place_ref, *refs):
+    pieces, out_ref, sems = refs[: len(at)], refs[-2], refs[-1]
     rows = pieces[0].shape[1]
     copies = []
     for index, piece in enumerate(pieces):
-        side = place_ref[1] if index < CHUNKS else 1 - place_ref[1]
-        start = pl.multiple_of((side * CHUNKS + index % CHUNKS) * rows, rows)
+        swapped, chunk = at[index]
+        side = 1 - place_ref[1] if swapped else place_ref[1]
+        start = pl.multiple_of((side * CHUNKS + chunk) * rows, rows)
         copies.append(pltpu.make_async_copy(piece, out_ref.at[:, pl.ds(start, rows), :], sems.at[index]))
     for copy in copies:
         copy.start()
@@ -339,44 +357,46 @@
         copy.wait()
 
 
-def assemble(place, pieces, like):
-    return pl.pallas_call(
-        assemble_kernel,
-        out_shape=jax.ShapeDtypeStruct(like.shape, like.dtype),
-        in_specs=[IN_SMEM] + [pl.BlockSpec(memory_space=pl.ANY)] * len(pieces),
+def assemble(place, pieces, at, like, onto=None):
+    given = () if onto is None else (onto,)
+    return pl.pallas_call(
+        functools.partial(assemble_kernel, at),
+        out_shape=pltpu.HBM(like.shape, like.dtype),
+        in_specs=[IN_SMEM] + [ANYWHERE] * (len(pieces) + len(given)),
         out_specs=ANYWHERE,
         scratch_shapes=[pltpu.SemaphoreType.DMA((len(pieces),))],
+        input_output_aliases={1 + len(pieces): 0} if given else {},
         compiler_params=pltpu.CompilerParams(vmem_limit_bytes=SMALL_VMEM_BYTES),
         cost_estimate=NO_COST,
         name="assemble",
-    )(place, *pieces)
+    )(place, *pieces, *given)
 
 
 def any_of(flags):
     return functools.reduce(jnp.logical_or, flags)
 
 
-def exchange(data, surface_traces, primaries, panel_owner, place, third):
+def exchange(data, surface_traces, primaries, panel_owner, place, flag, third):
     panels = panel_owner.shape[0]
     side = data.shape[1] // 2
     rows = side // CHUNKS
     taps = primaries.shape[2]
     core = lax.rem(lax.axis_index("shot"), 2)
-    plan, full = plan_of(panel_owner, place, data.shape[2])
     ring = lax.axis_size("rcv")
-    there = jnp.concatenate([lax.dynamic_slice_in_dim(array, (1 - core) * side, side, axis=1) for array in (surface_traces, data)])
-    met = flip(there, CORE)
-    other_data = met[surface_traces.shape[0] :]
+    met = flip(lax.dynamic_slice_in_dim(surface_traces, (1 - core) * side, side, axis=1), CORE)
     ahead = lax.ppermute(primaries, "rcv", [(i, i ^ 1) for i in range(ring)])
     blocks, bit = jnp.stack([primaries, ahead]), 2
     blocks = jnp.concatenate([blocks, flip(blocks, CORE)], axis=1)
     own_a, own_b = [], []
     for chunk in range(CHUNKS):
-        a, b = pick(chunk, panel_owner, place, surface_traces, met, [ahead] + own_a if own_a else [plan])
+        *extra, a, b = pick(chunk, panel_owner, place, surface_traces, met, [ahead, flag, own_a[-1]] if own_a else [])
+        if extra:
+            plan, full = extra
         own_a.append(a)
         own_b.append(b)
+    other_data = flip(cut(data, place, [own_a[-1]]), CORE)
     across, down = [flip(a, ACROSS) for a in own_a], [flip(b, DOWN) for b in own_b]
-    blocks = hand_on(blocks, [across[0], down[0]])
+    blocks = hand_on(blocks, [across[0], down[0], other_data])
     while bit < ring:
         blocks = jnp.concatenate([blocks, lax.ppermute(blocks, "rcv", [(i, i ^ bit) for i in range(ring)])])
         bit *= 2
@@ -396,7 +416,9 @@
         mine, others = sum_of(plan, place, second, bands, panels - 1 if third else 2, taps, (chunk, early, data, other_data))
         kept.append(mine)
         returned.append(flip(others, CORE))
-    return assemble(place, kept + returned, data)
+    places = [(False, chunk) for chunk in range(CHUNKS)] + [(True, chunk) for chunk in range(CHUNKS)]
+    residual = assemble(place, (kept + returned)[:-1], places[:-1], data)
+    return assemble(place, returned[-1:], places[-1:], data, residual)
 
 
 def square_shards(data, surface_traces, primaries, panel_owner):
@@ -404,7 +426,7 @@
     place = jnp.stack([me // 2, me % 2, lax.axis_index("rcv")]).astype(jnp.int32)
     holds_two = [jnp.sum(panel_owner // 2 == other) == 2 for other in range(SQUARE // 2)]
     neighbours_full = any_of([holds_two[at] & holds_two[at ^ bit] for at in range(SQUARE // 2) for bit in (1, 2) if at < at ^ bit])
-    arguments = (data, surface_traces, primaries, panel_owner, place)
+    arguments = (data, surface_traces, primaries, panel_owner, place, neighbours_full.astype(jnp.float32)[None])
     residual = exchange(*arguments, False)
     return lax.while_loop(lambda state: state[0], lambda state: (jnp.bool_(False), exchange(*arguments, True)), (neighbours_full, residual))[1]
 

time: 66.5 us -> 62.8 us (0.944); the launches traced: 66.1 us -> 61.6 us
  starting transfers between devices: 18.8 us -> 14.3 us
  Pallas kernels: 26.1 us -> 29.5 us
  local copies, waits for them, and re-layouts: 2.98 us -> 1.33 us
  other arithmetic: 2.44 us -> 1.23 us
    ppermute x12 -> x13, starting transfers between devices: 15.1 us -> 10.6 us  [flip(): return lax.ppermute(value, 'shot', [(i, i ^ bit) for i in range(SQUARE)])]
    pallas_call x4 -> x5, Pallas kernels: 3.99 us -> 7.09 us  [the longest x2 3.91 us: pick(): pl.pallas_call(functools.partial(pick_kernel, chunk), out_shape=tuple(out...]
    ppermute x1, waiting for transfers between devices: 0.33 us -> 3.19 us  [exchange(): lax.ppermute(blocks, 'rcv', [(i, i ^ bit) for i in range(ring)])]
    ppermute x12 -> x13, waiting for transfers between devices: 10.7 us -> 8.99 us  [flip(): return lax.ppermute(value, 'shot', [(i, i ^ bit) for i in range(SQUARE)])]
    ppermute x1, waiting for transfers between devices: 1.68 us -> 0.01 us  [exchange(): ahead = lax.ppermute(primaries, 'rcv', [(i, i ^ 1) for i in range(ring)])]
    concatenate x1 -> x0, other arithmetic: 1.29 us -> none  [exchange(): jnp.concatenate([lax.dynamic_slice_in_dim(array, (1 - core) * side, side,...]
    dynamic_slice x2 -> x1, local copies, waits for them, and re-layouts: 2.33 us -> 1.31 us  [exchange(): lax.dynamic_slice_in_dim(surface_traces, (1 - core) * side, side, axis=1)]
  transfers between devices with their start and end apart: 14 -> 15, of which waited for: 8 -> 7; matrix products, arithmetic and copies ran while one was open for 2% -> 2% of each run, Pallas kernels for 36% -> 43%
where the time goes in v6:
time: 62.8 us; the launch traced here: 61.6 us
  Pallas kernels  29.5 us (47%)
  starting transfers between devices  14.3 us (23%)
  waiting for transfers between devices  12.2 us (19%)
  between operations  2.86 us (5%)
  local copies, waits for them, and re-layouts  1.33 us (2%)
  other arithmetic  1.23 us (2%)
    pallas_call x4, Pallas kernels, sum_of(): pl.pallas_call(functools.partial(sum_kernel, last), out_shape=out_shape,...  14.1 us
    ppermute x13, starting transfers between devices, flip(): return lax.ppermute(value, 'shot', [(i, i ^ bit) for i in range(SQUARE)])  10.6 us
    ppermute x13, waiting for transfers between devices, flip(): return lax.ppermute(value, 'shot', [(i, i ^ bit) for i in range(SQUARE)])  8.99 us
    pallas_call x1, Pallas kernels, bands_of(): pl.pallas_call(band_kernel, out_shape=(jax.ShapeDtypeStruct((panels * hei...  8.32 us
    pallas_call x2, Pallas kernels, pick(): pl.pallas_call(functools.partial(pick_kernel, chunk), out_shape=tuple(out...  3.91 us
    ppermute x1, waiting for transfers between devices, exchange(): lax.ppermute(blocks, 'rcv', [(i, i ^ bit) for i in range(ring)])  3.19 us
    pallas_call x2, Pallas kernels, assemble(): pl.pallas_call(functools.partial(assemble_kernel, at), out_shape=pltpu.HB...  2.61 us
    ppermute x1, starting transfers between devices, exchange(): lax.ppermute(blocks, 'rcv', [(i, i ^ bit) for i in range(ring)])  2.37 us
  transfers between devices with their start and end apart: 15, of which 7 were waited for; matrix products, arithmetic and copies ran while one was open for 2% of the time, Pallas kernels for 43%

profile of v6, /device:TPU:1, one launch (start us, length us, event | category | flops | bytes accessed | tf_op | source)
XLA Modules:
  0.0 61.6 jit_solution(10889366912468951892)
XLA Ops:
  0.0 1.3 %constant_dynamic-slice_fusion.1 = bf16[16,128,256]{2,1,0:T(8,128)(2,1)S(1)} fusion(bf16[16,256,256]{2,1,0:T(8,128)(2,1)} %slot_ref.3, s32[]{:T(128)S(6)} %select_n.54), kind=kLoop, calls=%fused_computation.40 | loop fusion | bytes 2097156 | tf_op jit(solution)/shard_map/dynamic_slice | solution.py:386
  1.3 0.0 copy-start.4
  1.3 0.1 collective-permute-start.19
  1.4 0.1 pad_add_fusion.place_ref
  1.5 2.5 %collective-permute-done.19.met_ref = bf16[16,128,256]{2,1,0:T(8,128)(2,1)S(1)} collective-permute-done((bf16[16,128,256]{2,1,0:T(8,128)(2,1)S(1)}, bf16[16,128,256]{2,1,0:T(8,128)(2,1)S(1)}, u32[]{:S(2)}, u32[]{:S(2)}) %collective-permute-start.19) | collective-permute-done | bytes 1048608 | tf_op jit(solution)/shard_map/ppermute | solution.py:61
  4.1 1.7 %pick.6 = (bf16[16,64,256]{2,1,0:T(8,128)(2,1)S(1)}, bf16[16,64,256]{2,1,0:T(8,128)(2,1)S(1)}) custom-call(s32[4]{0:T(128)S(1)} %copy-done.5, s32[3]{0:T(128)S(1)} %pad_add_fusion.place_ref, bf16[16,256,256]{2,1,0:T(8,128)(2,1)} %slot_ref.3, bf16[16,128,256]{2,1,0:T(8,128)(2,1)S(1)} %collective-permute-done.19.met_ref), custom_call_target="tpu_custom_call" | custom-call | tf_op jit(solution)/shard_map/pick/pallas_call | solution.py:173
  5.7 2.5 %collective-permute-start.22 = (bf16[16,64,256]{2,1,0:T(8,128)(2,1)S(1)}, bf16[16,64,256]{2,1,0:T(8,128)(2,1)S(1)}, u32[]{:S(2)}, u32[]{:S(2)}) collective-permute-start(bf16[16,64,256]{2,1,0:T(8,128)(2,1)S(1)} %get-tuple-element.69.refs_2_.refs_0_), channel_id=1, source_target_pairs={{0,8},{4,12},{8,0},{12,4},{16,24},{20,28},{24,16},{28,20},{1,9},{5... | collective-permute-start | bytes 1572872 | tf_op jit(solution)/shard_map/ppermute | solution.py:61
  8.2 1.2 %collective-permute-start.23 = (bf16[16,64,256]{2,1,0:T(8,128)(2,1)S(1)}, bf16[16,64,256]{2,1,0:T(8,128)(2,1)S(1)}, u32[]{:S(2)}, u32[]{:S(2)}) collective-permute-start(bf16[16,64,256]{2,1,0:T(8,128)(2,1)S(1)} %get-tuple-element.71.refs_1_), channel_id=1, source_target_pairs={{0,16},{4,20},{8,24},{12,28},{16,0},{20,4},{24,8},{28,12},{1,17},{... | collective-permute-start | bytes 1572872 | tf_op jit(solution)/shard_map/ppermute | solution.py:61
  9.5 1.3 %collective-permute-start.20 = (bf16[6,16,64]{2,1,0:T(8,128)(2,1)S(1)}, bf16[6,16,64]{2,1,0:T(8,128)(2,1)S(1)}, u32[]{:S(2)}, u32[]{:S(2)}) collective-permute-start(bf16[6,16,64]{2,1,0:T(8,128)(2,1)S(1)} %copy-done.4), channel_id=1, source_target_pairs={{0,1},{1,0},{2,3},{3,2},{4,5},{5,4},{6,7},{7,6},{8,9},{9,8},{10,11... | collective-permute-start | bytes 36872 | tf_op jit(solution)/shard_map/ppermute | solution.py:387
  10.8 0.7 %fusion.11 = (s32[]{:T(128)}, s32[]{:T(128)}, s32[]{:T(128)}, s32[]{:T(128)}) fusion(s32[4]{0:T(128)S(1)} %copy-done.5), kind=kLoop, calls=%fused_computation.38 | loop fusion | flops 104 | bytes 32 | tf_op jit(solution)/shard_map/reduce_sum | solution.py:427
  14.0 0.0 copy-start.1
  14.0 0.0 collective-permute-done.20.refs_0_
  14.0 2.3 %pick.7 = (s32[14]{0:T(128)S(1)}, f32[1,256]{1,0:T(1,128)S(1)}, bf16[16,64,256]{2,1,0:T(8,128)(2,1)S(1)}, bf16[16,64,256]{2,1,0:T(8,128)(2,1)S(1)}) custom-call(s32[4]{0:T(128)S(1)} %copy-done.5, s32[3]{0:T(128)S(1)} %pad_add_fusion.place_ref, bf16[16,256,256]{2,1,0:T(8,128)(2,1)} %slot_ref.3, bf16[16,128,256]{2,1,0:T(8,128)(2,1)S(1)} %collective-permute-done.19.met_ref, ...), custom_call_target="tpu_custom_call" | custom-call | tf_op jit(solution)/shard_map/pick/pallas_call | solution.py:173
  16.3 0.6 cut.3
  16.9 0.1 collective-permute-start.24
  17.0 0.5 collective-permute-start.21
  17.5 1.2 %collective-permute-done.21 = bf16[2,6,16,64]{3,2,1,0:T(8,128)(2,1)S(1)} collective-permute-done((bf16[2,6,16,64]{3,2,1,0:T(8,128)(2,1)S(1)}, bf16[2,6,16,64]{3,2,1,0:T(8,128)(2,1)S(1)}, u32[]{:S(2)}, u32[]{:S(2)}) %collective-permute-start.21) | collective-permute-done | bytes 24608 | tf_op jit(solution)/shard_map/ppermute | solution.py:61
  18.8 0.3 collective-permute-start.28
  19.1 0.3 collective-permute-start.26
  19.4 0.0 collective-permute-done.24.refs_2_.refs_5_
  19.4 0.9 %collective-permute-done.22.refs_0_.refs_2_ = bf16[16,64,256]{2,1,0:T(8,128)(2,1)S(1)} collective-permute-done((bf16[16,64,256]{2,1,0:T(8,128)(2,1)S(1)}, bf16[16,64,256]{2,1,0:T(8,128)(2,1)S(1)}, u32[]{:S(2)}, u32[]{:S(2)}) %collective-permute-start.22) | collective-permute-done | bytes 524320 | tf_op jit(solution)/shard_map/ppermute | solution.py:61
  20.3 1.9 %collective-permute-done.23.refs_1_.refs_3_ = bf16[16,64,256]{2,1,0:T(8,128)(2,1)S(1)} collective-permute-done((bf16[16,64,256]{2,1,0:T(8,128)(2,1)S(1)}, bf16[16,64,256]{2,1,0:T(8,128)(2,1)S(1)}, u32[]{:S(2)}, u32[]{:S(2)}) %collective-permute-start.23) | collective-permute-done | bytes 524320 | tf_op jit(solution)/shard_map/ppermute | solution.py:61
  22.2 2.4 %collective-permute-start.25 = (bf16[2,12,16,64]{3,2,1,0:T(8,128)(2,1)S(1)}, bf16[2,12,16,64]{3,2,1,0:T(8,128)(2,1)S(1)}, u32[]{:S(2)}, u32[]{:S(2)}) collective-permute-start(bf16[2,12,16,64]{3,2,1,0:T(8,128)(2,1)S(1)} %hand_on.3), channel_id=1, source_target_pairs={{0,2},{1,3},{2,0},{3,1},{4,6},{5,7},{6,4},{7,5},{8,10},{9,11},{10,... | collective-permute-start | bytes 147464 | tf_op jit(solution)/shard_map/ppermute | solution.py:401
  24.6 0.1 broadcast_select_fusion.4
  24.7 0.1 collective-permute-start.31
  24.8 1.3 %collective-permute-start.32 = (bf16[16,64,256]{2,1,0:T(8,128)(2,1)S(1)}, bf16[16,64,256]{2,1,0:T(8,128)(2,1)S(1)}, u32[]{:S(2)}, u32[]{:S(2)}) collective-permute-start(bf16[16,64,256]{2,1,0:T(8,128)(2,1)S(1)} %get-tuple-element.106), channel_id=1, source_target_pairs={{0,16},{4,20},{8,24},{12,28},{16,0},{20,4},{24,8},{28,12},{1,17},{... | collective-permute-start | bytes 1572872 | tf_op jit(solution)/shard_map/ppermute | solution.py:61
  26.1 3.2 %collective-permute-done.25 = bf16[2,12,16,64]{3,2,1,0:T(8,128)(2,1)S(1)} collective-permute-done((bf16[2,12,16,64]{3,2,1,0:T(8,128)(2,1)S(1)}, bf16[2,12,16,64]{3,2,1,0:T(8,128)(2,1)S(1)}, u32[]{:S(2)}, u32[]{:S(2)}) %collective-permute-start.25) | collective-permute-done | bytes 49184 | tf_op jit(solution)/shard_map/ppermute | solution.py:401
  29.3 0.1 fusion.7.taps_ref
  29.3 8.3 %bands.3 = (bf16[4096,1536]{1,0:T(8,128)(2,1)S(1)}, f32[1,256]{1,0:T(1,128)S(1)}) custom-call(s32[3]{0:T(128)S(1)} %pad_add_fusion.place_ref, f32[4,12,16,128]{3,2,1,0:T(8,128)S(1)} %fusion.7.taps_ref, f32[1,256]{1,0:T(1,128)S(1)} %get-tuple-element.73.full_ref), custom_call_target="tpu_custom_call" | custom-call | flops 50331648 | bytes 12582912 | tf_op jit(solution)/shard_map/bands/pallas_call | solution.py:83
  37.7 0.0 collective-permute-done.26.refs_3_
  37.7 0.0 collective-permute-done.28.refs_2_
  37.7 0.2 broadcast_select_fusion.6
  37.9 0.1 collective-permute-start.27
  37.9 1.3 %collective-permute-start.29 = (bf16[16,64,256]{2,1,0:T(8,128)(2,1)S(1)}, bf16[16,64,256]{2,1,0:T(8,128)(2,1)S(1)}, u32[]{:S(2)}, u32[]{:S(2)}) collective-permute-start(bf16[16,64,256]{2,1,0:T(8,128)(2,1)S(1)} %get-tuple-element.108), channel_id=1, source_target_pairs={{0,16},{4,20},{8,24},{12,28},{16,0},{20,4},{24,8},{28,12},{1,17},{... | collective-permute-start | bytes 1572872 | tf_op jit(solution)/shard_map/ppermute | solution.py:61
  39.3 4.8 %early_sum.7.refs_3_ = f32[12,64,256]{2,1,0:T(8,128)S(1)} custom-call(s32[14]{0:T(128)S(1)} %get-tuple-element.70.plan_ref, s32[3]{0:T(128)S(1)} %pad_add_fusion.place_ref, bf16[16,64,256]{2,1,0:T(8,128)(2,1)S(1)} %get-tuple-element.69.refs_2_.refs_0_, bf16[16,64,256]{2,1,0:T(8,128)(2,1)S(1)} %get-tuple-element.71.refs_1_, ...), custom_call_target="tpu_custom_call" | custom-call | flops 3221225472 | bytes 12582912 | tf_op jit(solution)/shard_map/early_sum/pallas_call | solution.py:324
  44.1 4.8 %early_sum.6.refs_3_ = f32[12,64,256]{2,1,0:T(8,128)S(1)} custom-call(s32[14]{0:T(128)S(1)} %get-tuple-element.70.plan_ref, s32[3]{0:T(128)S(1)} %pad_add_fusion.place_ref, bf16[16,64,256]{2,1,0:T(8,128)(2,1)S(1)} %get-tuple-element.72.refs_0_, bf16[16,64,256]{2,1,0:T(8,128)(2,1)S(1)} %get-tuple-element.75.refs_1_, ...), custom_call_target="tpu_custom_call" | custom-call | flops 3221225472 | bytes 12582912 | tf_op jit(solution)/shard_map/early_sum/pallas_call | solution.py:324
  48.9 0.0 collective-permute-done.31.refs_0_
  48.9 0.0 collective-permute-done.32.refs_1_
  49.0 2.2 %residual.7 = (bf16[6,64,256]{2,1,0:T(8,128)(2,1)S(1)}, bf16[6,64,256]{2,1,0:T(8,128)(2,1)S(1)}) custom-call(s32[14]{0:T(128)S(1)} %get-tuple-element.70.plan_ref, s32[3]{0:T(128)S(1)} %pad_add_fusion.place_ref, bf16[16,64,256]{2,1,0:T(8,128)(2,1)S(1)} %collective-permute-done.31.refs_0_, bf16[16,64,256]{2,1,0:T(8,128)(2,1)S(1)} %collective-permute-done.32.refs_1_, ...), custom_call_target="tpu_custom_call" | custom-call | flops 1610612736 | bytes 6291456 | tf_op jit(solution)/shard_map/residual/pallas_call | solution.py:324
  51.2 1.6 %collective-permute-start.33 = (bf16[6,64,256]{2,1,0:T(8,128)(2,1)S(1)}, bf16[6,64,256]{2,1,0:T(8,128)(2,1)S(1)}, u32[]{:S(2)}, u32[]{:S(2)}) collective-permute-start(bf16[6,64,256]{2,1,0:T(8,128)(2,1)S(1)} %get-tuple-element.80), channel_id=1, source_target_pairs={{0,4},{4,0},{8,12},{12,8},{16,20},{20,16},{24,28},{28,24},{1,5},{5... | collective-permute-start | bytes 589832 | tf_op jit(solution)/shard_map/ppermute | solution.py:61
  52.8 1.9 %collective-permute-done.27.refs_0_ = bf16[16,64,256]{2,1,0:T(8,128)(2,1)S(1)} collective-permute-done((bf16[16,64,256]{2,1,0:T(8,128)(2,1)S(1)}, bf16[16,64,256]{2,1,0:T(8,128)(2,1)S(1)}, u32[]{:S(2)}, u32[]{:S(2)}) %collective-permute-start.27) | collective-permute-done | bytes 524320 | tf_op jit(solution)/shard_map/ppermute | solution.py:61
  54.7 0.5 collective-permute-done.29.refs_1_
  55.2 2.2 %residual.6 = (bf16[6,64,256]{2,1,0:T(8,128)(2,1)S(1)}, bf16[6,64,256]{2,1,0:T(8,128)(2,1)S(1)}) custom-call(s32[14]{0:T(128)S(1)} %get-tuple-element.70.plan_ref, s32[3]{0:T(128)S(1)} %pad_add_fusion.place_ref, bf16[16,64,256]{2,1,0:T(8,128)(2,1)S(1)} %collective-permute-done.27.refs_0_, bf16[16,64,256]{2,1,0:T(8,128)(2,1)S(1)} %collective-permute-done.29.refs_1_, ...), custom_call_target="tpu_custom_call" | custom-call | flops 1610612736 | bytes 6291456 | tf_op jit(solution)/shard_map/residual/pallas_call | solution.py:324
  57.4 0.0 copy-start
  57.4 1.1 %collective-permute-start.30 = (bf16[6,64,256]{2,1,0:T(8,128)(2,1)S(1)}, bf16[6,64,256]{2,1,0:T(8,128)(2,1)S(1)}, u32[]{:S(2)}, u32[]{:S(2)}) collective-permute-start(bf16[6,64,256]{2,1,0:T(8,128)(2,1)S(1)} %get-tuple-element.77), channel_id=1, source_target_pairs={{0,4},{4,0},{8,12},{12,8},{16,20},{20,16},{24,28},{28,24},{1,5},{5... | collective-permute-start | bytes 589832 | tf_op jit(solution)/shard_map/ppermute | solution.py:61
  58.6 1.4 %assemble.6.refs_1_ = bf16[6,256,256]{2,1,0:T(8,128)(2,1)} custom-call(s32[3]{0:T(128)S(1)} %pad_add_fusion.place_ref, bf16[6,64,256]{2,1,0:T(8,128)(2,1)S(1)} %get-tuple-element.78.refs_0_, bf16[6,64,256]{2,1,0:T(8,128)(2,1)S(1)} %get-tuple-element.79.refs_1_, bf16[6,64,256]{2,1,0:T(8,128)(2,1)S(1)} %collective-permute-done.33.refs_2_), custom_call_target="tpu_custom_call" | custom-call | tf_op jit(solution)/shard_map/assemble/pallas_call | solution.py:362
  60.0 1.2 %assemble.7 = bf16[6,256,256]{2,1,0:T(8,128)(2,1)} custom-call(s32[3]{0:T(128)S(1)} %pad_add_fusion.place_ref, bf16[6,64,256]{2,1,0:T(8,128)(2,1)S(1)} %collective-permute-done.30.refs_0_, bf16[6,256,256]{2,1,0:T(8,128)(2,1)} %assemble.6.refs_1_), custom_call_target="tpu_custom_call", output_to_operand_aliasing={{}: (2, {})} | custom-call | tf_op jit(solution)/shard_map/assemble/pallas_call | solution.py:362
  61.2 0.2 while.9
  (12 shorter events, 0.1 us)
Async XLA Ops:
  0.0 4.1 %copy-start.5 = (s32[4]{0:T(128)S(1)}, s32[4]{0:T(128)}, u32[]{:S(2)}) copy-start(s32[4]{0:T(128)} %owner_ref.3) | copy-start | bytes 52
  1.3 8.2 %copy-start.4 = (bf16[6,16,64]{2,1,0:T(8,128)(2,1)S(1)}, bf16[6,16,64]{2,1,0:T(8,128)(2,1)}, u32[]{:S(2)}) copy-start(bf16[6,16,64]{2,1,0:T(8,128)(2,1)} %param.8) | copy-start | bytes 36868
  1.3 2.7 %collective-permute-start.19 = (bf16[16,128,256]{2,1,0:T(8,128)(2,1)S(1)}, bf16[16,128,256]{2,1,0:T(8,128)(2,1)S(1)}, u32[]{:S(2)}, u32[]{:S(2)}) collective-permute-start(bf16[16,128,256]{2,1,0:T(8,128)(2,1)S(1)} %constant_dynamic-slice_fusion.1), channel_id=1, source_target_pairs={{0,4},{4,0},{8,12},{12,8},{16,20},{20,16},{24,28},{28,24},{1,5},{5... | collective-permute-start | bytes 3145736 | tf_op jit(solution)/shard_map/ppermute | solution.py:61
  5.7 14.6 %collective-permute-start.22 = (bf16[16,64,256]{2,1,0:T(8,128)(2,1)S(1)}, bf16[16,64,256]{2,1,0:T(8,128)(2,1)S(1)}, u32[]{:S(2)}, u32[]{:S(2)}) collective-permute-start(bf16[16,64,256]{2,1,0:T(8,128)(2,1)S(1)} %get-tuple-element.69.refs_2_.refs_0_), channel_id=1, source_target_pairs={{0,8},{4,12},{8,0},{12,4},{16,24},{20,28},{24,16},{28,20},{1,9},{5... | collective-permute-start | bytes 1572872 | tf_op jit(solution)/shard_map/ppermute | solution.py:61
  8.2 13.9 %collective-permute-start.23 = (bf16[16,64,256]{2,1,0:T(8,128)(2,1)S(1)}, bf16[16,64,256]{2,1,0:T(8,128)(2,1)S(1)}, u32[]{:S(2)}, u32[]{:S(2)}) collective-permute-start(bf16[16,64,256]{2,1,0:T(8,128)(2,1)S(1)} %get-tuple-element.71.refs_1_), channel_id=1, source_target_pairs={{0,16},{4,20},{8,24},{12,28},{16,0},{20,4},{24,8},{28,12},{1,17},{... | collective-permute-start | bytes 1572872 | tf_op jit(solution)/shard_map/ppermute | solution.py:61
  9.5 4.5 %collective-permute-start.20 = (bf16[6,16,64]{2,1,0:T(8,128)(2,1)S(1)}, bf16[6,16,64]{2,1,0:T(8,128)(2,1)S(1)}, u32[]{:S(2)}, u32[]{:S(2)}) collective-permute-start(bf16[6,16,64]{2,1,0:T(8,128)(2,1)S(1)} %copy-done.4), channel_id=1, source_target_pairs={{0,1},{1,0},{2,3},{3,2},{4,5},{5,4},{6,7},{7,6},{8,9},{9,8},{10,11... | collective-permute-start | bytes 36872 | tf_op jit(solution)/shard_map/ppermute | solution.py:387
  14.0 2.3 %copy-start.1 = (bf16[6,256,256]{2,1,0:T(8,128)(2,1)S(1)}, bf16[6,256,256]{2,1,0:T(8,128)(2,1)}, u32[]{:S(2)}) copy-start(bf16[6,256,256]{2,1,0:T(8,128)(2,1)} %refs_4_.3) | copy-start | bytes 2359300
  16.9 2.5 %collective-permute-start.24 = (bf16[6,128,256]{2,1,0:T(8,128)(2,1)S(1)}, bf16[6,128,256]{2,1,0:T(8,128)(2,1)S(1)}, u32[]{:S(2)}, u32[]{:S(2)}) collective-permute-start(bf16[6,128,256]{2,1,0:T(8,128)(2,1)S(1)} %cut.3), channel_id=1, source_target_pairs={{0,4},{4,0},{8,12},{12,8},{16,20},{20,16},{24,28},{28,24},{1,5},{5... | collective-permute-start | bytes 1179656 | tf_op jit(solution)/shard_map/ppermute | solution.py:61
  17.0 1.7 %collective-permute-start.21 = (bf16[2,6,16,64]{3,2,1,0:T(8,128)(2,1)S(1)}, bf16[2,6,16,64]{3,2,1,0:T(8,128)(2,1)S(1)}, u32[]{:S(2)}, u32[]{:S(2)}) collective-permute-start(bf16[2,6,16,64]{3,2,1,0:T(8,128)(2,1)S(1)} %pad_maximum_fusion.3), channel_id=1, source_target_pairs={{0,4},{4,0},{8,12},{12,8},{16,20},{20,16},{24,28},{28,24},{1,5},{5... | collective-permute-start | bytes 73736 | tf_op jit(solution)/shard_map/ppermute | solution.py:61
  18.8 18.9 %collective-permute-start.28 = (bf16[16,64,256]{2,1,0:T(8,128)(2,1)S(1)}, bf16[16,64,256]{2,1,0:T(8,128)(2,1)S(1)}, u32[]{:S(2)}, u32[]{:S(2)}) collective-permute-start(bf16[16,64,256]{2,1,0:T(8,128)(2,1)S(1)} %get-tuple-element.72.refs_0_), channel_id=1, source_target_pairs={{0,8},{4,12},{8,0},{12,4},{16,24},{20,28},{24,16},{28,20},{1,9},{5... | collective-permute-start | bytes 1572872 | tf_op jit(solution)/shard_map/ppermute | solution.py:61
  19.1 18.6 %collective-permute-start.26 = (bf16[16,64,256]{2,1,0:T(8,128)(2,1)S(1)}, bf16[16,64,256]{2,1,0:T(8,128)(2,1)S(1)}, u32[]{:S(2)}, u32[]{:S(2)}) collective-permute-start(bf16[16,64,256]{2,1,0:T(8,128)(2,1)S(1)} %get-tuple-element.75.refs_1_), channel_id=1, source_target_pairs={{0,16},{4,20},{8,24},{12,28},{16,0},{20,4},{24,8},{28,12},{1,17},{... | collective-permute-start | bytes 1572872 | tf_op jit(solution)/shard_map/ppermute | solution.py:61
  22.2 7.1 %collective-permute-start.25 = (bf16[2,12,16,64]{3,2,1,0:T(8,128)(2,1)S(1)}, bf16[2,12,16,64]{3,2,1,0:T(8,128)(2,1)S(1)}, u32[]{:S(2)}, u32[]{:S(2)}) collective-permute-start(bf16[2,12,16,64]{3,2,1,0:T(8,128)(2,1)S(1)} %hand_on.3), channel_id=1, source_target_pairs={{0,2},{1,3},{2,0},{3,1},{4,6},{5,7},{6,4},{7,5},{8,10},{9,11},{10,... | collective-permute-start | bytes 147464 | tf_op jit(solution)/shard_map/ppermute | solution.py:401
  24.7 24.2 %collective-permute-start.31 = (bf16[16,64,256]{2,1,0:T(8,128)(2,1)S(1)}, bf16[16,64,256]{2,1,0:T(8,128)(2,1)S(1)}, u32[]{:S(2)}, u32[]{:S(2)}) collective-permute-start(bf16[16,64,256]{2,1,0:T(8,128)(2,1)S(1)} %get-tuple-element.107), channel_id=1, source_target_pairs={{0,8},{4,12},{8,0},{12,4},{16,24},{20,28},{24,16},{28,20},{1,9},{5... | collective-permute-start | bytes 1572872 | tf_op jit(solution)/shard_map/ppermute | solution.py:61
  24.8 24.2 %collective-permute-start.32 = (bf16[16,64,256]{2,1,0:T(8,128)(2,1)S(1)}, bf16[16,64,256]{2,1,0:T(8,128)(2,1)S(1)}, u32[]{:S(2)}, u32[]{:S(2)}) collective-permute-start(bf16[16,64,256]{2,1,0:T(8,128)(2,1)S(1)} %get-tuple-element.106), channel_id=1, source_target_pairs={{0,16},{4,20},{8,24},{12,28},{16,0},{20,4},{24,8},{28,12},{1,17},{... | collective-permute-start | bytes 1572872 | tf_op jit(solution)/shard_map/ppermute | solution.py:61
  37.9 16.8 %collective-permute-start.27 = (bf16[16,64,256]{2,1,0:T(8,128)(2,1)S(1)}, bf16[16,64,256]{2,1,0:T(8,128)(2,1)S(1)}, u32[]{:S(2)}, u32[]{:S(2)}) collective-permute-start(bf16[16,64,256]{2,1,0:T(8,128)(2,1)S(1)} %get-tuple-element.109), channel_id=1, source_target_pairs={{0,8},{4,12},{8,0},{12,4},{16,24},{20,28},{24,16},{28,20},{1,9},{5... | collective-permute-start | bytes 1572872 | tf_op jit(solution)/shard_map/ppermute | solution.py:61
  37.9 17.3 %collective-permute-start.29 = (bf16[16,64,256]{2,1,0:T(8,128)(2,1)S(1)}, bf16[16,64,256]{2,1,0:T(8,128)(2,1)S(1)}, u32[]{:S(2)}, u32[]{:S(2)}) collective-permute-start(bf16[16,64,256]{2,1,0:T(8,128)(2,1)S(1)} %get-tuple-element.108), channel_id=1, source_target_pairs={{0,16},{4,20},{8,24},{12,28},{16,0},{20,4},{24,8},{28,12},{1,17},{... | collective-permute-start | bytes 1572872 | tf_op jit(solution)/shard_map/ppermute | solution.py:61
  51.2 7.4 %collective-permute-start.33 = (bf16[6,64,256]{2,1,0:T(8,128)(2,1)S(1)}, bf16[6,64,256]{2,1,0:T(8,128)(2,1)S(1)}, u32[]{:S(2)}, u32[]{:S(2)}) collective-permute-start(bf16[6,64,256]{2,1,0:T(8,128)(2,1)S(1)} %get-tuple-element.80), channel_id=1, source_target_pairs={{0,4},{4,0},{8,12},{12,8},{16,20},{20,16},{24,28},{28,24},{1,5},{5... | collective-permute-start | bytes 589832 | tf_op jit(solution)/shard_map/ppermute | solution.py:61
  57.4 3.8 %copy-start = (bf16[16,256,256]{2,1,0:T(8,128)(2,1)S(1)}, bf16[16,256,256]{2,1,0:T(8,128)(2,1)}, u32[]{:S(2)}) copy-start(bf16[16,256,256]{2,1,0:T(8,128)(2,1)} %slot_ref.3) | copy-start | bytes 6291460
  57.4 2.5 %collective-permute-start.30 = (bf16[6,64,256]{2,1,0:T(8,128)(2,1)S(1)}, bf16[6,64,256]{2,1,0:T(8,128)(2,1)S(1)}, u32[]{:S(2)}, u32[]{:S(2)}) collective-permute-start(bf16[6,64,256]{2,1,0:T(8,128)(2,1)S(1)} %get-tuple-element.77), channel_id=1, source_target_pairs={{0,4},{4,0},{8,12},{12,8},{16,20},{20,16},{24,28},{28,24},{1,5},{5... | collective-permute-start | bytes 589832 | tf_op jit(solution)/shard_map/ppermute | solution.py:61

commit v7 on v6

--- a/solution.py
+++ b/solution.py
@@ -132,9 +132,15 @@
         late = late + jnp.where(met_first, 0, 1)
     plan_ref[3 * panels] = early
     plan_ref[3 * panels + 1] = late
-
-
-def pick_kernel(chunk, owner_ref, place_ref, slot_ref, met_ref, *refs):
+    held = [jnp.int32(0)] * (SQUARE // 2)
+    for panel in range(panels):
+        held = [count + (owner_ref[panel] // 2 == place).astype(jnp.int32) for place, count in enumerate(held)]
+    full = [count == 2 for count in held]
+    pairs = [full[place] & full[place ^ bit] for place in range(SQUARE // 2) for bit in (1, 2) if place < place ^ bit]
+    plan_ref[3 * panels + 2] = functools.reduce(jnp.logical_or, pairs).astype(jnp.int32)
+
+
+def pick_kernel(chunk, owner_ref, place_ref, here_ref, there_ref, *refs):
     chip, core = place_ref[0], place_ref[1]
     first_owns, second_owns = jnp.bool_(False), jnp.bool_(False)
     for panel in range(owner_ref.shape[0]):
@@ -142,9 +148,6 @@
         second_owns = second_owns | (owner_ref[panel] == 2 * chip + 1)
     *others, a_ref, b_ref, sems = refs
     outs = (a_ref, b_ref)
-    points, rows, _ = a_ref.shape
-    here_ref = slot_ref.at[:, pl.ds(pl.multiple_of((core * CHUNKS + chunk) * rows, rows), rows), :]
-    there_ref = met_ref.at[:, pl.ds(chunk * rows, rows), :]
     for index, mine in enumerate((first_owns == (core == 0), second_owns == (core == 1))):
         @pl.when(mine)
         def _():
@@ -162,13 +165,13 @@
         pltpu.make_async_copy(there_ref, outs[index], sems.at[index]).wait()
 
 
-def pick(chunk, owner, place, slot, met, before):
-    points, length = slot.shape[0], slot.shape[2]
+def pick(chunk, owner, place, here, there, before):
+    length = here.shape[2]
     in_vmem = pl.BlockSpec(memory_space=pltpu.VMEM)
-    outs = [jax.ShapeDtypeStruct((points, met.shape[1] // CHUNKS, length), slot.dtype)] * 2
+    outs = [jax.ShapeDtypeStruct(here.shape, here.dtype)] * 2
     specs = [in_vmem] * 2
     if chunk == 1:
-        outs = [jax.ShapeDtypeStruct((3 * owner.shape[0] + 2,), jnp.int32), jax.ShapeDtypeStruct((1, length), jnp.float32)] + outs
+        outs = [jax.ShapeDtypeStruct((3 * owner.shape[0] + 3,), jnp.int32), jax.ShapeDtypeStruct((1, length), jnp.float32)] + outs
         specs = [IN_SMEM, in_vmem] + specs
     return pl.pallas_call(
         functools.partial(pick_kernel, chunk),
@@ -179,7 +182,7 @@
         compiler_params=pltpu.CompilerParams(vmem_limit_bytes=2 * SMALL_VMEM_BYTES),
         cost_estimate=NO_COST,
         name="pick",
-    )(owner, place, slot, met, *before)
+    )(owner, place, here, there, *before)
 
 
 def cut_kernel(place_ref, array_ref, *refs):
@@ -227,7 +230,7 @@
     window, spread, total, arrived = refs[-4:]
     step, steps = pl.program_id(0), pl.num_programs(0)
     slots, points, rows, length = window.shape
-    panels = (plan_ref.shape[0] - 2) // 3
+    panels = plan_ref.shape[0] // 3 - 1
     entries = panels * (2 if last else 1)
     wanted = plan_ref[3 * panels + (1 if last else 0)]
     half = spread.shape[1] // points
@@ -293,7 +296,7 @@
 
 def sum_of(plan, place, sources, bands, steps, taps, late=None):
     points, rows, length = sources[0].shape
-    panels = (plan.shape[0] - 2) // 3
+    panels = plan.shape[0] // 3 - 1
     height, columns = bands.shape[0] // panels, bands.shape[1]
     shots = columns // (2 * taps)
     last = late is not None
@@ -372,36 +375,33 @@
     )(place, *pieces, *given)
 
 
-def any_of(flags):
-    return functools.reduce(jnp.logical_or, flags)
-
-
-def exchange(data, surface_traces, primaries, panel_owner, place, flag, third):
+def exchange(data, surface_traces, primaries, panel_owner, place, third):
     panels = panel_owner.shape[0]
     side = data.shape[1] // 2
     rows = side // CHUNKS
     taps = primaries.shape[2]
     core = lax.rem(lax.axis_index("shot"), 2)
     ring = lax.axis_size("rcv")
-    met = flip(lax.dynamic_slice_in_dim(surface_traces, (1 - core) * side, side, axis=1), CORE)
     ahead = lax.ppermute(primaries, "rcv", [(i, i ^ 1) for i in range(ring)])
     blocks, bit = jnp.stack([primaries, ahead]), 2
     blocks = jnp.concatenate([blocks, flip(blocks, CORE)], axis=1)
     own_a, own_b = [], []
     for chunk in range(CHUNKS):
-        *extra, a, b = pick(chunk, panel_owner, place, surface_traces, met, [ahead, flag, own_a[-1]] if own_a else [])
+        here, there = (lax.dynamic_slice_in_dim(surface_traces, at * side + chunk * rows, rows, axis=1) for at in (core, 1 - core))
+        *extra, a, b = pick(chunk, panel_owner, place, here, flip(there, CORE), [ahead] if own_a else [])
         if extra:
             plan, full = extra
         own_a.append(a)
         own_b.append(b)
-    other_data = flip(cut(data, place, [own_a[-1]]), CORE)
     across, down = [flip(a, ACROSS) for a in own_a], [flip(b, DOWN) for b in own_b]
-    blocks = hand_on(blocks, [across[0], down[0], other_data])
+    neighbours_full = plan[-1] > 0
+    blocks = hand_on(blocks, [across[0], down[0], neighbours_full.astype(jnp.float32)[None]])
     while bit < ring:
         blocks = jnp.concatenate([blocks, lax.ppermute(blocks, "rcv", [(i, i ^ bit) for i in range(ring)])])
         bit *= 2
     blocks = jnp.pad(blocks.astype(jnp.float32), ((0, 0), (0, 0), (0, 0), (0, taps)))
     bands, full_later = bands_of(blocks, place, full)
+    other_data = flip(cut(data, place, [full_later]), CORE)
     rows_full = [full] + [full_later] * (CHUNKS - 1)
     for_across = [jnp.where(row[0] > 0, own, met) for row, own, met in zip(rows_full, own_b, down)]
     for_down = [jnp.where(row[0] > 0, own, met) for row, own, met in zip(rows_full, own_a, across)]
@@ -418,17 +418,15 @@
         returned.append(flip(others, CORE))
     places = [(False, chunk) for chunk in range(CHUNKS)] + [(True, chunk) for chunk in range(CHUNKS)]
     residual = assemble(place, (kept + returned)[:-1], places[:-1], data)
-    return assemble(place, returned[-1:], places[-1:], data, residual)
+    return neighbours_full, assemble(place, returned[-1:], places[-1:], data, residual)
 
 
 def square_shards(data, surface_traces, primaries, panel_owner):
     me = lax.axis_index("shot")
     place = jnp.stack([me // 2, me % 2, lax.axis_index("rcv")]).astype(jnp.int32)
-    holds_two = [jnp.sum(panel_owner // 2 == other) == 2 for other in range(SQUARE // 2)]
-    neighbours_full = any_of([holds_two[at] & holds_two[at ^ bit] for at in range(SQUARE // 2) for bit in (1, 2) if at < at ^ bit])
-    arguments = (data, surface_traces, primaries, panel_owner, place, neighbours_full.astype(jnp.float32)[None])
-    residual = exchange(*arguments, False)
-    return lax.while_loop(lambda state: state[0], lambda state: (jnp.bool_(False), exchange(*arguments, True)), (neighbours_full, residual))[1]
+    arguments = (data, surface_traces, primaries, panel_owner, place)
+    again = lambda state: (jnp.bool_(False), exchange(*arguments, True)[1])
+    return lax.while_loop(lambda state: state[0], again, exchange(*arguments, False))[1]
 
 
 def solution(mesh):

time: 62.8 us -> 61.4 us (0.978); the launches traced: 61.6 us -> 61.3 us
  starting transfers between devices: 14.3 us -> 19.4 us
  Pallas kernels: 29.5 us -> 27.4 us
  between operations: 2.86 us -> 1 us
  waiting for transfers between devices: 12.2 us -> 10.5 us
  local copies, waits for them, and re-layouts: 1.33 us -> 2.31 us
  other arithmetic: 1.23 us -> 0.42 us
    ppermute x13 -> x14, starting transfers between devices: 10.6 us -> 15.8 us  [flip(): return lax.ppermute(value, 'shot', [(i, i ^ bit) for i in range(SQUARE)])]
    ppermute x1, waiting for transfers between devices: 3.19 us -> 0.33 us  [exchange(): lax.ppermute(blocks, 'rcv', [(i, i ^ bit) for i in range(ring)])]
    pallas_call x2, Pallas kernels: 3.91 us -> 2.03 us  [pick(): pl.pallas_call(functools.partial(pick_kernel, chunk), out_shape=tuple(out...]
    ppermute x1, waiting for transfers between devices: 0.01 us -> 1.68 us  [exchange(): ahead = lax.ppermute(primaries, 'rcv', [(i, i ^ 1) for i in range(ring)])]
    reduce_sum x1 -> x0, other arithmetic: 0.74 us -> none  [square_shards(): jnp.sum(panel_owner // 2 == other) == 2]
    ppermute x13 -> x14, waiting for transfers between devices: 8.99 us -> 8.54 us  [flip(): return lax.ppermute(value, 'shot', [(i, i ^ bit) for i in range(SQUARE)])]
  transfers between devices with their start and end apart: 15 -> 16, of which waited for: 7 -> 8; matrix products, arithmetic and copies ran while one was open for 2% -> 2% of each run, Pallas kernels for 43% -> 43%
where the time goes in v7:
time: 61.4 us; the launch traced here: 61.3 us
  Pallas kernels  27.4 us (45%)
  starting transfers between devices  19.4 us (32%)
  waiting for transfers between devices  10.5 us (17%)
  local copies, waits for them, and re-layouts  2.31 us (4%)
  between operations  1 us (2%)
    ppermute x14, starting transfers between devices, flip(): return lax.ppermute(value, 'shot', [(i, i ^ bit) for i in range(SQUARE)])  15.8 us
    pallas_call x4, Pallas kernels, sum_of(): pl.pallas_call(functools.partial(sum_kernel, last), out_shape=out_shape,...  13.8 us
    ppermute x14, waiting for transfers between devices, flip(): return lax.ppermute(value, 'shot', [(i, i ^ bit) for i in range(SQUARE)])  8.54 us
    pallas_call x1, Pallas kernels, bands_of(): pl.pallas_call(band_kernel, out_shape=(jax.ShapeDtypeStruct((panels * hei...  8.32 us
    pallas_call x2, Pallas kernels, assemble(): pl.pallas_call(functools.partial(assemble_kernel, at), out_shape=pltpu.HB...  2.61 us
    ppermute x1, starting transfers between devices, exchange(): lax.ppermute(blocks, 'rcv', [(i, i ^ bit) for i in range(ring)])  2.37 us
    pallas_call x2, Pallas kernels, pick(): pl.pallas_call(functools.partial(pick_kernel, chunk), out_shape=tuple(out...  2.03 us
    dynamic_slice x1, local copies, waits for them, and re-layouts, exchange(): lax.dynamic_slice_in_dim(surface_traces, at * side + chunk * rows, rows,...  1.72 us
  transfers between devices with their start and end apart: 16, of which 8 were waited for; matrix products, arithmetic and copies ran while one was open for 2% of the time, Pallas kernels for 43%

profile of v7, /device:TPU:1, one launch (start us, length us, event | category | flops | bytes accessed | tf_op | source)
XLA Modules:
  0.0 61.3 jit_solution(18145435355075683740)
XLA Ops:
  0.0 1.7 %constant_dynamic-slice_fusion.4 = (bf16[16,64,256]{2,1,0:T(8,128)(2,1)S(1)}, bf16[16,64,256]{2,1,0:T(8,128)(2,1)S(1)}, bf16[16,64,256]{2,1,0:T(8,128)(2,1)S(1)}, bf16[16,64,256]{2,1,0:T(8,128)(2,1)S(1)}) fusion(bf16[16,256,256]{2,1,0:T(8,128)(2,1)} %param.7, s32[]{:T(128)S(6)} %select_n.66, s32[]{:T(128)S(6)} %select_n.65, s32[]{:T(128)S(6)} %select_n.64, ...), kind=kLoop, calls=%fused_computation.30 | loop fusion | bytes 4194320 | tf_op jit(solution)/shard_map/dynamic_slice | solution.py:390
  1.7 0.1 collective-permute-start.23
  1.8 0.5 collective-permute-start.20
  2.3 0.1 pad_add_fusion.place_ref
  2.4 1.3 %collective-permute-done.23.there_ref = bf16[16,64,256]{2,1,0:T(8,128)(2,1)S(1)} collective-permute-done((bf16[16,64,256]{2,1,0:T(8,128)(2,1)S(1)}, bf16[16,64,256]{2,1,0:T(8,128)(2,1)S(1)}, u32[]{:S(2)}, u32[]{:S(2)}) %collective-permute-start.23) | collective-permute-done | bytes 524320 | tf_op jit(solution)/shard_map/ppermute | solution.py:61
  3.7 0.7 %pick.7 = (bf16[16,64,256]{2,1,0:T(8,128)(2,1)S(1)}, bf16[16,64,256]{2,1,0:T(8,128)(2,1)S(1)}) custom-call(s32[4]{0:T(128)S(1)} %copy-done.2, s32[3]{0:T(128)S(1)} %pad_add_fusion.place_ref, bf16[16,64,256]{2,1,0:T(8,128)(2,1)S(1)} %get-tuple-element.100.here_ref, bf16[16,64,256]{2,1,0:T(8,128)(2,1)S(1)} %collective-permute-done.23.there_ref), custom_call_target="tpu_custom_call" | custom-call | tf_op jit(solution)/shard_map/pick/pallas_call | solution.py:176
  4.4 2.4 %collective-permute-start.24 = (bf16[16,64,256]{2,1,0:T(8,128)(2,1)S(1)}, bf16[16,64,256]{2,1,0:T(8,128)(2,1)S(1)}, u32[]{:S(2)}, u32[]{:S(2)}) collective-permute-start(bf16[16,64,256]{2,1,0:T(8,128)(2,1)S(1)} %get-tuple-element.65.refs_0_), channel_id=1, source_target_pairs={{0,8},{4,12},{8,0},{12,4},{16,24},{20,28},{24,16},{28,20},{1,9},{5... | collective-permute-start | bytes 1572872 | tf_op jit(solution)/shard_map/ppermute | solution.py:61
  6.8 1.2 %collective-permute-start.25 = (bf16[16,64,256]{2,1,0:T(8,128)(2,1)S(1)}, bf16[16,64,256]{2,1,0:T(8,128)(2,1)S(1)}, u32[]{:S(2)}, u32[]{:S(2)}) collective-permute-start(bf16[16,64,256]{2,1,0:T(8,128)(2,1)S(1)} %get-tuple-element.66.refs_1_), channel_id=1, source_target_pairs={{0,16},{4,20},{8,24},{12,28},{16,0},{20,4},{24,8},{28,12},{1,17},{... | collective-permute-start | bytes 1572872 | tf_op jit(solution)/shard_map/ppermute | solution.py:61
  8.0 1.3 %collective-permute-start.21 = (bf16[6,16,64]{2,1,0:T(8,128)(2,1)S(1)}, bf16[6,16,64]{2,1,0:T(8,128)(2,1)S(1)}, u32[]{:S(2)}, u32[]{:S(2)}) collective-permute-start(bf16[6,16,64]{2,1,0:T(8,128)(2,1)S(1)} %copy-done.1), channel_id=1, source_target_pairs={{0,1},{1,0},{2,3},{3,2},{4,5},{5,4},{6,7},{7,6},{8,9},{9,8},{10,11... | collective-permute-start | bytes 36872 | tf_op jit(solution)/shard_map/ppermute | solution.py:385
  9.3 1.7 %collective-permute-done.21.refs_0_ = bf16[6,16,64]{2,1,0:T(8,128)(2,1)S(1)} collective-permute-done((bf16[6,16,64]{2,1,0:T(8,128)(2,1)S(1)}, bf16[6,16,64]{2,1,0:T(8,128)(2,1)S(1)}, u32[]{:S(2)}, u32[]{:S(2)}) %collective-permute-start.21) | collective-permute-done | bytes 12320 | tf_op jit(solution)/shard_map/ppermute | solution.py:385
  11.0 1.9 %collective-permute-start.22 = (bf16[2,6,16,64]{3,2,1,0:T(8,128)(2,1)S(1)}, bf16[2,6,16,64]{3,2,1,0:T(8,128)(2,1)S(1)}, u32[]{:S(2)}, u32[]{:S(2)}) collective-permute-start(bf16[2,6,16,64]{3,2,1,0:T(8,128)(2,1)S(1)} %pad_maximum_fusion.3), channel_id=1, source_target_pairs={{0,4},{4,0},{8,12},{12,8},{16,20},{20,16},{24,28},{28,24},{1,5},{5... | collective-permute-start | bytes 73736 | tf_op jit(solution)/shard_map/ppermute | solution.py:61
  12.9 0.9 %collective-permute-done.22 = bf16[2,6,16,64]{3,2,1,0:T(8,128)(2,1)S(1)} collective-permute-done((bf16[2,6,16,64]{3,2,1,0:T(8,128)(2,1)S(1)}, bf16[2,6,16,64]{3,2,1,0:T(8,128)(2,1)S(1)}, u32[]{:S(2)}, u32[]{:S(2)}) %collective-permute-start.22) | collective-permute-done | bytes 24608 | tf_op jit(solution)/shard_map/ppermute | solution.py:61
  13.8 0.0 collective-permute-done.20.there_ref
  13.8 1.4 %pick.6 = (s32[15]{0:T(128)S(1)}, f32[1,256]{1,0:T(1,128)S(1)}, bf16[16,64,256]{2,1,0:T(8,128)(2,1)S(1)}, bf16[16,64,256]{2,1,0:T(8,128)(2,1)S(1)}) custom-call(s32[4]{0:T(128)S(1)} %copy-done.2, s32[3]{0:T(128)S(1)} %pad_add_fusion.place_ref, bf16[16,64,256]{2,1,0:T(8,128)(2,1)S(1)} %get-tuple-element.102.here_ref, ...), custom_call_target="tpu_custom_call" | custom-call | tf_op jit(solution)/shard_map/pick/pallas_call | solution.py:176
  15.2 0.6 slice.6
  16.4 0.3 collective-permute-start.27
  16.7 0.1 collective-permute-start.29
  16.8 1.9 %collective-permute-done.24.refs_0_.refs_2_ = bf16[16,64,256]{2,1,0:T(8,128)(2,1)S(1)} collective-permute-done((bf16[16,64,256]{2,1,0:T(8,128)(2,1)S(1)}, bf16[16,64,256]{2,1,0:T(8,128)(2,1)S(1)}, u32[]{:S(2)}, u32[]{:S(2)}) %collective-permute-start.24) | collective-permute-done | bytes 524320 | tf_op jit(solution)/shard_map/ppermute | solution.py:61
  18.8 0.8 %collective-permute-done.25.refs_1_.refs_3_ = bf16[16,64,256]{2,1,0:T(8,128)(2,1)S(1)} collective-permute-done((bf16[16,64,256]{2,1,0:T(8,128)(2,1)S(1)}, bf16[16,64,256]{2,1,0:T(8,128)(2,1)S(1)}, u32[]{:S(2)}, u32[]{:S(2)}) %collective-permute-start.25) | collective-permute-done | bytes 524320 | tf_op jit(solution)/shard_map/ppermute | solution.py:61
  19.6 0.0 copy-start
  19.6 2.4 %collective-permute-start.26 = (bf16[2,12,16,64]{3,2,1,0:T(8,128)(2,1)S(1)}, bf16[2,12,16,64]{3,2,1,0:T(8,128)(2,1)S(1)}, u32[]{:S(2)}, u32[]{:S(2)}) collective-permute-start(bf16[2,12,16,64]{3,2,1,0:T(8,128)(2,1)S(1)} %hand_on.3), channel_id=1, source_target_pairs={{0,2},{1,3},{2,0},{3,1},{4,6},{5,7},{6,4},{7,5},{8,10},{9,11},{10,... | collective-permute-start | bytes 147464 | tf_op jit(solution)/shard_map/ppermute | solution.py:400
  22.0 0.1 broadcast_select_fusion.4
  22.1 0.4 collective-permute-start.33
  22.5 1.2 %collective-permute-start.34 = (bf16[16,64,256]{2,1,0:T(8,128)(2,1)S(1)}, bf16[16,64,256]{2,1,0:T(8,128)(2,1)S(1)}, u32[]{:S(2)}, u32[]{:S(2)}) collective-permute-start(bf16[16,64,256]{2,1,0:T(8,128)(2,1)S(1)} %get-tuple-element.103), channel_id=1, source_target_pairs={{0,16},{4,20},{8,24},{12,28},{16,0},{20,4},{24,8},{28,12},{1,17},{... | collective-permute-start | bytes 1572872 | tf_op jit(solution)/shard_map/ppermute | solution.py:61
  23.7 0.3 collective-permute-done.26
  24.1 0.1 fusion.7.taps_ref
  24.1 8.3 %bands.3 = (bf16[4096,1536]{1,0:T(8,128)(2,1)S(1)}, f32[1,256]{1,0:T(1,128)S(1)}) custom-call(s32[3]{0:T(128)S(1)} %pad_add_fusion.place_ref, f32[4,12,16,128]{3,2,1,0:T(8,128)S(1)} %fusion.7.taps_ref, f32[1,256]{1,0:T(1,128)S(1)} %get-tuple-element.67.full_ref), custom_call_target="tpu_custom_call" | custom-call | flops 50331648 | bytes 12582912 | tf_op jit(solution)/shard_map/bands/pallas_call | solution.py:83
  32.5 0.6 cut.3
  33.1 3.8 %collective-permute-start.31 = (bf16[6,128,256]{2,1,0:T(8,128)(2,1)S(1)}, bf16[6,128,256]{2,1,0:T(8,128)(2,1)S(1)}, u32[]{:S(2)}, u32[]{:S(2)}) collective-permute-start(bf16[6,128,256]{2,1,0:T(8,128)(2,1)S(1)} %cut.3), channel_id=1, source_target_pairs={{0,4},{4,0},{8,12},{12,8},{16,20},{20,16},{24,28},{28,24},{1,5},{5... | collective-permute-start | bytes 1179656 | tf_op jit(solution)/shard_map/ppermute | solution.py:61
  36.9 0.0 collective-permute-done.27.refs_3_
  36.9 0.0 collective-permute-done.29.refs_2_
  36.9 0.1 broadcast_select_fusion.6
  37.0 0.6 collective-permute-start.28
  37.6 1.0 %collective-permute-start.30 = (bf16[16,64,256]{2,1,0:T(8,128)(2,1)S(1)}, bf16[16,64,256]{2,1,0:T(8,128)(2,1)S(1)}, u32[]{:S(2)}, u32[]{:S(2)}) collective-permute-start(bf16[16,64,256]{2,1,0:T(8,128)(2,1)S(1)} %get-tuple-element.105), channel_id=1, source_target_pairs={{0,16},{4,20},{8,24},{12,28},{16,0},{20,4},{24,8},{28,12},{1,17},{... | collective-permute-start | bytes 1572872 | tf_op jit(solution)/shard_map/ppermute | solution.py:61
  38.6 3.5 %early_sum.7.refs_3_ = f32[12,64,256]{2,1,0:T(8,128)S(1)} custom-call(s32[15]{0:T(128)S(1)} %get-tuple-element.64.plan_ref, s32[3]{0:T(128)S(1)} %pad_add_fusion.place_ref, bf16[16,64,256]{2,1,0:T(8,128)(2,1)S(1)} %get-tuple-element.65.refs_0_, bf16[16,64,256]{2,1,0:T(8,128)(2,1)S(1)} %get-tuple-element.66.refs_1_, ...), custom_call_target="tpu_custom_call" | custom-call | flops 3221225472 | bytes 12582912 | tf_op jit(solution)/shard_map/early_sum/pallas_call | solution.py:327
  42.1 3.5 %early_sum.6.refs_3_ = f32[12,64,256]{2,1,0:T(8,128)S(1)} custom-call(s32[15]{0:T(128)S(1)} %get-tuple-element.64.plan_ref, s32[3]{0:T(128)S(1)} %pad_add_fusion.place_ref, bf16[16,64,256]{2,1,0:T(8,128)(2,1)S(1)} %get-tuple-element.70.refs_0_, bf16[16,64,256]{2,1,0:T(8,128)(2,1)S(1)} %get-tuple-element.69.refs_1_, ...), custom_call_target="tpu_custom_call" | custom-call | flops 3221225472 | bytes 12582912 | tf_op jit(solution)/shard_map/early_sum/pallas_call | solution.py:327
  45.7 0.0 collective-permute-done.33.refs_0_
  45.7 0.0 collective-permute-done.34.refs_1_
  45.7 3.4 %residual.7 = (bf16[6,64,256]{2,1,0:T(8,128)(2,1)S(1)}, bf16[6,64,256]{2,1,0:T(8,128)(2,1)S(1)}) custom-call(s32[15]{0:T(128)S(1)} %get-tuple-element.64.plan_ref, s32[3]{0:T(128)S(1)} %pad_add_fusion.place_ref, bf16[16,64,256]{2,1,0:T(8,128)(2,1)S(1)} %collective-permute-done.33.refs_0_, bf16[16,64,256]{2,1,0:T(8,128)(2,1)S(1)} %collective-permute-done.34.refs_1_, ...), custom_call_target="tpu_custom_call" | custom-call | flops 1610612736 | bytes 6291456 | tf_op jit(solution)/shard_map/residual/pallas_call | solution.py:327
  49.1 0.7 %collective-permute-start.35 = (bf16[6,64,256]{2,1,0:T(8,128)(2,1)S(1)}, bf16[6,64,256]{2,1,0:T(8,128)(2,1)S(1)}, u32[]{:S(2)}, u32[]{:S(2)}) collective-permute-start(bf16[6,64,256]{2,1,0:T(8,128)(2,1)S(1)} %get-tuple-element.75), channel_id=1, source_target_pairs={{0,4},{4,0},{8,12},{12,8},{16,20},{20,16},{24,28},{28,24},{1,5},{5... | collective-permute-start | bytes 589832 | tf_op jit(solution)/shard_map/ppermute | solution.py:61
  49.8 2.2 %collective-permute-done.28.refs_0_ = bf16[16,64,256]{2,1,0:T(8,128)(2,1)S(1)} collective-permute-done((bf16[16,64,256]{2,1,0:T(8,128)(2,1)S(1)}, bf16[16,64,256]{2,1,0:T(8,128)(2,1)S(1)}, u32[]{:S(2)}, u32[]{:S(2)}) %collective-permute-start.28) | collective-permute-done | bytes 524320 | tf_op jit(solution)/shard_map/ppermute | solution.py:61
  52.0 1.3 %collective-permute-done.30.refs_1_ = bf16[16,64,256]{2,1,0:T(8,128)(2,1)S(1)} collective-permute-done((bf16[16,64,256]{2,1,0:T(8,128)(2,1)S(1)}, bf16[16,64,256]{2,1,0:T(8,128)(2,1)S(1)}, u32[]{:S(2)}, u32[]{:S(2)}) %collective-permute-start.30) | collective-permute-done | bytes 524320 | tf_op jit(solution)/shard_map/ppermute | solution.py:61
  53.3 3.4 %residual.6 = (bf16[6,64,256]{2,1,0:T(8,128)(2,1)S(1)}, bf16[6,64,256]{2,1,0:T(8,128)(2,1)S(1)}) custom-call(s32[15]{0:T(128)S(1)} %get-tuple-element.64.plan_ref, s32[3]{0:T(128)S(1)} %pad_add_fusion.place_ref, bf16[16,64,256]{2,1,0:T(8,128)(2,1)S(1)} %collective-permute-done.28.refs_0_, bf16[16,64,256]{2,1,0:T(8,128)(2,1)S(1)} %collective-permute-done.30.refs_1_, ...), custom_call_target="tpu_custom_call" | custom-call | flops 1610612736 | bytes 6291456 | tf_op jit(solution)/shard_map/residual/pallas_call | solution.py:327
  56.7 1.6 %collective-permute-start.32 = (bf16[6,64,256]{2,1,0:T(8,128)(2,1)S(1)}, bf16[6,64,256]{2,1,0:T(8,128)(2,1)S(1)}, u32[]{:S(2)}, u32[]{:S(2)}) collective-permute-start(bf16[6,64,256]{2,1,0:T(8,128)(2,1)S(1)} %get-tuple-element.72), channel_id=1, source_target_pairs={{0,4},{4,0},{8,12},{12,8},{16,20},{20,16},{24,28},{28,24},{1,5},{5... | collective-permute-start | bytes 589832 | tf_op jit(solution)/shard_map/ppermute | solution.py:61
  58.3 0.0 collective-permute-done.35.refs_2_
  58.3 1.4 %assemble.6.refs_1_ = bf16[6,256,256]{2,1,0:T(8,128)(2,1)} custom-call(s32[3]{0:T(128)S(1)} %pad_add_fusion.place_ref, bf16[6,64,256]{2,1,0:T(8,128)(2,1)S(1)} %get-tuple-element.73.refs_0_, bf16[6,64,256]{2,1,0:T(8,128)(2,1)S(1)} %get-tuple-element.74.refs_1_, bf16[6,64,256]{2,1,0:T(8,128)(2,1)S(1)} %collective-permute-done.35.refs_2_), custom_call_target="tpu_custom_call" | custom-call | tf_op jit(solution)/shard_map/assemble/pallas_call | solution.py:365
  59.7 1.2 %assemble.7 = bf16[6,256,256]{2,1,0:T(8,128)(2,1)} custom-call(s32[3]{0:T(128)S(1)} %pad_add_fusion.place_ref, bf16[6,64,256]{2,1,0:T(8,128)(2,1)S(1)} %collective-permute-done.32.refs_0_, bf16[6,256,256]{2,1,0:T(8,128)(2,1)} %assemble.6.refs_1_), custom_call_target="tpu_custom_call", output_to_operand_aliasing={{}: (2, {})} | custom-call | tf_op jit(solution)/shard_map/assemble/pallas_call | solution.py:365
  60.9 0.2 while.9
  (12 shorter events, 0.1 us)
Async XLA Ops:
  0.0 3.7 %copy-start.2 = (s32[4]{0:T(128)S(1)}, s32[4]{0:T(128)}, u32[]{:S(2)}) copy-start(s32[4]{0:T(128)} %owner_ref.3) | copy-start | bytes 52
  0.0 8.0 %copy-start.1 = (bf16[6,16,64]{2,1,0:T(8,128)(2,1)S(1)}, bf16[6,16,64]{2,1,0:T(8,128)(2,1)}, u32[]{:S(2)}) copy-start(bf16[6,16,64]{2,1,0:T(8,128)(2,1)} %param.8) | copy-start | bytes 36868
  1.7 2.0 %collective-permute-start.23 = (bf16[16,64,256]{2,1,0:T(8,128)(2,1)S(1)}, bf16[16,64,256]{2,1,0:T(8,128)(2,1)S(1)}, u32[]{:S(2)}, u32[]{:S(2)}) collective-permute-start(bf16[16,64,256]{2,1,0:T(8,128)(2,1)S(1)} %get-tuple-element.99), channel_id=1, source_target_pairs={{0,4},{4,0},{8,12},{12,8},{16,20},{20,16},{24,28},{28,24},{1,5},{5... | collective-permute-start | bytes 1572872 | tf_op jit(solution)/shard_map/ppermute | solution.py:61
  1.8 11.9 %collective-permute-start.20 = (bf16[16,64,256]{2,1,0:T(8,128)(2,1)S(1)}, bf16[16,64,256]{2,1,0:T(8,128)(2,1)S(1)}, u32[]{:S(2)}, u32[]{:S(2)}) collective-permute-start(bf16[16,64,256]{2,1,0:T(8,128)(2,1)S(1)} %get-tuple-element.101), channel_id=1, source_target_pairs={{0,4},{4,0},{8,12},{12,8},{16,20},{20,16},{24,28},{28,24},{1,5},{5... | collective-permute-start | bytes 1572872 | tf_op jit(solution)/shard_map/ppermute | solution.py:61
  4.4 14.4 %collective-permute-start.24 = (bf16[16,64,256]{2,1,0:T(8,128)(2,1)S(1)}, bf16[16,64,256]{2,1,0:T(8,128)(2,1)S(1)}, u32[]{:S(2)}, u32[]{:S(2)}) collective-permute-start(bf16[16,64,256]{2,1,0:T(8,128)(2,1)S(1)} %get-tuple-element.65.refs_0_), channel_id=1, source_target_pairs={{0,8},{4,12},{8,0},{12,4},{16,24},{20,28},{24,16},{28,20},{1,9},{5... | collective-permute-start | bytes 1572872 | tf_op jit(solution)/shard_map/ppermute | solution.py:61
  6.8 12.8 %collective-permute-start.25 = (bf16[16,64,256]{2,1,0:T(8,128)(2,1)S(1)}, bf16[16,64,256]{2,1,0:T(8,128)(2,1)S(1)}, u32[]{:S(2)}, u32[]{:S(2)}) collective-permute-start(bf16[16,64,256]{2,1,0:T(8,128)(2,1)S(1)} %get-tuple-element.66.refs_1_), channel_id=1, source_target_pairs={{0,16},{4,20},{8,24},{12,28},{16,0},{20,4},{24,8},{28,12},{1,17},{... | collective-permute-start | bytes 1572872 | tf_op jit(solution)/shard_map/ppermute | solution.py:61
  8.0 3.0 %collective-permute-start.21 = (bf16[6,16,64]{2,1,0:T(8,128)(2,1)S(1)}, bf16[6,16,64]{2,1,0:T(8,128)(2,1)S(1)}, u32[]{:S(2)}, u32[]{:S(2)}) collective-permute-start(bf16[6,16,64]{2,1,0:T(8,128)(2,1)S(1)} %copy-done.1), channel_id=1, source_target_pairs={{0,1},{1,0},{2,3},{3,2},{4,5},{5,4},{6,7},{7,6},{8,9},{9,8},{10,11... | collective-permute-start | bytes 36872 | tf_op jit(solution)/shard_map/ppermute | solution.py:385
  11.0 2.7 %collective-permute-start.22 = (bf16[2,6,16,64]{3,2,1,0:T(8,128)(2,1)S(1)}, bf16[2,6,16,64]{3,2,1,0:T(8,128)(2,1)S(1)}, u32[]{:S(2)}, u32[]{:S(2)}) collective-permute-start(bf16[2,6,16,64]{3,2,1,0:T(8,128)(2,1)S(1)} %pad_maximum_fusion.3), channel_id=1, source_target_pairs={{0,4},{4,0},{8,12},{12,8},{16,20},{20,16},{24,28},{28,24},{1,5},{5... | collective-permute-start | bytes 73736 | tf_op jit(solution)/shard_map/ppermute | solution.py:61
  16.4 20.5 %collective-permute-start.27 = (bf16[16,64,256]{2,1,0:T(8,128)(2,1)S(1)}, bf16[16,64,256]{2,1,0:T(8,128)(2,1)S(1)}, u32[]{:S(2)}, u32[]{:S(2)}) collective-permute-start(bf16[16,64,256]{2,1,0:T(8,128)(2,1)S(1)} %get-tuple-element.69.refs_1_), channel_id=1, source_target_pairs={{0,16},{4,20},{8,24},{12,28},{16,0},{20,4},{24,8},{28,12},{1,17},{... | collective-permute-start | bytes 1572872 | tf_op jit(solution)/shard_map/ppermute | solution.py:61
  16.7 20.2 %collective-permute-start.29 = (bf16[16,64,256]{2,1,0:T(8,128)(2,1)S(1)}, bf16[16,64,256]{2,1,0:T(8,128)(2,1)S(1)}, u32[]{:S(2)}, u32[]{:S(2)}) collective-permute-start(bf16[16,64,256]{2,1,0:T(8,128)(2,1)S(1)} %get-tuple-element.70.refs_0_), channel_id=1, source_target_pairs={{0,8},{4,12},{8,0},{12,4},{16,24},{20,28},{24,16},{28,20},{1,9},{5... | collective-permute-start | bytes 1572872 | tf_op jit(solution)/shard_map/ppermute | solution.py:61
  19.6 12.8 %copy-start = (bf16[6,256,256]{2,1,0:T(8,128)(2,1)S(1)}, bf16[6,256,256]{2,1,0:T(8,128)(2,1)}, u32[]{:S(2)}) copy-start(bf16[6,256,256]{2,1,0:T(8,128)(2,1)} %refs_4_.3) | copy-start | bytes 2359300
  19.6 4.4 %collective-permute-start.26 = (bf16[2,12,16,64]{3,2,1,0:T(8,128)(2,1)S(1)}, bf16[2,12,16,64]{3,2,1,0:T(8,128)(2,1)S(1)}, u32[]{:S(2)}, u32[]{:S(2)}) collective-permute-start(bf16[2,12,16,64]{3,2,1,0:T(8,128)(2,1)S(1)} %hand_on.3), channel_id=1, source_target_pairs={{0,2},{1,3},{2,0},{3,1},{4,6},{5,7},{6,4},{7,5},{8,10},{9,11},{10,... | collective-permute-start | bytes 147464 | tf_op jit(solution)/shard_map/ppermute | solution.py:400
  22.1 23.5 %collective-permute-start.33 = (bf16[16,64,256]{2,1,0:T(8,128)(2,1)S(1)}, bf16[16,64,256]{2,1,0:T(8,128)(2,1)S(1)}, u32[]{:S(2)}, u32[]{:S(2)}) collective-permute-start(bf16[16,64,256]{2,1,0:T(8,128)(2,1)S(1)} %get-tuple-element.104), channel_id=1, source_target_pairs={{0,8},{4,12},{8,0},{12,4},{16,24},{20,28},{24,16},{28,20},{1,9},{5... | collective-permute-start | bytes 1572872 | tf_op jit(solution)/shard_map/ppermute | solution.py:61
  22.5 23.2 %collective-permute-start.34 = (bf16[16,64,256]{2,1,0:T(8,128)(2,1)S(1)}, bf16[16,64,256]{2,1,0:T(8,128)(2,1)S(1)}, u32[]{:S(2)}, u32[]{:S(2)}) collective-permute-start(bf16[16,64,256]{2,1,0:T(8,128)(2,1)S(1)} %get-tuple-element.103), channel_id=1, source_target_pairs={{0,16},{4,20},{8,24},{12,28},{16,0},{20,4},{24,8},{28,12},{1,17},{... | collective-permute-start | bytes 1572872 | tf_op jit(solution)/shard_map/ppermute | solution.py:61
  33.1 12.6 %collective-permute-start.31 = (bf16[6,128,256]{2,1,0:T(8,128)(2,1)S(1)}, bf16[6,128,256]{2,1,0:T(8,128)(2,1)S(1)}, u32[]{:S(2)}, u32[]{:S(2)}) collective-permute-start(bf16[6,128,256]{2,1,0:T(8,128)(2,1)S(1)} %cut.3), channel_id=1, source_target_pairs={{0,4},{4,0},{8,12},{12,8},{16,20},{20,16},{24,28},{28,24},{1,5},{5... | collective-permute-start | bytes 1179656 | tf_op jit(solution)/shard_map/ppermute | solution.py:61
  37.0 15.0 %collective-permute-start.28 = (bf16[16,64,256]{2,1,0:T(8,128)(2,1)S(1)}, bf16[16,64,256]{2,1,0:T(8,128)(2,1)S(1)}, u32[]{:S(2)}, u32[]{:S(2)}) collective-permute-start(bf16[16,64,256]{2,1,0:T(8,128)(2,1)S(1)} %get-tuple-element.106), channel_id=1, source_target_pairs={{0,8},{4,12},{8,0},{12,4},{16,24},{20,28},{24,16},{28,20},{1,9},{5... | collective-permute-start | bytes 1572872 | tf_op jit(solution)/shard_map/ppermute | solution.py:61
  37.6 15.7 %collective-permute-start.30 = (bf16[16,64,256]{2,1,0:T(8,128)(2,1)S(1)}, bf16[16,64,256]{2,1,0:T(8,128)(2,1)S(1)}, u32[]{:S(2)}, u32[]{:S(2)}) collective-permute-start(bf16[16,64,256]{2,1,0:T(8,128)(2,1)S(1)} %get-tuple-element.105), channel_id=1, source_target_pairs={{0,16},{4,20},{8,24},{12,28},{16,0},{20,4},{24,8},{28,12},{1,17},{... | collective-permute-start | bytes 1572872 | tf_op jit(solution)/shard_map/ppermute | solution.py:61
  49.1 9.2 %collective-permute-start.35 = (bf16[6,64,256]{2,1,0:T(8,128)(2,1)S(1)}, bf16[6,64,256]{2,1,0:T(8,128)(2,1)S(1)}, u32[]{:S(2)}, u32[]{:S(2)}) collective-permute-start(bf16[6,64,256]{2,1,0:T(8,128)(2,1)S(1)} %get-tuple-element.75), channel_id=1, source_target_pairs={{0,4},{4,0},{8,12},{12,8},{16,20},{20,16},{24,28},{28,24},{1,5},{5... | collective-permute-start | bytes 589832 | tf_op jit(solution)/shard_map/ppermute | solution.py:61
  56.7 3.0 %collective-permute-start.32 = (bf16[6,64,256]{2,1,0:T(8,128)(2,1)S(1)}, bf16[6,64,256]{2,1,0:T(8,128)(2,1)S(1)}, u32[]{:S(2)}, u32[]{:S(2)}) collective-permute-start(bf16[6,64,256]{2,1,0:T(8,128)(2,1)S(1)} %get-tuple-element.72), channel_id=1, source_target_pairs={{0,4},{4,0},{8,12},{12,8},{16,20},{20,16},{24,28},{28,24},{1,5},{5... | collective-permute-start | bytes 589832 | tf_op jit(solution)/shard_map/ppermute | solution.py:61

commit v8 on v7

--- a/solution.py
+++ b/solution.py
@@ -387,7 +387,12 @@
     blocks = jnp.concatenate([blocks, flip(blocks, CORE)], axis=1)
     own_a, own_b = [], []
     for chunk in range(CHUNKS):
-        here, there = (lax.dynamic_slice_in_dim(surface_traces, at * side + chunk * rows, rows, axis=1) for at in (core, 1 - core))
+        here = lax.dynamic_slice_in_dim(surface_traces, core * side + chunk * rows, rows, axis=1)
+        if chunk == 0:
+            apart = surface_traces.reshape(surface_traces.shape[0], 2 * CHUNKS, rows, -1)
+            there = lax.dynamic_index_in_dim(apart, (1 - core) * CHUNKS, axis=1, keepdims=False)
+        else:
+            there = lax.dynamic_slice_in_dim(surface_traces, (1 - core) * side + chunk * rows, rows, axis=1)
         *extra, a, b = pick(chunk, panel_owner, place, here, flip(there, CORE), [ahead] if own_a else [])
         if extra:
             plan, full = extra

time: 61.4 us -> 59.7 us (0.972)
  waiting for transfers between devices: 10.5 us -> 7.58 us
  local copies, waits for them, and re-layouts: 2.31 us -> 3.17 us
    ppermute x14, waiting for transfers between devices: 8.54 us -> 5.57 us  [flip(): return lax.ppermute(value, 'shot', [(i, i ^ bit) for i in range(SQUARE)])]
    squeeze x0 -> x1, local copies, waits for them, and re-layouts: none -> 1.09 us  [exchange(): lax.dynamic_index_in_dim(apart, (1 - core) * CHUNKS, axis=1, keepdims=False)]
  transfers between devices with their start and end apart: 16 -> 16, of which waited for: 8 -> 7; matrix products, arithmetic and copies ran while one was open for 2% -> 4% of each run, Pallas kernels for 43% -> 44%
where the time goes in v8:
time: 59.7 us; the launch traced here: 59.6 us
  Pallas kernels  27.4 us (46%)
  starting transfers between devices  19.8 us (33%)
  waiting for transfers between devices  7.58 us (13%)
  local copies, waits for them, and re-layouts  3.17 us (5%)
  between operations  1 us (2%)
    ppermute x14, starting transfers between devices, flip(): return lax.ppermute(value, 'shot', [(i, i ^ bit) for i in range(SQUARE)])  16.2 us
    pallas_call x4, Pallas kernels, sum_of(): pl.pallas_call(functools.partial(sum_kernel, last), out_shape=out_shape,...  13.8 us
    pallas_call x1, Pallas kernels, bands_of(): pl.pallas_call(band_kernel, out_shape=(jax.ShapeDtypeStruct((panels * hei...  8.32 us
    ppermute x14, waiting for transfers between devices, flip(): return lax.ppermute(value, 'shot', [(i, i ^ bit) for i in range(SQUARE)])  5.57 us
    pallas_call x2, Pallas kernels, assemble(): pl.pallas_call(functools.partial(assemble_kernel, at), out_shape=pltpu.HB...  2.61 us
    ppermute x1, starting transfers between devices, exchange(): lax.ppermute(blocks, 'rcv', [(i, i ^ bit) for i in range(ring)])  2.37 us
    pallas_call x2, Pallas kernels, pick(): pl.pallas_call(functools.partial(pick_kernel, chunk), out_shape=tuple(out...  2.04 us
    ppermute x1, waiting for transfers between devices, exchange(): ahead = lax.ppermute(primaries, 'rcv', [(i, i ^ 1) for i in range(ring)])  1.68 us
  transfers between devices with their start and end apart: 16, of which 7 were waited for; matrix products, arithmetic and copies ran while one was open for 4% of the time, Pallas kernels for 44%

profile of v8, /device:TPU:1, one launch (start us, length us, event | category | flops | bytes accessed | tf_op | source)
XLA Modules:
  0.0 59.6 jit_solution(18227218600515737908)
XLA Ops:
  0.0 1.1 %dynamic-slice_bitcast_fusion.1 = bf16[16,64,256]{2,1,0:T(8,128)(2,1)S(1)} fusion(bf16[16,4,64,256]{3,2,1,0:T(8,128)(2,1)} %bitcast.10, s32[]{:T(128)S(6)} %select_n.68), kind=kLoop, calls=%fused_computation.17 | loop fusion | bytes 1048580 | tf_op jit(solution)/shard_map/jit(dynamic_index_in_dim)/squeeze | solution.py:393
  1.1 0.1 collective-permute-start.23
  1.2 1.5 %constant_dynamic-slice_fusion.3 = (bf16[16,64,256]{2,1,0:T(8,128)(2,1)S(1)}, bf16[16,64,256]{2,1,0:T(8,128)(2,1)S(1)}, bf16[16,64,256]{2,1,0:T(8,128)(2,1)S(1)}) fusion(bf16[16,256,256]{2,1,0:T(8,128)(2,1)} %param.7, s32[]{:T(128)S(6)} %select_n.67, s32[]{:T(128)S(6)} %select_n.66, s32[]{:T(128)S(6)} %select_n.65), kind=kLoop, calls=%fused_computation.31 | loop fusion | bytes 3145740 | tf_op jit(solution)/shard_map/dynamic_slice | solution.py:390
  2.7 0.5 collective-permute-start.20
  3.2 0.1 pad_add_fusion.place_ref
  3.3 0.0 collective-permute-done.23.there_ref
  3.3 0.7 %pick.7 = (bf16[16,64,256]{2,1,0:T(8,128)(2,1)S(1)}, bf16[16,64,256]{2,1,0:T(8,128)(2,1)S(1)}) custom-call(s32[4]{0:T(128)S(1)} %copy-done.2, s32[3]{0:T(128)S(1)} %pad_add_fusion.place_ref, bf16[16,64,256]{2,1,0:T(8,128)(2,1)S(1)} %get-tuple-element.98.here_ref, bf16[16,64,256]{2,1,0:T(8,128)(2,1)S(1)} %collective-permute-done.23.there_ref), custom_call_target="tpu_custom_call" | custom-call | tf_op jit(solution)/shard_map/pick/pallas_call | solution.py:176
  4.0 2.3 %collective-permute-start.24 = (bf16[16,64,256]{2,1,0:T(8,128)(2,1)S(1)}, bf16[16,64,256]{2,1,0:T(8,128)(2,1)S(1)}, u32[]{:S(2)}, u32[]{:S(2)}) collective-permute-start(bf16[16,64,256]{2,1,0:T(8,128)(2,1)S(1)} %get-tuple-element.65.refs_0_), channel_id=1, source_target_pairs={{0,8},{4,12},{8,0},{12,4},{16,24},{20,28},{24,16},{28,20},{1,9},{5... | collective-permute-start | bytes 1572872 | tf_op jit(solution)/shard_map/ppermute | solution.py:61
  6.3 1.2 %collective-permute-start.25 = (bf16[16,64,256]{2,1,0:T(8,128)(2,1)S(1)}, bf16[16,64,256]{2,1,0:T(8,128)(2,1)S(1)}, u32[]{:S(2)}, u32[]{:S(2)}) collective-permute-start(bf16[16,64,256]{2,1,0:T(8,128)(2,1)S(1)} %get-tuple-element.66.refs_1_), channel_id=1, source_target_pairs={{0,16},{4,20},{8,24},{12,28},{16,0},{20,4},{24,8},{28,12},{1,17},{... | collective-permute-start | bytes 1572872 | tf_op jit(solution)/shard_map/ppermute | solution.py:61
  7.5 1.3 %collective-permute-start.21 = (bf16[6,16,64]{2,1,0:T(8,128)(2,1)S(1)}, bf16[6,16,64]{2,1,0:T(8,128)(2,1)S(1)}, u32[]{:S(2)}, u32[]{:S(2)}) collective-permute-start(bf16[6,16,64]{2,1,0:T(8,128)(2,1)S(1)} %copy-done.1), channel_id=1, source_target_pairs={{0,1},{1,0},{2,3},{3,2},{4,5},{5,4},{6,7},{7,6},{8,9},{9,8},{10,11... | collective-permute-start | bytes 36872 | tf_op jit(solution)/shard_map/ppermute | solution.py:385
  8.8 1.7 %collective-permute-done.21.refs_0_ = bf16[6,16,64]{2,1,0:T(8,128)(2,1)S(1)} collective-permute-done((bf16[6,16,64]{2,1,0:T(8,128)(2,1)S(1)}, bf16[6,16,64]{2,1,0:T(8,128)(2,1)S(1)}, u32[]{:S(2)}, u32[]{:S(2)}) %collective-permute-start.21) | collective-permute-done | bytes 12320 | tf_op jit(solution)/shard_map/ppermute | solution.py:385
  10.5 1.9 %collective-permute-start.22 = (bf16[2,6,16,64]{3,2,1,0:T(8,128)(2,1)S(1)}, bf16[2,6,16,64]{3,2,1,0:T(8,128)(2,1)S(1)}, u32[]{:S(2)}, u32[]{:S(2)}) collective-permute-start(bf16[2,6,16,64]{3,2,1,0:T(8,128)(2,1)S(1)} %pad_maximum_fusion.3), channel_id=1, source_target_pairs={{0,4},{4,0},{8,12},{12,8},{16,20},{20,16},{24,28},{28,24},{1,5},{5... | collective-permute-start | bytes 73736 | tf_op jit(solution)/shard_map/ppermute | solution.py:61
  12.5 0.9 %collective-permute-done.22 = bf16[2,6,16,64]{3,2,1,0:T(8,128)(2,1)S(1)} collective-permute-done((bf16[2,6,16,64]{3,2,1,0:T(8,128)(2,1)S(1)}, bf16[2,6,16,64]{3,2,1,0:T(8,128)(2,1)S(1)}, u32[]{:S(2)}, u32[]{:S(2)}) %collective-permute-start.22) | collective-permute-done | bytes 24608 | tf_op jit(solution)/shard_map/ppermute | solution.py:61
  13.4 0.0 collective-permute-done.20.there_ref
  13.4 1.4 %pick.6 = (s32[15]{0:T(128)S(1)}, f32[1,256]{1,0:T(1,128)S(1)}, bf16[16,64,256]{2,1,0:T(8,128)(2,1)S(1)}, bf16[16,64,256]{2,1,0:T(8,128)(2,1)S(1)}) custom-call(s32[4]{0:T(128)S(1)} %copy-done.2, s32[3]{0:T(128)S(1)} %pad_add_fusion.place_ref, bf16[16,64,256]{2,1,0:T(8,128)(2,1)S(1)} %get-tuple-element.100.here_ref, ...), custom_call_target="tpu_custom_call" | custom-call | tf_op jit(solution)/shard_map/pick/pallas_call | solution.py:176
  14.8 0.6 slice.6
  16.0 0.3 collective-permute-start.27
  16.3 0.1 collective-permute-start.29
  16.4 1.7 %collective-permute-done.24.refs_0_.refs_2_ = bf16[16,64,256]{2,1,0:T(8,128)(2,1)S(1)} collective-permute-done((bf16[16,64,256]{2,1,0:T(8,128)(2,1)S(1)}, bf16[16,64,256]{2,1,0:T(8,128)(2,1)S(1)}, u32[]{:S(2)}, u32[]{:S(2)}) %collective-permute-start.24) | collective-permute-done | bytes 524320 | tf_op jit(solution)/shard_map/ppermute | solution.py:61
  18.2 0.8 %collective-permute-done.25.refs_1_.refs_3_ = bf16[16,64,256]{2,1,0:T(8,128)(2,1)S(1)} collective-permute-done((bf16[16,64,256]{2,1,0:T(8,128)(2,1)S(1)}, bf16[16,64,256]{2,1,0:T(8,128)(2,1)S(1)}, u32[]{:S(2)}, u32[]{:S(2)}) %collective-permute-start.25) | collective-permute-done | bytes 524320 | tf_op jit(solution)/shard_map/ppermute | solution.py:61
  19.0 0.0 copy-start
  19.0 2.4 %collective-permute-start.26 = (bf16[2,12,16,64]{3,2,1,0:T(8,128)(2,1)S(1)}, bf16[2,12,16,64]{3,2,1,0:T(8,128)(2,1)S(1)}, u32[]{:S(2)}, u32[]{:S(2)}) collective-permute-start(bf16[2,12,16,64]{3,2,1,0:T(8,128)(2,1)S(1)} %hand_on.3), channel_id=1, source_target_pairs={{0,2},{1,3},{2,0},{3,1},{4,6},{5,7},{6,4},{7,5},{8,10},{9,11},{10,... | collective-permute-start | bytes 147464 | tf_op jit(solution)/shard_map/ppermute | solution.py:405
  21.4 0.1 broadcast_select_fusion.4
  21.5 0.4 collective-permute-start.33
  21.9 1.2 %collective-permute-start.34 = (bf16[16,64,256]{2,1,0:T(8,128)(2,1)S(1)}, bf16[16,64,256]{2,1,0:T(8,128)(2,1)S(1)}, u32[]{:S(2)}, u32[]{:S(2)}) collective-permute-start(bf16[16,64,256]{2,1,0:T(8,128)(2,1)S(1)} %get-tuple-element.101), channel_id=1, source_target_pairs={{0,16},{4,20},{8,24},{12,28},{16,0},{20,4},{24,8},{28,12},{1,17},{... | collective-permute-start | bytes 1572872 | tf_op jit(solution)/shard_map/ppermute | solution.py:61
  23.2 0.3 collective-permute-done.26
  23.5 0.1 fusion.7.taps_ref
  23.6 8.3 %bands.3 = (bf16[4096,1536]{1,0:T(8,128)(2,1)S(1)}, f32[1,256]{1,0:T(1,128)S(1)}) custom-call(s32[3]{0:T(128)S(1)} %pad_add_fusion.place_ref, f32[4,12,16,128]{3,2,1,0:T(8,128)S(1)} %fusion.7.taps_ref, f32[1,256]{1,0:T(1,128)S(1)} %get-tuple-element.67.full_ref), custom_call_target="tpu_custom_call" | custom-call | flops 50331648 | bytes 12582912 | tf_op jit(solution)/shard_map/bands/pallas_call | solution.py:83
  31.9 0.6 cut.3
  32.5 4.1 %collective-permute-start.31 = (bf16[6,128,256]{2,1,0:T(8,128)(2,1)S(1)}, bf16[6,128,256]{2,1,0:T(8,128)(2,1)S(1)}, u32[]{:S(2)}, u32[]{:S(2)}) collective-permute-start(bf16[6,128,256]{2,1,0:T(8,128)(2,1)S(1)} %cut.3), channel_id=1, source_target_pairs={{0,4},{4,0},{8,12},{12,8},{16,20},{20,16},{24,28},{28,24},{1,5},{5... | collective-permute-start | bytes 1179656 | tf_op jit(solution)/shard_map/ppermute | solution.py:61
  36.6 0.0 collective-permute-done.27.refs_3_
  36.6 0.1 broadcast_select_fusion.6
  36.7 0.6 collective-permute-start.28
  37.2 1.0 %collective-permute-start.30 = (bf16[16,64,256]{2,1,0:T(8,128)(2,1)S(1)}, bf16[16,64,256]{2,1,0:T(8,128)(2,1)S(1)}, u32[]{:S(2)}, u32[]{:S(2)}) collective-permute-start(bf16[16,64,256]{2,1,0:T(8,128)(2,1)S(1)} %get-tuple-element.103), channel_id=1, source_target_pairs={{0,16},{4,20},{8,24},{12,28},{16,0},{20,4},{24,8},{28,12},{1,17},{... | collective-permute-start | bytes 1572872 | tf_op jit(solution)/shard_map/ppermute | solution.py:61
  38.2 4.7 %early_sum.7.refs_3_ = f32[12,64,256]{2,1,0:T(8,128)S(1)} custom-call(s32[15]{0:T(128)S(1)} %get-tuple-element.64.plan_ref, s32[3]{0:T(128)S(1)} %pad_add_fusion.place_ref, bf16[16,64,256]{2,1,0:T(8,128)(2,1)S(1)} %get-tuple-element.65.refs_0_, bf16[16,64,256]{2,1,0:T(8,128)(2,1)S(1)} %get-tuple-element.66.refs_1_, ...), custom_call_target="tpu_custom_call" | custom-call | flops 3221225472 | bytes 12582912 | tf_op jit(solution)/shard_map/early_sum/pallas_call | solution.py:327
  43.0 4.7 %early_sum.6.refs_3_ = f32[12,64,256]{2,1,0:T(8,128)S(1)} custom-call(s32[15]{0:T(128)S(1)} %get-tuple-element.64.plan_ref, s32[3]{0:T(128)S(1)} %pad_add_fusion.place_ref, bf16[16,64,256]{2,1,0:T(8,128)(2,1)S(1)} %get-tuple-element.70.refs_0_, bf16[16,64,256]{2,1,0:T(8,128)(2,1)S(1)} %get-tuple-element.69.refs_1_, ...), custom_call_target="tpu_custom_call" | custom-call | flops 3221225472 | bytes 12582912 | tf_op jit(solution)/shard_map/early_sum/pallas_call | solution.py:327
  47.7 0.0 collective-permute-done.34.refs_1_
  47.7 2.2 %residual.7 = (bf16[6,64,256]{2,1,0:T(8,128)(2,1)S(1)}, bf16[6,64,256]{2,1,0:T(8,128)(2,1)S(1)}) custom-call(s32[15]{0:T(128)S(1)} %get-tuple-element.64.plan_ref, s32[3]{0:T(128)S(1)} %pad_add_fusion.place_ref, bf16[16,64,256]{2,1,0:T(8,128)(2,1)S(1)} %collective-permute-done.33.refs_0_, bf16[16,64,256]{2,1,0:T(8,128)(2,1)S(1)} %collective-permute-done.34.refs_1_, ...), custom_call_target="tpu_custom_call" | custom-call | flops 1610612736 | bytes 6291456 | tf_op jit(solution)/shard_map/residual/pallas_call | solution.py:327
  49.9 0.7 %collective-permute-start.35 = (bf16[6,64,256]{2,1,0:T(8,128)(2,1)S(1)}, bf16[6,64,256]{2,1,0:T(8,128)(2,1)S(1)}, u32[]{:S(2)}, u32[]{:S(2)}) collective-permute-start(bf16[6,64,256]{2,1,0:T(8,128)(2,1)S(1)} %get-tuple-element.75), channel_id=1, source_target_pairs={{0,4},{4,0},{8,12},{12,8},{16,20},{20,16},{24,28},{28,24},{1,5},{5... | collective-permute-start | bytes 589832 | tf_op jit(solution)/shard_map/ppermute | solution.py:61
  50.6 1.0 %collective-permute-done.28.refs_0_ = bf16[16,64,256]{2,1,0:T(8,128)(2,1)S(1)} collective-permute-done((bf16[16,64,256]{2,1,0:T(8,128)(2,1)S(1)}, bf16[16,64,256]{2,1,0:T(8,128)(2,1)S(1)}, u32[]{:S(2)}, u32[]{:S(2)}) %collective-permute-start.28) | collective-permute-done | bytes 524320 | tf_op jit(solution)/shard_map/ppermute | solution.py:61
  51.6 1.1 %collective-permute-done.30.refs_1_ = bf16[16,64,256]{2,1,0:T(8,128)(2,1)S(1)} collective-permute-done((bf16[16,64,256]{2,1,0:T(8,128)(2,1)S(1)}, bf16[16,64,256]{2,1,0:T(8,128)(2,1)S(1)}, u32[]{:S(2)}, u32[]{:S(2)}) %collective-permute-start.30) | collective-permute-done | bytes 524320 | tf_op jit(solution)/shard_map/ppermute | solution.py:61
  52.7 2.2 %residual.6 = (bf16[6,64,256]{2,1,0:T(8,128)(2,1)S(1)}, bf16[6,64,256]{2,1,0:T(8,128)(2,1)S(1)}) custom-call(s32[15]{0:T(128)S(1)} %get-tuple-element.64.plan_ref, s32[3]{0:T(128)S(1)} %pad_add_fusion.place_ref, bf16[16,64,256]{2,1,0:T(8,128)(2,1)S(1)} %collective-permute-done.28.refs_0_, bf16[16,64,256]{2,1,0:T(8,128)(2,1)S(1)} %collective-permute-done.30.refs_1_, ...), custom_call_target="tpu_custom_call" | custom-call | flops 1610612736 | bytes 6291456 | tf_op jit(solution)/shard_map/residual/pallas_call | solution.py:327
  54.9 1.7 %collective-permute-start.32 = (bf16[6,64,256]{2,1,0:T(8,128)(2,1)S(1)}, bf16[6,64,256]{2,1,0:T(8,128)(2,1)S(1)}, u32[]{:S(2)}, u32[]{:S(2)}) collective-permute-start(bf16[6,64,256]{2,1,0:T(8,128)(2,1)S(1)} %get-tuple-element.72), channel_id=1, source_target_pairs={{0,4},{4,0},{8,12},{12,8},{16,20},{20,16},{24,28},{28,24},{1,5},{5... | collective-permute-start | bytes 589832 | tf_op jit(solution)/shard_map/ppermute | solution.py:61
  56.6 0.0 collective-permute-done.35.refs_2_
  56.6 1.4 %assemble.6.refs_1_ = bf16[6,256,256]{2,1,0:T(8,128)(2,1)} custom-call(s32[3]{0:T(128)S(1)} %pad_add_fusion.place_ref, bf16[6,64,256]{2,1,0:T(8,128)(2,1)S(1)} %get-tuple-element.73.refs_0_, bf16[6,64,256]{2,1,0:T(8,128)(2,1)S(1)} %get-tuple-element.74.refs_1_, bf16[6,64,256]{2,1,0:T(8,128)(2,1)S(1)} %collective-permute-done.35.refs_2_), custom_call_target="tpu_custom_call" | custom-call | tf_op jit(solution)/shard_map/assemble/pallas_call | solution.py:365
  58.0 0.0 collective-permute-done.32.refs_0_
  58.0 1.2 %assemble.7 = bf16[6,256,256]{2,1,0:T(8,128)(2,1)} custom-call(s32[3]{0:T(128)S(1)} %pad_add_fusion.place_ref, bf16[6,64,256]{2,1,0:T(8,128)(2,1)S(1)} %collective-permute-done.32.refs_0_, bf16[6,256,256]{2,1,0:T(8,128)(2,1)} %assemble.6.refs_1_), custom_call_target="tpu_custom_call", output_to_operand_aliasing={{}: (2, {})} | custom-call | tf_op jit(solution)/shard_map/assemble/pallas_call | solution.py:365
  59.2 0.2 while.9
  (13 shorter events, 0.1 us)
Async XLA Ops:
  0.0 3.3 %copy-start.2 = (s32[4]{0:T(128)S(1)}, s32[4]{0:T(128)}, u32[]{:S(2)}) copy-start(s32[4]{0:T(128)} %owner_ref.3) | copy-start | bytes 52
  1.1 2.2 %collective-permute-start.23 = (bf16[16,64,256]{2,1,0:T(8,128)(2,1)S(1)}, bf16[16,64,256]{2,1,0:T(8,128)(2,1)S(1)}, u32[]{:S(2)}, u32[]{:S(2)}) collective-permute-start(bf16[16,64,256]{2,1,0:T(8,128)(2,1)S(1)} %dynamic-slice_bitcast_fusion.1), channel_id=1, source_target_pairs={{0,4},{4,0},{8,12},{12,8},{16,20},{20,16},{24,28},{28,24},{1,5},{5... | collective-permute-start | bytes 1572872 | tf_op jit(solution)/shard_map/ppermute | solution.py:61
  1.2 6.3 %copy-start.1 = (bf16[6,16,64]{2,1,0:T(8,128)(2,1)S(1)}, bf16[6,16,64]{2,1,0:T(8,128)(2,1)}, u32[]{:S(2)}) copy-start(bf16[6,16,64]{2,1,0:T(8,128)(2,1)} %param.8) | copy-start | bytes 36868
  2.7 10.7 %collective-permute-start.20 = (bf16[16,64,256]{2,1,0:T(8,128)(2,1)S(1)}, bf16[16,64,256]{2,1,0:T(8,128)(2,1)S(1)}, u32[]{:S(2)}, u32[]{:S(2)}) collective-permute-start(bf16[16,64,256]{2,1,0:T(8,128)(2,1)S(1)} %get-tuple-element.99), channel_id=1, source_target_pairs={{0,4},{4,0},{8,12},{12,8},{16,20},{20,16},{24,28},{28,24},{1,5},{5... | collective-permute-start | bytes 1572872 | tf_op jit(solution)/shard_map/ppermute | solution.py:61
  4.0 14.2 %collective-permute-start.24 = (bf16[16,64,256]{2,1,0:T(8,128)(2,1)S(1)}, bf16[16,64,256]{2,1,0:T(8,128)(2,1)S(1)}, u32[]{:S(2)}, u32[]{:S(2)}) collective-permute-start(bf16[16,64,256]{2,1,0:T(8,128)(2,1)S(1)} %get-tuple-element.65.refs_0_), channel_id=1, source_target_pairs={{0,8},{4,12},{8,0},{12,4},{16,24},{20,28},{24,16},{28,20},{1,9},{5... | collective-permute-start | bytes 1572872 | tf_op jit(solution)/shard_map/ppermute | solution.py:61
  6.3 12.7 %collective-permute-start.25 = (bf16[16,64,256]{2,1,0:T(8,128)(2,1)S(1)}, bf16[16,64,256]{2,1,0:T(8,128)(2,1)S(1)}, u32[]{:S(2)}, u32[]{:S(2)}) collective-permute-start(bf16[16,64,256]{2,1,0:T(8,128)(2,1)S(1)} %get-tuple-element.66.refs_1_), channel_id=1, source_target_pairs={{0,16},{4,20},{8,24},{12,28},{16,0},{20,4},{24,8},{28,12},{1,17},{... | collective-permute-start | bytes 1572872 | tf_op jit(solution)/shard_map/ppermute | solution.py:61
  7.5 3.0 %collective-permute-start.21 = (bf16[6,16,64]{2,1,0:T(8,128)(2,1)S(1)}, bf16[6,16,64]{2,1,0:T(8,128)(2,1)S(1)}, u32[]{:S(2)}, u32[]{:S(2)}) collective-permute-start(bf16[6,16,64]{2,1,0:T(8,128)(2,1)S(1)} %copy-done.1), channel_id=1, source_target_pairs={{0,1},{1,0},{2,3},{3,2},{4,5},{5,4},{6,7},{7,6},{8,9},{9,8},{10,11... | collective-permute-start | bytes 36872 | tf_op jit(solution)/shard_map/ppermute | solution.py:385
  10.5 2.8 %collective-permute-start.22 = (bf16[2,6,16,64]{3,2,1,0:T(8,128)(2,1)S(1)}, bf16[2,6,16,64]{3,2,1,0:T(8,128)(2,1)S(1)}, u32[]{:S(2)}, u32[]{:S(2)}) collective-permute-start(bf16[2,6,16,64]{3,2,1,0:T(8,128)(2,1)S(1)} %pad_maximum_fusion.3), channel_id=1, source_target_pairs={{0,4},{4,0},{8,12},{12,8},{16,20},{20,16},{24,28},{28,24},{1,5},{5... | collective-permute-start | bytes 73736 | tf_op jit(solution)/shard_map/ppermute | solution.py:61
  16.0 20.5 %collective-permute-start.27 = (bf16[16,64,256]{2,1,0:T(8,128)(2,1)S(1)}, bf16[16,64,256]{2,1,0:T(8,128)(2,1)S(1)}, u32[]{:S(2)}, u32[]{:S(2)}) collective-permute-start(bf16[16,64,256]{2,1,0:T(8,128)(2,1)S(1)} %get-tuple-element.69.refs_1_), channel_id=1, source_target_pairs={{0,16},{4,20},{8,24},{12,28},{16,0},{20,4},{24,8},{28,12},{1,17},{... | collective-permute-start | bytes 1572872 | tf_op jit(solution)/shard_map/ppermute | solution.py:61
  16.3 20.3 %collective-permute-start.29 = (bf16[16,64,256]{2,1,0:T(8,128)(2,1)S(1)}, bf16[16,64,256]{2,1,0:T(8,128)(2,1)S(1)}, u32[]{:S(2)}, u32[]{:S(2)}) collective-permute-start(bf16[16,64,256]{2,1,0:T(8,128)(2,1)S(1)} %get-tuple-element.70.refs_0_), channel_id=1, source_target_pairs={{0,8},{4,12},{8,0},{12,4},{16,24},{20,28},{24,16},{28,20},{1,9},{5... | collective-permute-start | bytes 1572872 | tf_op jit(solution)/shard_map/ppermute | solution.py:61
  19.0 12.8 %copy-start = (bf16[6,256,256]{2,1,0:T(8,128)(2,1)S(1)}, bf16[6,256,256]{2,1,0:T(8,128)(2,1)}, u32[]{:S(2)}) copy-start(bf16[6,256,256]{2,1,0:T(8,128)(2,1)} %refs_4_.3) | copy-start | bytes 2359300
  19.0 4.4 %collective-permute-start.26 = (bf16[2,12,16,64]{3,2,1,0:T(8,128)(2,1)S(1)}, bf16[2,12,16,64]{3,2,1,0:T(8,128)(2,1)S(1)}, u32[]{:S(2)}, u32[]{:S(2)}) collective-permute-start(bf16[2,12,16,64]{3,2,1,0:T(8,128)(2,1)S(1)} %hand_on.3), channel_id=1, source_target_pairs={{0,2},{1,3},{2,0},{3,1},{4,6},{5,7},{6,4},{7,5},{8,10},{9,11},{10,... | collective-permute-start | bytes 147464 | tf_op jit(solution)/shard_map/ppermute | solution.py:405
  21.5 26.2 %collective-permute-start.33 = (bf16[16,64,256]{2,1,0:T(8,128)(2,1)S(1)}, bf16[16,64,256]{2,1,0:T(8,128)(2,1)S(1)}, u32[]{:S(2)}, u32[]{:S(2)}) collective-permute-start(bf16[16,64,256]{2,1,0:T(8,128)(2,1)S(1)} %get-tuple-element.102), channel_id=1, source_target_pairs={{0,8},{4,12},{8,0},{12,4},{16,24},{20,28},{24,16},{28,20},{1,9},{5... | collective-permute-start | bytes 1572872 | tf_op jit(solution)/shard_map/ppermute | solution.py:61
  21.9 25.8 %collective-permute-start.34 = (bf16[16,64,256]{2,1,0:T(8,128)(2,1)S(1)}, bf16[16,64,256]{2,1,0:T(8,128)(2,1)S(1)}, u32[]{:S(2)}, u32[]{:S(2)}) collective-permute-start(bf16[16,64,256]{2,1,0:T(8,128)(2,1)S(1)} %get-tuple-element.101), channel_id=1, source_target_pairs={{0,16},{4,20},{8,24},{12,28},{16,0},{20,4},{24,8},{28,12},{1,17},{... | collective-permute-start | bytes 1572872 | tf_op jit(solution)/shard_map/ppermute | solution.py:61
  32.5 15.2 %collective-permute-start.31 = (bf16[6,128,256]{2,1,0:T(8,128)(2,1)S(1)}, bf16[6,128,256]{2,1,0:T(8,128)(2,1)S(1)}, u32[]{:S(2)}, u32[]{:S(2)}) collective-permute-start(bf16[6,128,256]{2,1,0:T(8,128)(2,1)S(1)} %cut.3), channel_id=1, source_target_pairs={{0,4},{4,0},{8,12},{12,8},{16,20},{20,16},{24,28},{28,24},{1,5},{5... | collective-permute-start | bytes 1179656 | tf_op jit(solution)/shard_map/ppermute | solution.py:61
  36.7 14.9 %collective-permute-start.28 = (bf16[16,64,256]{2,1,0:T(8,128)(2,1)S(1)}, bf16[16,64,256]{2,1,0:T(8,128)(2,1)S(1)}, u32[]{:S(2)}, u32[]{:S(2)}) collective-permute-start(bf16[16,64,256]{2,1,0:T(8,128)(2,1)S(1)} %get-tuple-element.104), channel_id=1, source_target_pairs={{0,8},{4,12},{8,0},{12,4},{16,24},{20,28},{24,16},{28,20},{1,9},{5... | collective-permute-start | bytes 1572872 | tf_op jit(solution)/shard_map/ppermute | solution.py:61
  37.2 15.5 %collective-permute-start.30 = (bf16[16,64,256]{2,1,0:T(8,128)(2,1)S(1)}, bf16[16,64,256]{2,1,0:T(8,128)(2,1)S(1)}, u32[]{:S(2)}, u32[]{:S(2)}) collective-permute-start(bf16[16,64,256]{2,1,0:T(8,128)(2,1)S(1)} %get-tuple-element.103), channel_id=1, source_target_pairs={{0,16},{4,20},{8,24},{12,28},{16,0},{20,4},{24,8},{28,12},{1,17},{... | collective-permute-start | bytes 1572872 | tf_op jit(solution)/shard_map/ppermute | solution.py:61
  49.9 6.7 %collective-permute-start.35 = (bf16[6,64,256]{2,1,0:T(8,128)(2,1)S(1)}, bf16[6,64,256]{2,1,0:T(8,128)(2,1)S(1)}, u32[]{:S(2)}, u32[]{:S(2)}) collective-permute-start(bf16[6,64,256]{2,1,0:T(8,128)(2,1)S(1)} %get-tuple-element.75), channel_id=1, source_target_pairs={{0,4},{4,0},{8,12},{12,8},{16,20},{20,16},{24,28},{28,24},{1,5},{5... | collective-permute-start | bytes 589832 | tf_op jit(solution)/shard_map/ppermute | solution.py:61
  54.9 3.1 %collective-permute-start.32 = (bf16[6,64,256]{2,1,0:T(8,128)(2,1)S(1)}, bf16[6,64,256]{2,1,0:T(8,128)(2,1)S(1)}, u32[]{:S(2)}, u32[]{:S(2)}) collective-permute-start(bf16[6,64,256]{2,1,0:T(8,128)(2,1)S(1)} %get-tuple-element.72), channel_id=1, source_target_pairs={{0,4},{4,0},{8,12},{12,8},{16,20},{20,16},{24,28},{28,24},{1,5},{5... | collective-permute-start | bytes 589832 | tf_op jit(solution)/shard_map/ppermute | solution.py:61
